TPU v7x, 256 devices: a whole 4x4x8 slice. The times are simulated.
256 devices in a mesh: lon: 16 (over x, y), lat: 16 (over z, core).
Axes of the slice: x: 4, y: 4, z: 8, core: 2. Of those that a mesh axis runs over, the one named last changes fastest.
Arguments:
- tracer: float32 [4096, 128, 128], P('lon', 'lat'), may hold values from -6 to 6
- offsets: int32 [128], P('lat'), may hold values from 0 to 4095
- frac_lon: float32 [128], P('lat'), may hold values from 0 to 1
- frac_lat: float32 [128], P('lat'), may hold values from 0 to 1
- frac_lev: float32 [128], P('lat'), may hold values from 0 to 1
- metric: float32 [128], P('lat'), may hold values from 0.5 to 2
- vertical_coef: float32 [128], replicated, may hold values from 0.5 to 4
- inverses: float32 [128, 128, 128], P('lat'), may hold values from -0.1 to 0.6, as said below
Outputs:
- advected: float32 [4096, 128, 128], P('lon', 'lat')
- pressure: float32 [4096, 128, 128], P('lon', 'lat')
- residual: float32 [4096, 128, 128], P('lon', 'lat')
Inputs may be any that keep to these rules, and one draw needn't show every extreme that they name: `inverses`: one matrix for each latitude row.
All inputs are finite; a program needn't handle non-finite values.
Results may differ from a plain program's by a relative error of at most 0.00016.
Values sent between devices are 32-bit elements; how exact they have to be, the bound alone decides.
No kernel may reach another device: no remote copies, remote signals or barrier semaphores. Data moves between devices by JAX's collectives and lax.ppermute only.
A program may use at most 128 MiB of HBM per device.

v0:
```python
import jax
import jax.numpy as jnp
from jax import lax
from jax.sharding import Mesh
from jax.sharding import PartitionSpec as P

ITERS = 3
LON = ("lon_0", "lon_1")
LAT = ("lat_0", "lat_1")
LON_LAT = ("lon_0", "lon_1", "lat_0", "lat_1")


def extended(cells, sides, width, closed):
    for axis, dim in sides:
        count = lax.axis_size(axis)
        ends = count if closed else count - 1
        head = lax.slice_in_dim(cells, 0, width, axis=dim)
        tail = lax.slice_in_dim(cells, cells.shape[dim] - width, cells.shape[dim], axis=dim)
        cells = jnp.concatenate(
            [
                lax.ppermute(tail, axis, [(i, (i + 1) % count) for i in range(ends)]),
                cells,
                lax.ppermute(head, axis, [((i + 1) % count, i) for i in range(ends)]),
            ],
            axis=dim,
        )
    return cells


def over_axes(x, axes):
    for axis in axes:
        x = lax.psum(x, axis)
    return x


def cubic_weights(fraction):
    return (
        -fraction * (fraction - 1.0) * (fraction - 2.0) / 6.0,
        (fraction + 1.0) * (fraction - 1.0) * (fraction - 2.0) / 2.0,
        -(fraction + 1.0) * fraction * (fraction - 2.0) / 2.0,
        (fraction + 1.0) * fraction * (fraction - 1.0) / 6.0,
    )


def operate(field, metric, vertical_coef):
    lon_padded = extended(field, ((LON, 0),), 1, True)
    lat_padded = extended(field, ((LAT, 1),), 1, False)
    zeros_level = jnp.zeros_like(field[:, :, :1])
    upper = jnp.concatenate([field[:, :, 1:], zeros_level], 2)
    lower = jnp.concatenate([zeros_level, field[:, :, :-1]], 2)
    result = metric[None, :, None] * (2.0 * field - lon_padded[2:] - lon_padded[:-2])
    result = result + (2.0 * field - lat_padded[:, 2:] - lat_padded[:, :-2])
    result = result + vertical_coef[None, None, :] * (2.0 * field - upper - lower)
    return result + 0.1 * field


def precondition(inverses, field):
    return jnp.einsum("jkm,xjm->xjk", inverses, field, precision=lax.Precision.HIGHEST)


def inner(first_field, second_field):
    return jnp.sum(first_field * second_field)


def body(tracer, offsets, frac_lon, frac_lat, frac_lev, metric, vertical_coef, inverses):
    width = tracer.shape[0]
    rows_here = tracer.shape[1]
    levels = tracer.shape[2]
    lat_weights = cubic_weights(frac_lat)
    padded = extended(tracer, ((LAT, 1),), 2, False)
    lat_mixed = jnp.zeros_like(tracer)
    for tap_index in range(4):
        lat_mixed = (
            lat_mixed
            + lat_weights[tap_index][None, :, None]
            * padded[:, 1 + tap_index : 1 + tap_index + rows_here]
        )
    lev_weights = cubic_weights(frac_lev)
    level_index = jnp.arange(levels, dtype=jnp.int32)
    level_delta = level_index[:, None] - level_index[None, :]
    vertical_table = jnp.zeros((rows_here, levels, levels), jnp.float32)
    for tap_index in range(4):
        vertical_table = (
            vertical_table
            + (level_delta == tap_index - 1).astype(jnp.float32)[None]
            * lev_weights[tap_index][:, None, None]
        )
    lev_mixed = jnp.einsum(
        "xjc,jck->xjk", lat_mixed, vertical_table, precision=lax.Precision.HIGHEST
    )
    lon_weights = cubic_weights(frac_lon)
    local_cells = jnp.arange(width, dtype=jnp.int32)
    total_cells = width * lax.axis_size(LON)
    arrival = lax.axis_index(LON) * width + local_cells
    piece = lax.all_gather(lev_mixed, LON, axis=0, tiled=True)
    cells = jnp.arange(piece.shape[0], dtype=jnp.int32)
    tap_shift = jnp.mod(
        cells[None, None, :] - arrival[None, :, None] + offsets[:, None, None] + 1, total_cells
    )
    lon_table = jnp.zeros((rows_here, width, piece.shape[0]), jnp.float32)
    for tap_index in range(4):
        lon_table = (
            lon_table
            + (tap_shift == tap_index).astype(jnp.float32) * lon_weights[tap_index][:, None, None]
        )
    advected = jnp.einsum("jic,cjl->ijl", lon_table, piece, precision=lax.Precision.HIGHEST)
    pressure = jnp.zeros_like(advected)
    residual = advected
    first = precondition(inverses, residual)
    directions = [first]
    images = [operate(first, metric, vertical_coef)]
    along, first_square = (
        over_axes(inner(residual, images[0]), LON_LAT),
        over_axes(inner(images[0], images[0]), LON_LAT),
    )
    gram = [[first_square]]
    for step in range(ITERS):
        alpha = along / gram[step][step]
        pressure = pressure + alpha * directions[step]
        residual = residual - alpha * images[step]
        if step + 1 < ITERS:
            search = precondition(inverses, residual)
            image_new = operate(search, metric, vertical_coef)
            cross_terms = tuple((inner(image_new, images[prior]) for prior in range(step + 1)))
            residual_terms = tuple((inner(residual, images[prior]) for prior in range(step + 1)))
            summed = jax.tree.map(
                lambda part: over_axes(part, LON_LAT),
                cross_terms
                + (inner(image_new, image_new), inner(residual, image_new))
                + residual_terms,
            )
            crosses = summed[: step + 1]
            self_square = summed[step + 1]
            residual_cross = summed[step + 2]
            residual_prior = summed[step + 3 :]
            factors = [-crosses[prior] / gram[prior][prior] for prior in range(step + 1)]
            direction_new = search
            combined = image_new
            for prior in range(step + 1):
                direction_new = direction_new + factors[prior] * directions[prior]
                combined = combined + factors[prior] * images[prior]
            new_row = []
            for prior in range(step + 1):
                entry = crosses[prior]
                for other in range(step + 1):
                    entry = entry + factors[other] * gram[other][prior]
                new_row.append(entry)
            new_square = self_square
            along = residual_cross
            for prior in range(step + 1):
                new_square = new_square + 2.0 * factors[prior] * crosses[prior]
                along = along + factors[prior] * residual_prior[prior]
                for other in range(step + 1):
                    new_square = new_square + factors[prior] * factors[other] * gram[prior][other]
            for prior in range(step + 1):
                gram[prior].append(new_row[prior])
            gram.append(new_row + [new_square])
            directions.append(direction_new)
            images.append(combined)
    return (advected, pressure, residual)


def solution(mesh):
    split = Mesh(mesh.devices.reshape(4, 4, 8, 2), ("lon_0", "lon_1", "lat_0", "lat_1"))
    placed = (P(LON, LAT, None), P(LAT), P(LAT), P(LAT), P(LAT), P(LAT), P(), P(LAT, None, None))
    return jax.shard_map(
        body,
        mesh=split,
        in_specs=placed,
        out_specs=(P(LON, LAT, None), P(LON, LAT, None), P(LON, LAT, None)),
        check_vma=False,
    )
```

profile of v0, /device:TPU:1, one launch (start us, length us, event | category | flops | bytes accessed | tf_op | source)
XLA Modules:
  0.0 460.9 jit_solution(13656612194522790697)
XLA Ops:
  9.0 5.1 %collective-permute-start.1 = (f32[256,2,128]{2,0,1:T(8,128)S(1)}, f32[256,2,128]{2,0,1:T(8,128)S(1)}, u32[]{:S(2)}, u32[]{:S(2)}) collective-permute-start(f32[256,2,128]{2,0,1:T(8,128)S(1)} %copy.41), channel_id=1, source_target_pairs={{1,0},{2,1},{3,2},{4,3},{5,4},{6,5},{7,6},{8,7},{9,8},{10,9},{11,1... | collective-permute-start | bytes 786440 | tf_op jit(solution)/shard_map/ppermute | solution.py:23
  27.5 126.5 %all-gather.2.cloned.1.call-done = f32[4096,8,128]{0,2,1:T(8,128)} async-done(((f32[256,8,128]{0,2,1:T(8,128)}), f32[4096,8,128]{0,2,1:T(8,128)}) %all-gather.2.cloned.1.call-update) | async-done | bytes 16777232 | tf_op jit(solution)/shard_map/all_gather | solution.py:95
  154.0 63.4 %fusion.29 = f32[256,8,128]{0,2,1:T(8,128)S(1)} fusion(f32[4096,8,128]{0,2,1:T(8,128)} %all-gather.2.cloned.1.call-done, f32[8]{0:T(128)S(1)} %get-tuple-element.94, f32[8]{0:T(128)S(1)} %get-tuple-element.95, f32[8]{0:T(128)S(1)} %get-tuple-element.93, f32[8]{0:T(128)S(1)} %get-tuple-element.92, s32[8]{0:T(128)S(1)} %copy-done.7, ...), kind=kOutput, calls=%fused_computation.37 | convolution fusion | flops 13086228480 | bytes 22020256 | tf_op jit(solution)/shard_map/jic,cjl->ijl/dot_general | solution.py:106
  232.1 9.1 %collective-permute-done.2 = f32[1,8,128]{0,2,1:T(8,128)S(1)} collective-permute-done((f32[1,8,128]{0,2,1:T(8,128)}, f32[1,8,128]{0,2,1:T(8,128)S(1)}, u32[]{:S(2)}, u32[]{:S(2)}) %collective-permute-start.2) | collective-permute-done | bytes 4128 | tf_op jit(solution)/shard_map/ppermute | solution.py:23
  241.2 5.6 %collective-permute-done.3 = f32[1,8,128]{0,2,1:T(8,128)} collective-permute-done((f32[1,8,128]{0,2,1:T(8,128)}, f32[1,8,128]{0,2,1:T(8,128)}, u32[]{:S(2)}, u32[]{:S(2)}) %collective-permute-start.3) | collective-permute-done | bytes 4128 | tf_op jit(solution)/shard_map/ppermute | solution.py:21
  246.8 3.6 multiply_reduce_fusion.10
  250.4 6.9 %all-reduce.14 = (f32[]{:T(128)}, f32[]{:T(128)}) all-reduce(f32[]{:T(128)} %get-tuple-element.20, f32[]{:T(128)} %get-tuple-element.19), channel_id=1, replica_groups=mesh['lon_0'=4,'lon_1'=4,'lat_0'=8,'lat_1'=2] {'lon_0'}, use_global_device_ids=true, to_apply=%region_1.2 | all-reduce | flops 2 | bytes 16 | tf_op jit(solution)/shard_map/psum | solution.py:32
  257.4 6.7 %all-reduce.11 = (f32[]{:T(128)}, f32[]{:T(128)}) all-reduce(f32[]{:T(128)} %get-tuple-element.55, f32[]{:T(128)} %get-tuple-element.56), channel_id=1, replica_groups=mesh['lon_0'=4,'lon_1'=4,'lat_0'=8,'lat_1'=2] {'lon_1'}, use_global_device_ids=true, to_apply=%region_2.3 | all-reduce | flops 2 | bytes 16 | tf_op jit(solution)/shard_map/psum | solution.py:32
  264.0 12.6 %all-reduce.8 = (f32[]{:T(128)}, f32[]{:T(128)}) all-reduce(f32[]{:T(128)} %get-tuple-element.43, f32[]{:T(128)} %get-tuple-element.44), channel_id=1, replica_groups=mesh['lon_0'=4,'lon_1'=4,'lat_0'=8,'lat_1'=2] {'lat_0'}, use_global_device_ids=true, to_apply=%region_3.4 | all-reduce | flops 2 | bytes 16 | tf_op jit(solution)/shard_map/psum | solution.py:32
  276.7 11.4 %all-reduce.17 = (f32[]{:T(128)}, f32[]{:T(128)}) all-reduce(f32[]{:T(128)} %get-tuple-element.31, f32[]{:T(128)} %get-tuple-element.32), channel_id=1, replica_groups=mesh['lon_0'=4,'lon_1'=4,'lat_0'=8,'lat_1'=2] {'lat_1'}, use_global_device_ids=true, to_apply=%region_4.5 | all-reduce | flops 2 | bytes 16 | tf_op jit(solution)/shard_map/psum | solution.py:32
  300.5 11.1 %collective-permute-done.6 = f32[1,8,128]{0,2,1:T(8,128)S(1)} collective-permute-done((f32[1,8,128]{0,2,1:T(8,128)S(1)}, f32[1,8,128]{0,2,1:T(8,128)S(1)}, u32[]{:S(2)}, u32[]{:S(2)}) %collective-permute-start.6) | collective-permute-done | bytes 4128 | tf_op jit(solution)/shard_map/ppermute | solution.py:23
  311.6 5.6 %collective-permute-done.7 = f32[1,8,128]{0,2,1:T(8,128)S(1)} collective-permute-done((f32[1,8,128]{0,2,1:T(8,128)S(1)}, f32[1,8,128]{0,2,1:T(8,128)S(1)}, u32[]{:S(2)}, u32[]{:S(2)}) %collective-permute-start.7) | collective-permute-done | bytes 4128 | tf_op jit(solution)/shard_map/ppermute | solution.py:21
  317.2 4.1 multiply_reduce_fusion.6
  321.3 6.8 %all-reduce.13 = (f32[]{:T(128)}, f32[]{:T(128)}, f32[]{:T(128)}, f32[]{:T(128)}) all-reduce(f32[]{:T(128)} %get-tuple-element.16, f32[]{:T(128)} %get-tuple-element.18, f32[]{:T(128)} %get-tuple-element.17, f32[]{:T(128)} %get-tuple-element.15), channel_id=1, replica_groups=mesh['lon_0'=4,'lon_1'=4,'lat_0'=8,'lat_1'=2] {'lon_0'}, use_global_device_ids=true, to_apply=%region_16.17 | all-reduce | flops 4 | bytes 32 | tf_op jit(solution)/shard_map/psum | solution.py:32
  328.2 6.7 %all-reduce.10 = (f32[]{:T(128)}, f32[]{:T(128)}, f32[]{:T(128)}, f32[]{:T(128)}) all-reduce(f32[]{:T(128)} %get-tuple-element.51, f32[]{:T(128)} %get-tuple-element.52, f32[]{:T(128)} %get-tuple-element.53, f32[]{:T(128)} %get-tuple-element.54), channel_id=1, replica_groups=mesh['lon_0'=4,'lon_1'=4,'lat_0'=8,'lat_1'=2] {'lon_1'}, use_global_device_ids=true, to_apply=%region_17.18 | all-reduce | flops 4 | bytes 32 | tf_op jit(solution)/shard_map/psum | solution.py:32
  334.9 12.7 %all-reduce.7 = (f32[]{:T(128)}, f32[]{:T(128)}, f32[]{:T(128)}, f32[]{:T(128)}) all-reduce(f32[]{:T(128)} %get-tuple-element.39, f32[]{:T(128)} %get-tuple-element.40, f32[]{:T(128)} %get-tuple-element.41, f32[]{:T(128)} %get-tuple-element.42), channel_id=1, replica_groups=mesh['lon_0'=4,'lon_1'=4,'lat_0'=8,'lat_1'=2] {'lat_0'}, use_global_device_ids=true, to_apply=%region_18.19 | all-reduce | flops 4 | bytes 32 | tf_op jit(solution)/shard_map/psum | solution.py:32
  347.6 10.4 %all-reduce.16 = (f32[]{:T(128)}, f32[]{:T(128)}, f32[]{:T(128)}, f32[]{:T(128)}) all-reduce(f32[]{:T(128)} %get-tuple-element.27, f32[]{:T(128)} %get-tuple-element.28, f32[]{:T(128)} %get-tuple-element.29, f32[]{:T(128)} %get-tuple-element.30), channel_id=1, replica_groups=mesh['lon_0'=4,'lon_1'=4,'lat_0'=8,'lat_1'=2] {'lat_1'}, use_global_device_ids=true, to_apply=%region_19.20 | all-reduce | flops 4 | bytes 32 | tf_op jit(solution)/shard_map/psum | solution.py:32
  380.9 8.8 %collective-permute-done.10 = f32[1,8,128]{0,2,1:T(8,128)S(1)} collective-permute-done((f32[1,8,128]{0,2,1:T(8,128)}, f32[1,8,128]{0,2,1:T(8,128)S(1)}, u32[]{:S(2)}, u32[]{:S(2)}) %collective-permute-start.10) | collective-permute-done | bytes 4128 | tf_op jit(solution)/shard_map/ppermute | solution.py:23
  389.7 5.6 %collective-permute-done.11 = f32[1,8,128]{0,2,1:T(8,128)} collective-permute-done((f32[1,8,128]{0,2,1:T(8,128)}, f32[1,8,128]{0,2,1:T(8,128)}, u32[]{:S(2)}, u32[]{:S(2)}) %collective-permute-start.11) | collective-permute-done | bytes 4128 | tf_op jit(solution)/shard_map/ppermute | solution.py:21
  395.4 6.7 %multiply_reduce_fusion.1 = (f32[]{:T(128)}, f32[]{:T(128)}, f32[]{:T(128)}, f32[]{:T(128)}, f32[]{:T(128)}, /*index=5*/f32[]{:T(128)}, f32[256,8,128]{0,2,1:T(8,128)}) fusion(f32[256,8,128]{0,2,1:T(8,128)} %multiply_add_fusion.1, f32[256,8,128]{0,2,1:T(8,128)} %copy-done.3, f32[]{:T(128)S(6)} %div.68, f32[256,8,128]{0,2,1:T(8,128)} %copy-done.2, ...), kind=kLoop, calls=%fused_computation.94 | loop fusion | flops 8126458 | bytes 7594556 | tf_op jit(solution)/shard_map/reduce_sum | solution.py:62
  402.1 6.8 %all-reduce.12 = (f32[]{:T(128)}, f32[]{:T(128)}, f32[]{:T(128)}, f32[]{:T(128)}, f32[]{:T(128)}, /*index=5*/f32[]{:T(128)}) all-reduce(f32[]{:T(128)} %get-tuple-element.11, f32[]{:T(128)} %get-tuple-element.13, f32[]{:T(128)} %get-tuple-element.10, ...), channel_id=1, replica_groups=mesh['lon_0'=4,'lon_1'=4,'lat_0'=8,'lat_1'=2] {'lon_0'}, use_global_device_ids=true, to_apply=%region_46.47 | all-reduce | flops 6 | bytes 48 | tf_op jit(solution)/shard_map/psum | solution.py:32
  408.9 6.7 %all-reduce.9 = (f32[]{:T(128)}, f32[]{:T(128)}, f32[]{:T(128)}, f32[]{:T(128)}, f32[]{:T(128)}, /*index=5*/f32[]{:T(128)}) all-reduce(f32[]{:T(128)} %get-tuple-element.45, f32[]{:T(128)} %get-tuple-element.46, f32[]{:T(128)} %get-tuple-element.47, ...), channel_id=1, replica_groups=mesh['lon_0'=4,'lon_1'=4,'lat_0'=8,'lat_1'=2] {'lon_1'}, use_global_device_ids=true, to_apply=%region_47.48 | all-reduce | flops 6 | bytes 48 | tf_op jit(solution)/shard_map/psum | solution.py:32
  415.6 12.6 %all-reduce.6 = (f32[]{:T(128)}, f32[]{:T(128)}, f32[]{:T(128)}, f32[]{:T(128)}, f32[]{:T(128)}, /*index=5*/f32[]{:T(128)}) all-reduce(f32[]{:T(128)} %get-tuple-element.33, f32[]{:T(128)} %get-tuple-element.34, f32[]{:T(128)} %get-tuple-element.35, ...), channel_id=1, replica_groups=mesh['lon_0'=4,'lon_1'=4,'lat_0'=8,'lat_1'=2] {'lat_0'}, use_global_device_ids=true, to_apply=%region_48.49 | all-reduce | flops 6 | bytes 48 | tf_op jit(solution)/shard_map/psum | solution.py:32
  428.2 10.6 %all-reduce.15 = (f32[]{:T(128)}, f32[]{:T(128)}, f32[]{:T(128)}, f32[]{:T(128)}, f32[]{:T(128)}, /*index=5*/f32[]{:T(128)}) all-reduce(f32[]{:T(128)} %get-tuple-element.21, f32[]{:T(128)} %get-tuple-element.22, f32[]{:T(128)} %get-tuple-element.23, ...), channel_id=1, replica_groups=mesh['lon_0'=4,'lon_1'=4,'lat_0'=8,'lat_1'=2] {'lat_1'}, use_global_device_ids=true, to_apply=%region_49.50 | all-reduce | flops 6 | bytes 48 | tf_op jit(solution)/shard_map/psum | solution.py:32
  (73 shorter events, 66.7 us)
Async XLA Ops:
  7.2 210.3 %copy-start = (f32[8,128,128]{2,1,0:T(8,128)S(1)}, f32[8,128,128]{2,1,0:T(8,128)}, u32[]{:S(2)}) copy-start(f32[8,128,128]{2,1,0:T(8,128)} %param.15) | copy-start | bytes 1572868
  7.2 146.8 %copy-start.7 = (s32[8]{0:T(128)S(1)}, s32[8]{0:T(128)}, u32[]{:S(2)}) copy-start(s32[8]{0:T(128)} %param.9) | copy-start | bytes 100
  7.2 146.8 %all-gather.2.cloned.1.call-start = ((), (), s32[]{:S(2)}) async-start(), calls=%async_computation | async-start | bytes 17825792 | tf_op jit(solution)/shard_map/all_gather | solution.py:95
  9.0 10.6 %collective-permute-start.1 = (f32[256,2,128]{2,0,1:T(8,128)S(1)}, f32[256,2,128]{2,0,1:T(8,128)S(1)}, u32[]{:S(2)}, u32[]{:S(2)}) collective-permute-start(f32[256,2,128]{2,0,1:T(8,128)S(1)} %copy.41), channel_id=1, source_target_pairs={{1,0},{2,1},{3,2},{4,3},{5,4},{6,5},{7,6},{8,7},{9,8},{10,9},{11,1... | collective-permute-start | bytes 786440 | tf_op jit(solution)/shard_map/ppermute | solution.py:23
  14.2 5.2 %collective-permute-start = (f32[256,2,128]{2,0,1:T(8,128)S(1)}, f32[256,2,128]{2,0,1:T(8,128)S(1)}, u32[]{:S(2)}, u32[]{:S(2)}) collective-permute-start(f32[256,2,128]{2,0,1:T(8,128)S(1)} %copy.40), channel_id=1, source_target_pairs={{0,1},{1,2},{2,3},{3,4},{4,5},{5,6},{6,7},{7,8},{8,9},{9,10},{10,1... | collective-permute-start | bytes 786440 | tf_op jit(solution)/shard_map/ppermute | solution.py:21
  154.0 92.8 %copy-start.5 = (f32[128]{0:T(128)S(1)}, f32[128]{0:T(128)}, u32[]{:S(2)}) copy-start(f32[128]{0:T(128)} %param.14) | copy-start | bytes 1540
  154.0 92.9 %copy-start.6 = (f32[8]{0:T(128)S(1)}, f32[8]{0:T(128)}, u32[]{:S(2)}) copy-start(f32[8]{0:T(128)} %param.13) | copy-start | bytes 100
  217.4 29.4 %copy-start.4 = (f32[256,8,128]{0,2,1:T(8,128)}, f32[256,8,128]{0,2,1:T(8,128)S(1)}, u32[]{:S(2)}) copy-start(f32[256,8,128]{0,2,1:T(8,128)S(1)} %fusion.29) | copy-start | bytes 3145732
  220.3 26.5 %collective-permute-start.4 = (f32[256,1,128]{0,2,1:T(8,128)}, f32[256,1,128]{0,2,1:T(8,128)S(1)}, u32[]{:S(2)}, u32[]{:S(2)}) collective-permute-start(f32[256,1,128]{0,2,1:T(8,128)} %get-tuple-element.86), channel_id=1, source_target_pairs={{1,0},{2,1},{3,2},{4,3},{5,4},{6,5},{7,6},{8,7},{9,8},{10,9},{11,1... | collective-permute-start | bytes 393224 | tf_op jit(solution)/shard_map/ppermute | solution.py:23
  223.7 23.1 %collective-permute-start.5 = (f32[256,1,128]{0,2,1:T(8,128)S(1)}, f32[256,1,128]{0,2,1:T(8,128)S(1)}, u32[]{:S(2)}, u32[]{:S(2)}) collective-permute-start(f32[256,1,128]{0,2,1:T(8,128)S(1)} %get-tuple-element.87), channel_id=1, source_target_pairs={{0,1},{1,2},{2,3},{3,4},{4,5},{5,6},{6,7},{7,8},{8,9},{9,10},{10,1... | collective-permute-start | bytes 393224 | tf_op jit(solution)/shard_map/ppermute | solution.py:21
  226.8 14.4 %collective-permute-start.2 = (f32[1,8,128]{0,2,1:T(8,128)}, f32[1,8,128]{0,2,1:T(8,128)S(1)}, u32[]{:S(2)}, u32[]{:S(2)}) collective-permute-start(f32[1,8,128]{0,2,1:T(8,128)} %get-tuple-element.84), channel_id=1, source_target_pairs={{16,0},{32,16},{48,32},{64,48},{80,64},{96,80},{112,96},{128,112},... | collective-permute-start | bytes 12296 | tf_op jit(solution)/shard_map/ppermute | solution.py:23
  229.3 17.5 %collective-permute-start.3 = (f32[1,8,128]{0,2,1:T(8,128)}, f32[1,8,128]{0,2,1:T(8,128)}, u32[]{:S(2)}, u32[]{:S(2)}) collective-permute-start(f32[1,8,128]{0,2,1:T(8,128)} %get-tuple-element.85), channel_id=1, source_target_pairs={{0,16},{16,32},{32,48},{48,64},{64,80},{80,96},{96,112},{112,128},... | collective-permute-start | bytes 12296 | tf_op jit(solution)/shard_map/ppermute | solution.py:21
  250.4 39.0 %copy-start.2 = (f32[256,8,128]{0,2,1:T(8,128)}, f32[256,8,128]{0,2,1:T(8,128)S(1)}, u32[]{:S(2)}) copy-start(f32[256,8,128]{0,2,1:T(8,128)S(1)} %get-tuple-element.71) | copy-start | bytes 3145732
  290.8 26.4 %copy-start.3 = (f32[256,8,128]{0,2,1:T(8,128)}, f32[256,8,128]{0,2,1:T(8,128)S(1)}, u32[]{:S(2)}) copy-start(f32[256,8,128]{0,2,1:T(8,128)S(1)} %multiply_subtract_fusion.5) | copy-start | bytes 3145732
  292.1 25.1 %collective-permute-start.8 = (f32[256,1,128]{0,2,1:T(8,128)S(1)}, f32[256,1,128]{0,2,1:T(8,128)S(1)}, u32[]{:S(2)}, u32[]{:S(2)}) collective-permute-start(f32[256,1,128]{0,2,1:T(8,128)S(1)} %get-tuple-element.80), channel_id=1, source_target_pairs={{1,0},{2,1},{3,2},{4,3},{5,4},{6,5},{7,6},{8,7},{9,8},{10,9},{11,1... | collective-permute-start | bytes 393224 | tf_op jit(solution)/shard_map/ppermute | solution.py:23
  294.4 22.8 %collective-permute-start.9 = (f32[256,1,128]{0,2,1:T(8,128)S(1)}, f32[256,1,128]{0,2,1:T(8,128)S(1)}, u32[]{:S(2)}, u32[]{:S(2)}) collective-permute-start(f32[256,1,128]{0,2,1:T(8,128)S(1)} %get-tuple-element.81), channel_id=1, source_target_pairs={{0,1},{1,2},{2,3},{3,4},{4,5},{5,6},{6,7},{7,8},{8,9},{9,10},{10,1... | collective-permute-start | bytes 393224 | tf_op jit(solution)/shard_map/ppermute | solution.py:21
  297.7 13.8 %collective-permute-start.6 = (f32[1,8,128]{0,2,1:T(8,128)S(1)}, f32[1,8,128]{0,2,1:T(8,128)S(1)}, u32[]{:S(2)}, u32[]{:S(2)}) collective-permute-start(f32[1,8,128]{0,2,1:T(8,128)S(1)} %get-tuple-element.78), channel_id=1, source_target_pairs={{16,0},{32,16},{48,32},{64,48},{80,64},{96,80},{112,96},{128,112},... | collective-permute-start | bytes 12296 | tf_op jit(solution)/shard_map/ppermute | solution.py:23
  300.3 17.0 %collective-permute-start.7 = (f32[1,8,128]{0,2,1:T(8,128)S(1)}, f32[1,8,128]{0,2,1:T(8,128)S(1)}, u32[]{:S(2)}, u32[]{:S(2)}) collective-permute-start(f32[1,8,128]{0,2,1:T(8,128)S(1)} %get-tuple-element.79), channel_id=1, source_target_pairs={{0,16},{16,32},{32,48},{48,64},{64,80},{80,96},{96,112},{112,128},... | collective-permute-start | bytes 12296 | tf_op jit(solution)/shard_map/ppermute | solution.py:21
  367.8 10.3 %copy-start.1 = (f32[256,8,128]{0,2,1:T(8,128)}, f32[256,8,128]{0,2,1:T(8,128)S(1)}, u32[]{:S(2)}) copy-start(f32[256,8,128]{0,2,1:T(8,128)S(1)} %convolution_bitcast_fusion) | copy-start | bytes 3145732
  369.7 25.7 %collective-permute-start.12 = (f32[256,1,128]{0,2,1:T(8,128)}, f32[256,1,128]{0,2,1:T(8,128)S(1)}, u32[]{:S(2)}, u32[]{:S(2)}) collective-permute-start(f32[256,1,128]{0,2,1:T(8,128)} %get-tuple-element.74), channel_id=1, source_target_pairs={{1,0},{2,1},{3,2},{4,3},{5,4},{6,5},{7,6},{8,7},{9,8},{10,9},{11,1... | collective-permute-start | bytes 393224 | tf_op jit(solution)/shard_map/ppermute | solution.py:23
  371.9 23.4 %collective-permute-start.13 = (f32[256,1,128]{0,2,1:T(8,128)S(1)}, f32[256,1,128]{0,2,1:T(8,128)S(1)}, u32[]{:S(2)}, u32[]{:S(2)}) collective-permute-start(f32[256,1,128]{0,2,1:T(8,128)S(1)} %get-tuple-element.75), channel_id=1, source_target_pairs={{0,1},{1,2},{2,3},{3,4},{4,5},{5,6},{6,7},{7,8},{8,9},{9,10},{10,1... | collective-permute-start | bytes 393224 | tf_op jit(solution)/shard_map/ppermute | solution.py:21
  375.2 14.5 %collective-permute-start.10 = (f32[1,8,128]{0,2,1:T(8,128)}, f32[1,8,128]{0,2,1:T(8,128)S(1)}, u32[]{:S(2)}, u32[]{:S(2)}) collective-permute-start(f32[1,8,128]{0,2,1:T(8,128)} %get-tuple-element.72), channel_id=1, source_target_pairs={{16,0},{32,16},{48,32},{64,48},{80,64},{96,80},{112,96},{128,112},... | collective-permute-start | bytes 12296 | tf_op jit(solution)/shard_map/ppermute | solution.py:23
  378.1 17.3 %collective-permute-start.11 = (f32[1,8,128]{0,2,1:T(8,128)}, f32[1,8,128]{0,2,1:T(8,128)}, u32[]{:S(2)}, u32[]{:S(2)}) collective-permute-start(f32[1,8,128]{0,2,1:T(8,128)} %get-tuple-element.73), channel_id=1, source_target_pairs={{0,16},{16,32},{32,48},{48,64},{64,80},{80,96},{96,112},{112,128},... | collective-permute-start | bytes 12296 | tf_op jit(solution)/shard_map/ppermute | solution.py:21
Sparse Core Ops, SparseCore 0:
  24.5 129.4 all-gather.1
where the time goes:
time: 462 us; the launch traced here: 461 us
  waiting for transfers between devices  173 us (37%)
  blocking collectives  111 us (24%)
  matrix products  70.5 us (15%)
  starting transfers between devices  32.6 us (7%)
  other arithmetic  30.2 us (7%)
  between operations  27.8 us (6%)
  local copies, waits for them, and re-layouts  15.8 us (3%)
    all_gather x1, waiting for transfers between devices, body(): piece = lax.all_gather(lev_mixed, LON, axis=0, tiled=True)  126 us
    psum x12, blocking collectives, over_axes(): x = lax.psum(x, axis)  111 us
    dot_general x1, matrix products, body(): jnp.einsum('jic,cjl->ijl', lon_table, piece, precision=lax.Precision.HIGH...  63.4 us
    ppermute x7, waiting for transfers between devices, extended(): lax.ppermute(head, axis, [((i + 1) % count, i) for i in range(ends)])  29 us
    ppermute x7, starting transfers between devices, extended(): lax.ppermute(head, axis, [((i + 1) % count, i) for i in range(ends)])  20.9 us
    ppermute x7, waiting for transfers between devices, extended(): lax.ppermute(tail, axis, [(i, (i + 1) % count) for i in range(ends)])  17.5 us
    reduce_sum x3, other arithmetic, inner(): return jnp.sum(first_field * second_field)  14.4 us
    ppermute x7, starting transfers between devices, extended(): lax.ppermute(tail, axis, [(i, (i + 1) % count) for i in range(ends)])  11.6 us
  transfers between devices with their start and end apart: 15, of which 8 were waited for; matrix products, arithmetic and copies ran while one was open for 2% of the time, Pallas kernels for 0%

commit v1 on v0

v1 whole, which is shorter than its diff:
```python
import functools

import jax
import jax.numpy as jnp
from jax import lax
from jax.experimental import pallas as pl
from jax.experimental.pallas import tpu as pltpu
from jax.sharding import Mesh
from jax.sharding import PartitionSpec as P

LON = ("lon_0", "lon_1")
LAT = ("lat_0", "lat_1")
LON_LAT = ("lon_0", "lon_1", "lat_0", "lat_1")
W = 256
R = 8
L = 128
H = 3
E = W + 8
NL = 16
MIB = 1 << 20


def weights(f):
    sixth = 1.0 / 6.0
    return (
        -f * (f - 1.0) * (f - 2.0) * sixth,
        (f + 1.0) * (f - 1.0) * (f - 2.0) * 0.5,
        -(f + 1.0) * f * (f - 2.0) * 0.5,
        (f + 1.0) * f * (f - 1.0) * sixth,
    )


def halves(x):
    high = x.astype(jnp.bfloat16)
    return high, (x - high.astype(jnp.float32)).astype(jnp.bfloat16)


def dot_nt(a, b):
    return lax.dot_general(
        a, b, (((1,), (1,)), ((), ())), preferred_element_type=jnp.float32
    )


def row_of(j):
    return pl.ds(j, W, stride=R)


def edges_kernel(tracer, inverses, metric, up, down, up_inv, down_inv):
    up[...] = tracer[row_of(R - 1), :]
    down[0:W, :] = tracer[row_of(0), :]
    down[W : 2 * W, :] = tracer[row_of(1), :]
    for i in range(H):
        up_inv[i * L : (i + 1) * L, :] = inverses[R - H + i]
        down_inv[i * L : (i + 1) * L, :] = inverses[i]
    sub = lax.broadcasted_iota(jnp.int32, (8, L), 0)
    for ref, first in ((up_inv, R - H), (down_inv, 0)):
        tile = jnp.zeros((8, L), jnp.float32)
        for i in range(H):
            tile = jnp.where(sub == i, metric[first + i], tile)
        ref[H * L : H * L + 8, :] = tile


def mix_kernel(frac_lat, frac_lev, tracer, south, north, out):
    delta = lax.broadcasted_iota(jnp.int32, (L, L), 1) - lax.broadcasted_iota(
        jnp.int32, (L, L), 0
    )

    def row(k):
        if k < 0:
            return south[...]
        if k >= R:
            return north[(k - R) * W : (k - R + 1) * W, :]
        return tracer[row_of(k), :]

    for j in range(R):
        w = weights(frac_lat[j])
        mixed = w[0] * row(j - 1) + w[1] * row(j) + w[2] * row(j + 1) + w[3] * row(j + 2)
        v = weights(frac_lev[j])
        table = jnp.zeros((L, L), jnp.float32)
        for m in range(4):
            table = jnp.where(delta == m - 1, v[m], table)
        t_high, t_low = halves(table)
        m_high, m_low = halves(mixed)
        left = jnp.concatenate(
            [
                jnp.concatenate([t_high, t_high], 1),
                jnp.concatenate([t_low, t_low], 1),
            ],
            0,
        )
        both = dot_nt(left, jnp.concatenate([m_high, m_low], 1))
        turned = (both[:L] + both[L:]).reshape(NL, 8, W)
        out[:, 0, j] = turned[:, :, :128]
        out[:, 1, j] = turned[:, :, 128:]


def shift_kernel(offsets, frac_lon, cells, out, spun):
    lane = lax.broadcasted_iota(jnp.int32, (8, 128), 1)
    blocks = 2 * NL
    for j in range(R):
        w = weights(frac_lon[j])
        off = offsets[j]
        turns = lax.shift_right_logical(off, 7)
        rest = jnp.bitwise_and(off, 127)
        for b in range(blocks):
            here = cells[b, j]
            before = cells[(b - 1) % blocks, j]
            after = cells[(b + 1) % blocks, j]
            west = pltpu.roll(jnp.where(lane == 127, before, here), 1, 1)
            east = pltpu.roll(jnp.where(lane == 0, after, here), 127, 1)
            far = pltpu.roll(jnp.where(lane < 2, after, here), 126, 1)
            value = w[0] * west + w[1] * here + w[2] * east + w[3] * far
            spun[b, j] = pltpu.roll(value, rest, 1)
        moved = []
        for b in range(blocks):
            near = spun[jnp.bitwise_and(b - turns, blocks - 1), j]
            past = spun[jnp.bitwise_and(b - turns - 1, blocks - 1), j]
            moved.append(jnp.where(lane >= rest, near, past))
        for d in range(NL):
            out[d, j] = moved[2 * d]
            out[d, R + j] = moved[2 * d + 1]
            rim = jnp.where(
                lane < 4,
                moved[(2 * d + 2) % blocks],
                pltpu.roll(moved[(2 * d - 1) % blocks], 8, 1),
            )
            if j == 0:
                out[d, 2 * R] = jnp.where(lane < 8, rim, 0.0)
            else:
                rim = pltpu.roll(rim, 8 * j, 1)
                slot = (lane >= 8 * j) & (lane < 8 * j + 8)
                out[d, 2 * R] = jnp.where(slot, rim, out[d, 2 * R])


def turn_kernel(cells, advected, low, middle, high):
    rim = cells[:, 2 * R].reshape(L, 128).T
    for j in range(R):
        if j < H:
            ref, base = low, j
        elif j < R - H:
            ref, base = middle, j - H
        else:
            ref, base = high, j - (R - H)
        for h in range(2):
            tile = cells[:, h * R + j].reshape(L, 128).T
            ref[base, h * 128 : (h + 1) * 128, :] = tile
            advected[pl.ds(h * 128 * R + j, 128, stride=R), :] = tile
        ref[base, W:E, :] = rim[8 * j : 8 * j + 8]


def krylov_kernel(
    metric, vertical, inverses, south_inv, north_inv, south, low, middle, high, north,
    directions, images, sums, field, search,
):
    lane = lax.broadcasted_iota(jnp.int32, (1, L), 1)
    coef = vertical[...]
    upper_coef = jnp.where(lane == L - 1, 0.0, coef)
    lower_coef = jnp.where(lane == 0, 0.0, coef)

    def start(j):
        if j < 0:
            return south[j + H]
        if j < H:
            return low[j]
        if j < R - H:
            return middle[j - H]
        if j < R:
            return high[j - (R - H)]
        return north[j - R]

    def inverse(j):
        if j < 0:
            return south_inv[(j + H) * L : (j + H + 1) * L, :]
        if j >= R:
            return north_inv[(j - R) * L : (j - R + 1) * L, :]
        return inverses[j]

    def metric_of(j):
        if j < 0:
            return south_inv[H * L + j + H : H * L + j + H + 1, :]
        if j >= R:
            return north_inv[H * L + j - R : H * L + j - R + 1, :]
        return jnp.full((1, L), metric[j], jnp.float32)

    def precondition(j, value):
        m_high, m_low = halves(inverse(j))
        v_high, v_low = halves(value)
        right = jnp.concatenate(
            [
                jnp.concatenate([m_high, m_high], 1),
                jnp.concatenate([m_low, m_low], 1),
            ],
            0,
        )
        both = dot_nt(jnp.concatenate([v_high, v_low], 1), right)
        return both[:, :L] + both[:, L:]

    totals = [jnp.zeros((8, L), jnp.float32) for _ in range(9)]

    def add(index, a, b):
        totals[index] = totals[index] + jnp.sum((a * b).reshape(W // 8, 8, L), 0)

    for depth in range(3):
        reach = H - depth
        for j in range(-reach, R + reach):
            value = start(j) if depth == 0 else field[j + H]
            search[j + H] = precondition(j, value)
        for j in range(-reach + 1, R + reach - 1):
            q = search[j + H]
            m = metric_of(j)
            result = q * (2.0 * m + 2.0 * coef + 2.1)
            result = result - m * (pltpu.roll(q, 1, 0) + pltpu.roll(q, E - 1, 0))
            result = result - (search[j + H - 1] + search[j + H + 1])
            result = result - upper_coef * pltpu.roll(q, L - 1, 1)
            result = result - lower_coef * pltpu.roll(q, 1, 1)
            field[j + H] = result
            if 0 <= j < R:
                own = result[:W]
                directions[depth, j] = q[:W]
                images[depth, j] = own
                add(depth, start(j)[:W], own)
                for other in range(depth):
                    add(3 + depth * (depth + 1) // 2 + other, images[other, j], own)
                add(3 + depth * (depth + 1) // 2 + depth, own, own)
    row = jnp.zeros((1, L), jnp.float32)
    for index in range(9):
        total = jnp.sum(jnp.sum(totals[index], 0, keepdims=True), 1, keepdims=True)
        row = jnp.where(lane == index, total, row)
    sums[...] = jnp.broadcast_to(row, sums.shape)


def finish_kernel(sums, low, middle, high, directions, images, pressure, residual):
    lane = lax.broadcasted_iota(jnp.int32, (1, L), 1)
    row = jnp.sum(sums[...], 0, keepdims=True)

    def entry(index):
        value = jnp.sum(jnp.where(lane == index, row, 0.0), 1, keepdims=True)
        return jnp.broadcast_to(value, (1, L))

    b1, b2, b3, g11, g12, g22, g13, g23, g33 = (entry(i) for i in range(9))
    l21 = g12 / g11
    l31 = g13 / g11
    d2 = g22 - l21 * g12
    cross = g23 - l21 * g13
    l32 = cross / d2
    d3 = g33 - l31 * g13 - l32 * cross
    c2 = b2 - l21 * b1
    y1 = b1 / g11
    y2 = c2 / d2
    y3 = (b3 - l31 * b1 - l32 * c2) / d3
    k3 = y3
    k2 = y2 - l32 * k3
    k1 = y1 - l21 * k2 - l31 * k3
    for j in range(R):
        if j < H:
            first = low[j, :W]
        elif j < R - H:
            first = middle[j - H, :W]
        else:
            first = high[j - (R - H), :W]
        pressure[row_of(j), :] = (
            k1 * directions[0, j] + k2 * directions[1, j] + k3 * directions[2, j]
        )
        residual[row_of(j), :] = (
            first - k1 * images[0, j] - k2 * images[1, j] - k3 * images[2, j]
        )


VMEM = pl.BlockSpec(memory_space=pltpu.VMEM)
SMEM = pl.BlockSpec(memory_space=pltpu.SMEM)


def call(kernel, ins, outs, scratch=(), limit=32, cost=(0, 4 * MIB)):
    return pl.pallas_call(
        kernel,
        out_shape=tuple(jax.ShapeDtypeStruct(s, jnp.float32) for s in outs),
        in_specs=list(ins),
        out_specs=tuple(VMEM for _ in outs),
        scratch_shapes=[pltpu.VMEM(s, jnp.float32) for s in scratch],
        compiler_params=pltpu.CompilerParams(vmem_limit_bytes=limit * MIB),
        cost_estimate=pl.CostEstimate(
            flops=cost[0], bytes_accessed=cost[1], transcendentals=0
        ),
    )


def body(count, tracer, offsets, frac_lon, frac_lat, frac_lev, metric, vertical_coef, inverses):
    north_of = [(i, i + 1) for i in range(count - 1)]
    south_of = [(i + 1, i) for i in range(count - 1)]
    flat = tracer.reshape(W * R, L)
    up, down, up_inv, down_inv = call(
        edges_kernel,
        (VMEM, VMEM, SMEM),
        ((W, L), (2 * W, L), (H * L + 8, L), (H * L + 8, L)),
    )(flat, inverses, metric)
    south_row = lax.ppermute(up, LAT, north_of)
    north_rows = lax.ppermute(down, LAT, south_of)
    south_inv = lax.ppermute(up_inv, LAT, north_of)
    north_inv = lax.ppermute(down_inv, LAT, south_of)
    (turned,) = call(
        mix_kernel, (SMEM, SMEM, VMEM, VMEM, VMEM), ((NL, 2, R, 8, 128),)
    )(frac_lat, frac_lev, flat, south_row, north_rows)
    lines = lax.all_to_all(turned, LON, 0, 0, tiled=True)
    (moved,) = call(
        shift_kernel,
        (SMEM, SMEM, VMEM),
        ((NL, 2 * R + 1, 8, 128),),
        scratch=((2 * NL, R, 8, 128),),
    )(offsets, frac_lon, lines.reshape(2 * NL, R, 8, 128))
    back = lax.all_to_all(moved, LON, 0, 0, tiled=True)
    advected, low, middle, high = call(
        turn_kernel,
        (VMEM,),
        ((W * R, L), (H, E, L), (R - 2 * H, E, L), (H, E, L)),
    )(back)
    south = lax.ppermute(high, LAT, north_of)
    north = lax.ppermute(low, LAT, south_of)
    directions, images, sums = call(
        krylov_kernel,
        (SMEM,) + (VMEM,) * 9,
        ((3, R, W, L), (3, R, W, L), (count * NL, L)),
        scratch=((R + 2 * H, E, L), (R + 2 * H, E, L)),
    )(metric, vertical_coef.reshape(1, L), inverses, south_inv, north_inv, south, low, middle, high, north)
    gathered = lax.all_to_all(sums, LON_LAT, 0, 0, tiled=True)
    pressure, residual = call(
        finish_kernel, (VMEM,) * 6, ((W * R, L), (W * R, L))
    )(gathered, low, middle, high, directions, images)
    return tuple(x.reshape(W, R, L) for x in (advected, pressure, residual))


def solution(mesh):
    count = mesh.shape["lat"]
    split = Mesh(mesh.devices.reshape(4, 4, count // 2, 2), LON_LAT)
    placed = (P(LON, LAT, None), P(LAT), P(LAT), P(LAT), P(LAT), P(LAT), P(), P(LAT, None, None))
    return jax.shard_map(
        functools.partial(body, count),
        mesh=split,
        in_specs=placed,
        out_specs=(P(LON, LAT, None),) * 3,
        check_vma=False,
    )
```

time: 462 us -> 126 us (0.27)
  waiting for transfers between devices: 173 us -> 7.04 us
  matrix products: 70.5 us -> 0 us
  blocking collectives: 111 us -> 65.2 us
  other arithmetic: 30.2 us -> 0 us
  Pallas kernels: 0 us -> 28.4 us
  between operations: 27.8 us -> 0.77 us
  starting transfers between devices: 32.6 us -> 19.6 us
  local copies, waits for them, and re-layouts: 15.8 us -> 4.26 us
    all_gather x1 -> x0, waiting for transfers between devices: 126 us -> none  [body(): piece = lax.all_gather(lev_mixed, LON, axis=0, tiled=True)]
    psum x12 -> x0, blocking collectives: 111 us -> none  [over_axes(): x = lax.psum(x, axis)]
    dot_general x5 -> x0, matrix products: 70.5 us -> none  [the longest x1 63.4 us: body(): jnp.einsum('jic,cjl->ijl', lon_table, piece, precision=lax.Precision.HIGH...]
    all_to_all x0 -> x3, blocking collectives: none -> 65.2 us  [the longest x1 22.2 us: body(): lines = lax.all_to_all(turned, LON, 0, 0, tiled=True)]
    ppermute x14 -> x6, waiting for transfers between devices: 46.6 us -> 7.04 us  [the longest x1 4.4 us: body(): north_inv = lax.ppermute(down_inv, LAT, south_of)]
    pallas_call x0 -> x6, Pallas kernels: none -> 28.4 us  [the longest x1 17.5 us: body(): call(shift_kernel, (SMEM, SMEM, VMEM), ((NL, 2 * R + 1, 8, 128),), scratc...]
    reduce_sum x3 -> x0, other arithmetic: 14.4 us -> none  [inner(): return jnp.sum(first_field * second_field)]
    ppermute x14 -> x6, starting transfers between devices: 32.6 us -> 19.6 us  [the longest x1 5.15 us: body(): north_rows = lax.ppermute(down, LAT, south_of)]
  transfers between devices with their start and end apart: 15 -> 6, of which waited for: 8 -> 3; matrix products, arithmetic and copies ran while one was open for 2% -> 0% of each run, Pallas kernels for 0% -> 0%
where the time goes in v1:
time: 126 us; the launch traced here: 125 us
  blocking collectives  65.2 us (52%)
  Pallas kernels  28.4 us (23%)
  starting transfers between devices  19.6 us (16%)
  waiting for transfers between devices  7.04 us (6%)
  local copies, waits for them, and re-layouts  4.26 us (3%)
    all_to_all x1, blocking collectives, body(): lines = lax.all_to_all(turned, LON, 0, 0, tiled=True)  22.2 us
    all_to_all x1, blocking collectives, body(): gathered = lax.all_to_all(sums, LON_LAT, 0, 0, tiled=True)  21.8 us
    all_to_all x1, blocking collectives, body(): back = lax.all_to_all(moved, LON, 0, 0, tiled=True)  21.3 us
    pallas_call x1, Pallas kernels, body(): call(shift_kernel, (SMEM, SMEM, VMEM), ((NL, 2 * R + 1, 8, 128),), scratc...  17.5 us
    ppermute x1, starting transfers between devices, body(): north_rows = lax.ppermute(down, LAT, south_of)  5.15 us
    pallas_call x1, Pallas kernels, body(): call(krylov_kernel, (SMEM,) + (VMEM,) * 9, ((3, R, W, L), (3, R, W, L), (...  5.1 us
    ppermute x1, starting transfers between devices, body(): south = lax.ppermute(high, LAT, north_of)  5.09 us
    ppermute x1, waiting for transfers between devices, body(): north_inv = lax.ppermute(down_inv, LAT, south_of)  4.4 us
  transfers between devices with their start and end apart: 6, of which 3 were waited for; matrix products, arithmetic and copies ran while one was open for 0% of the time, Pallas kernels for 0%

profile of v1, /device:TPU:1, one launch (start us, length us, event | category | flops | bytes accessed | tf_op | source)
XLA Modules:
  0.0 125.3 jit_solution(6757324285999606815)
XLA Ops:
  0.7 1.2 copy-done
  1.9 1.0 copy-done.1
  2.9 0.7 copy-done.3
  3.6 0.6 shard_map.103
  4.2 5.1 %collective-permute-start.1 = (f32[512,128]{1,0:T(8,128)S(1)}, f32[512,128]{1,0:T(8,128)S(1)}, u32[]{:S(2)}, u32[]{:S(2)}) collective-permute-start(f32[512,128]{1,0:T(8,128)S(1)} %get-tuple-element.17), channel_id=1, source_target_pairs={{1,0},{2,1},{3,2},{4,3},{5,4},{6,5},{7,6},{8,7},{9,8},{10,9},{11,1... | collective-permute-start | bytes 786440 | tf_op jit(solution)/shard_map/ppermute | solution.py:297
  9.4 1.9 %collective-permute-start = (f32[256,128]{1,0:T(8,128)S(1)}, f32[256,128]{1,0:T(8,128)S(1)}, u32[]{:S(2)}, u32[]{:S(2)}) collective-permute-start(f32[256,128]{1,0:T(8,128)S(1)} %get-tuple-element.16), channel_id=1, source_target_pairs={{0,1},{1,2},{2,3},{3,4},{4,5},{5,6},{6,7},{7,8},{8,9},{9,10},{10,1... | collective-permute-start | bytes 393224 | tf_op jit(solution)/shard_map/ppermute | solution.py:296
  11.3 1.9 %collective-permute-done.south = f32[256,128]{1,0:T(8,128)S(1)} collective-permute-done((f32[256,128]{1,0:T(8,128)S(1)}, f32[256,128]{1,0:T(8,128)S(1)}, u32[]{:S(2)}, u32[]{:S(2)}) %collective-permute-start) | collective-permute-done | bytes 131104 | tf_op jit(solution)/shard_map/ppermute | solution.py:296
  13.3 0.0 collective-permute-done.1.north
  13.3 0.7 copy-done.5
  13.9 0.7 copy-done.6
  14.6 1.3 %shard_map.104 = f32[16,2,8,8,128]{4,3,2,1,0:T(8,128)S(1)} custom-call(f32[8]{0:T(128)S(1)} %copy-done.5, f32[8]{0:T(128)S(1)} %copy-done.6, f32[2048,128]{1,0:T(8,128)S(1)} %bitcast.11, f32[256,128]{1,0:T(8,128)S(1)} %collective-permute-done.south, f32[512,128]{1,0:T(8,128)S(1)} %collective-permute-done.1.north), custom_call_target="tpu_custom_call" | custom-call | bytes 4194304 | tf_op jit(solution)/shard_map/pallas_call | solution.py:300
  15.9 22.2 %all_to_all.21 = f32[16,2,8,8,128]{4,3,2,1,0:T(8,128)S(1)} all-to-all(f32[16,2,8,8,128]{4,3,2,1,0:T(8,128)S(1)} %shard_map.104), channel_id=1, replica_groups=mesh['lon_0'=4,'lon_1'=4,'lat_0'=8,'lat_1'=2] {'lon_0','lon_1'}, dimensions={0} | all-to-all | bytes 2097152 | tf_op jit(solution)/shard_map/all_to_all | solution.py:303
  38.1 17.5 %shard_map.105 = f32[16,17,8,128]{3,2,1,0:T(8,128)S(1)} custom-call(s32[8]{0:T(128)S(1)} %copy-done.8, f32[8]{0:T(128)S(1)} %copy-done.9, f32[32,8,8,128]{3,2,1,0:T(8,128)S(1)} %bitcast.12), custom_call_target="tpu_custom_call" | custom-call | bytes 4194304 | tf_op jit(solution)/shard_map/pallas_call | solution.py:304
  55.6 21.3 %all_to_all.22.cells = f32[16,17,8,128]{3,2,1,0:T(8,128)S(1)} all-to-all(f32[16,17,8,128]{3,2,1,0:T(8,128)S(1)} %shard_map.105), channel_id=1, replica_groups=mesh['lon_0'=4,'lon_1'=4,'lat_0'=8,'lat_1'=2] {'lon_0','lon_1'}, dimensions={0} | all-to-all | bytes 2228224 | tf_op jit(solution)/shard_map/all_to_all | solution.py:310
  76.9 1.3 %shard_map.106 = (f32[2048,128]{1,0:T(8,128)}, f32[3,264,128]{2,1,0:T(8,128)S(1)}, f32[2,264,128]{2,1,0:T(8,128)S(1)}, f32[3,264,128]{2,1,0:T(8,128)S(1)}) custom-call(f32[16,17,8,128]{3,2,1,0:T(8,128)S(1)} %all_to_all.22.cells), custom_call_target="tpu_custom_call" | custom-call | bytes 4194304 | tf_op jit(solution)/shard_map/pallas_call | solution.py:311
  78.2 5.1 %collective-permute-start.4 = (f32[3,264,128]{2,1,0:T(8,128)S(1)}, f32[3,264,128]{2,1,0:T(8,128)S(1)}, u32[]{:S(2)}, u32[]{:S(2)}) collective-permute-start(f32[3,264,128]{2,1,0:T(8,128)S(1)} %get-tuple-element.21.high), channel_id=1, source_target_pairs={{0,1},{1,2},{2,3},{3,4},{4,5},{5,6},{6,7},{7,8},{8,9},{9,10},{10,1... | collective-permute-start | bytes 1216520 | tf_op jit(solution)/shard_map/ppermute | solution.py:316
  83.3 1.9 %collective-permute-start.5 = (f32[3,264,128]{2,1,0:T(8,128)S(1)}, f32[3,264,128]{2,1,0:T(8,128)S(1)}, u32[]{:S(2)}, u32[]{:S(2)}) collective-permute-start(f32[3,264,128]{2,1,0:T(8,128)S(1)} %get-tuple-element.22.low), channel_id=1, source_target_pairs={{1,0},{2,1},{3,2},{4,3},{5,4},{6,5},{7,6},{8,7},{9,8},{10,9},{11,1... | collective-permute-start | bytes 1216520 | tf_op jit(solution)/shard_map/ppermute | solution.py:317
  85.3 3.6 %collective-permute-start.2 = (f32[392,128]{1,0:T(8,128)S(1)}, f32[392,128]{1,0:T(8,128)S(1)}, u32[]{:S(2)}, u32[]{:S(2)}) collective-permute-start(f32[392,128]{1,0:T(8,128)S(1)} %get-tuple-element.19), channel_id=1, source_target_pairs={{0,1},{1,2},{2,3},{3,4},{4,5},{5,6},{6,7},{7,8},{8,9},{9,10},{10,1... | collective-permute-start | bytes 602120 | tf_op jit(solution)/shard_map/ppermute | solution.py:298
  88.9 1.9 %collective-permute-start.3 = (f32[392,128]{1,0:T(8,128)S(1)}, f32[392,128]{1,0:T(8,128)S(1)}, u32[]{:S(2)}, u32[]{:S(2)}) collective-permute-start(f32[392,128]{1,0:T(8,128)S(1)} %get-tuple-element.20), channel_id=1, source_target_pairs={{1,0},{2,1},{3,2},{4,3},{5,4},{6,5},{7,6},{8,7},{9,8},{10,9},{11,1... | collective-permute-start | bytes 602120 | tf_op jit(solution)/shard_map/ppermute | solution.py:299
  90.8 0.7 collective-permute-done.2.south_inv
  91.5 4.4 %collective-permute-done.3.north_inv = f32[392,128]{1,0:T(8,128)S(1)} collective-permute-done((f32[392,128]{1,0:T(8,128)S(1)}, f32[392,128]{1,0:T(8,128)S(1)}, u32[]{:S(2)}, u32[]{:S(2)}) %collective-permute-start.3) | collective-permute-done | bytes 200736 | tf_op jit(solution)/shard_map/ppermute | solution.py:299
  96.0 5.1 %shard_map.107 = (f32[3,8,256,128]{3,2,1,0:T(8,128)S(1)}, f32[3,8,256,128]{3,2,1,0:T(8,128)S(1)}, f32[256,128]{1,0:T(8,128)S(1)}) custom-call(f32[8]{0:T(128)S(1)} %copy-done.4, f32[1,128]{1,0:T(1,128)S(1)} %bitcast.15, f32[8,128,128]{2,1,0:T(8,128)S(1)} %copy-done.2, f32[392,128]{1,0:T(8,128)S(1)} %collective-permute-done.2.south_inv, ...), custom_call_target="tpu_custom_call" | custom-call | bytes 4194304 | tf_op jit(solution)/shard_map/pallas_call | solution.py:318
  101.1 21.8 %all_to_all.23 = f32[256,1,128]{2,1,0:T(1,128)S(1)} all-to-all(f32[256,1,128]{2,1,0:T(1,128)S(1)} %bitcast.14), channel_id=1, replica_groups=mesh['lon_0'=4,'lon_1'=4,'lat_0'=8,'lat_1'=2] {'lon_0','lon_1','lat_0','..., dimensions={0} | all-to-all | bytes 262144 | tf_op jit(solution)/shard_map/all_to_all | solution.py:324
  122.8 2.5 %shard_map.108 = (f32[2048,128]{1,0:T(8,128)}, f32[2048,128]{1,0:T(8,128)}) custom-call(f32[256,128]{1,0:T(8,128)S(1)} %bitcast.13, f32[3,264,128]{2,1,0:T(8,128)S(1)} %get-tuple-element.22.low, f32[2,264,128]{2,1,0:T(8,128)S(1)} %get-tuple-element.23.middle, f32[3,264,128]{2,1,0:T(8,128)S(1)} %get-tuple-element.21.high, ...), custom_call_target="tpu_custom_call" | custom-call | bytes 4194304 | tf_op jit(solution)/shard_map/pallas_call | solution.py:325
  (17 shorter events, 0.0 us)
Async XLA Ops:
  0.6 37.5 %copy-start.9 = (f32[8]{0:T(128)S(1)}, f32[8]{0:T(128)}, u32[]{:S(2)}) copy-start(f32[8]{0:T(128)} %frac_lon.1) | copy-start | bytes 100
  0.6 37.5 %copy-start.8 = (s32[8]{0:T(128)S(1)}, s32[8]{0:T(128)}, u32[]{:S(2)}) copy-start(s32[8]{0:T(128)} %offsets.1) | copy-start | bytes 100
  0.7 1.2 copy-start
  1.9 1.0 copy-start.1
  2.9 0.7 copy-start.3
  4.2 9.0 %collective-permute-start.1 = (f32[512,128]{1,0:T(8,128)S(1)}, f32[512,128]{1,0:T(8,128)S(1)}, u32[]{:S(2)}, u32[]{:S(2)}) collective-permute-start(f32[512,128]{1,0:T(8,128)S(1)} %get-tuple-element.17), channel_id=1, source_target_pairs={{1,0},{2,1},{3,2},{4,3},{5,4},{6,5},{7,6},{8,7},{9,8},{10,9},{11,1... | collective-permute-start | bytes 786440 | tf_op jit(solution)/shard_map/ppermute | solution.py:297
  9.4 3.9 %collective-permute-start = (f32[256,128]{1,0:T(8,128)S(1)}, f32[256,128]{1,0:T(8,128)S(1)}, u32[]{:S(2)}, u32[]{:S(2)}) collective-permute-start(f32[256,128]{1,0:T(8,128)S(1)} %get-tuple-element.16), channel_id=1, source_target_pairs={{0,1},{1,2},{2,3},{3,4},{4,5},{5,6},{6,7},{7,8},{8,9},{9,10},{10,1... | collective-permute-start | bytes 393224 | tf_op jit(solution)/shard_map/ppermute | solution.py:296
  13.3 0.7 copy-start.5
  13.9 0.7 copy-start.6
  38.1 57.9 %copy-start.2 = (f32[8,128,128]{2,1,0:T(8,128)S(1)}, f32[8,128,128]{2,1,0:T(8,128)}, u32[]{:S(2)}) copy-start(f32[8,128,128]{2,1,0:T(8,128)} %inverses.3) | copy-start | bytes 1572868
  38.1 57.9 %copy-start.4 = (f32[8]{0:T(128)S(1)}, f32[8]{0:T(128)}, u32[]{:S(2)}) copy-start(f32[8]{0:T(128)} %metric.3) | copy-start | bytes 100
  38.1 57.9 %copy-start.7 = (f32[128]{0:T(128)S(1)}, f32[128]{0:T(128)}, u32[]{:S(2)}) copy-start(f32[128]{0:T(128)} %param.14) | copy-start | bytes 1540
  78.2 17.7 %collective-permute-start.4 = (f32[3,264,128]{2,1,0:T(8,128)S(1)}, f32[3,264,128]{2,1,0:T(8,128)S(1)}, u32[]{:S(2)}, u32[]{:S(2)}) collective-permute-start(f32[3,264,128]{2,1,0:T(8,128)S(1)} %get-tuple-element.21.high), channel_id=1, source_target_pairs={{0,1},{1,2},{2,3},{3,4},{4,5},{5,6},{6,7},{7,8},{8,9},{9,10},{10,1... | collective-permute-start | bytes 1216520 | tf_op jit(solution)/shard_map/ppermute | solution.py:316
  83.3 12.6 %collective-permute-start.5 = (f32[3,264,128]{2,1,0:T(8,128)S(1)}, f32[3,264,128]{2,1,0:T(8,128)S(1)}, u32[]{:S(2)}, u32[]{:S(2)}) collective-permute-start(f32[3,264,128]{2,1,0:T(8,128)S(1)} %get-tuple-element.22.low), channel_id=1, source_target_pairs={{1,0},{2,1},{3,2},{4,3},{5,4},{6,5},{7,6},{8,7},{9,8},{10,9},{11,1... | collective-permute-start | bytes 1216520 | tf_op jit(solution)/shard_map/ppermute | solution.py:317
  85.3 6.3 %collective-permute-start.2 = (f32[392,128]{1,0:T(8,128)S(1)}, f32[392,128]{1,0:T(8,128)S(1)}, u32[]{:S(2)}, u32[]{:S(2)}) collective-permute-start(f32[392,128]{1,0:T(8,128)S(1)} %get-tuple-element.19), channel_id=1, source_target_pairs={{0,1},{1,2},{2,3},{3,4},{4,5},{5,6},{6,7},{7,8},{8,9},{9,10},{10,1... | collective-permute-start | bytes 602120 | tf_op jit(solution)/shard_map/ppermute | solution.py:298
  88.9 7.0 %collective-permute-start.3 = (f32[392,128]{1,0:T(8,128)S(1)}, f32[392,128]{1,0:T(8,128)S(1)}, u32[]{:S(2)}, u32[]{:S(2)}) collective-permute-start(f32[392,128]{1,0:T(8,128)S(1)} %get-tuple-element.20), channel_id=1, source_target_pairs={{1,0},{2,1},{3,2},{4,3},{5,4},{6,5},{7,6},{8,7},{9,8},{10,9},{11,1... | collective-permute-start | bytes 602120 | tf_op jit(solution)/shard_map/ppermute | solution.py:299

commit v2 on v1

v2 whole, which is shorter than its diff:
```python
import functools

import jax
import jax.numpy as jnp
from jax import lax
from jax.experimental import pallas as pl
from jax.experimental.pallas import tpu as pltpu
from jax.sharding import Mesh
from jax.sharding import PartitionSpec as P

LON = ("lon_0", "lon_1")
LAT = ("lat_0", "lat_1")
LON_LAT = ("lon_0", "lon_1", "lat_0", "lat_1")
W = 256
R = 8
L = 128
H = 3
E = W + 8
NL = 16
B = 2 * NL
T = H * E
MIB = 1 << 20


def weights(f):
    sixth = 1.0 / 6.0
    return (
        -f * (f - 1.0) * (f - 2.0) * sixth,
        (f + 1.0) * (f - 1.0) * (f - 2.0) * 0.5,
        -(f + 1.0) * f * (f - 2.0) * 0.5,
        (f + 1.0) * f * (f - 1.0) * sixth,
    )


def halves(x):
    high = x.astype(jnp.bfloat16)
    return high, (x - high.astype(jnp.float32)).astype(jnp.bfloat16)


def dot_nt(a, b):
    return lax.dot_general(
        a, b, (((1,), (1,)), ((), ())), preferred_element_type=jnp.float32
    )


def row_of(j):
    return pl.ds(j, W, stride=R)


def is_even():
    return lax.axis_index("lat_1") == 0


def edges_kernel(tracer, pair, cross):
    even = is_even()
    last = tracer[row_of(R - 1), :]
    first = tracer[row_of(0), :]
    second = tracer[row_of(1), :]
    pair[0:W] = jnp.where(even, last, first)
    pair[W : 2 * W] = second
    cross[0:W] = jnp.where(even, first, last)
    cross[W : 2 * W] = second


def mix_kernel(fractions, tracer, pair, cross, out):
    even = is_even()
    delta = lax.broadcasted_iota(jnp.int32, (L, L), 1) - lax.broadcasted_iota(
        jnp.int32, (L, L), 0
    )

    def row(k):
        if k < 0:
            return jnp.where(even, cross[0:W], pair[0:W])
        if k >= R:
            part = slice((k - R) * W, (k - R + 1) * W)
            return jnp.where(even, pair[part], cross[part])
        return tracer[row_of(k), :]

    for j in range(R):
        w = weights(fractions[j : j + 1, :])
        mixed = w[0] * row(j - 1) + w[1] * row(j) + w[2] * row(j + 1) + w[3] * row(j + 2)
        v = weights(fractions[R + j : R + j + 1, :])
        table = jnp.zeros((L, L), jnp.float32)
        for m in range(4):
            table = jnp.where(delta == m - 1, v[m], table)
        t_high, t_low = halves(table)
        m_high, m_low = halves(mixed)
        left = jnp.concatenate(
            [
                jnp.concatenate([t_high, t_high], 1),
                jnp.concatenate([t_low, t_low], 1),
            ],
            0,
        )
        both = dot_nt(left, jnp.concatenate([m_high, m_low], 1))
        turned = (both[:L] + both[L:]).reshape(NL, 8, W)
        out[:, 0, j] = turned[:, :, :128]
        out[:, 1, j] = turned[:, :, 128:]


def shift_kernel(offsets, frac_lon, cells, out, twice):
    delta = lax.broadcasted_iota(jnp.int32, (128, 128), 0) - lax.broadcasted_iota(
        jnp.int32, (128, 128), 1
    )
    lane = lax.broadcasted_iota(jnp.int32, (1, 1, 128), 2)
    rims = jnp.zeros((NL, 8, 128), jnp.float32)
    for j in range(R):
        w = weights(frac_lon[j])
        off = offsets[j]
        turns = lax.shift_right_logical(off, 7)
        rest = jnp.bitwise_and(off, 127)
        placed = delta + rest
        left, right_high, right_low = [], [], []
        for k in range(3):
            table = jnp.zeros((128, 128), jnp.float32)
            for m in range(4):
                table = jnp.where(placed == m - 1 - 128 * (k - 1), w[m], table)
            t_high, t_low = halves(table)
            right_high += [t_high, t_high]
            right_low += [t_low, t_low]
            if k == 0:
                part = jnp.concatenate([cells[B - 1 :, j], cells[: B - 1, j]], 0)
            elif k == 1:
                part = cells[:, j]
            else:
                part = jnp.concatenate([cells[1:, j], cells[:1, j]], 0)
            left += list(halves(part.reshape(B * 8, 128)))
        right = jnp.concatenate(
            [jnp.concatenate(right_high, 0), jnp.concatenate(right_low, 0)], 1
        )
        both = jnp.dot(
            jnp.concatenate(left, 1), right, preferred_element_type=jnp.float32
        )
        value = (both[:, :128] + both[:, 128:]).reshape(B, 8, 128)
        twice[j, :B] = value
        twice[j, B:] = value
        start = jnp.bitwise_and(B - turns, B - 1)
        moved = twice[j, pl.ds(start, B)].reshape(NL, 2, 8, 128)
        near, far = moved[:, 0], moved[:, 1]
        out[:, j] = near
        out[:, R + j] = far
        east = jnp.concatenate([near[1:], near[:1]], 0)
        west = jnp.concatenate([far[NL - 1 :], far[: NL - 1]], 0)
        rim = jnp.where(lane < 64, east, west)
        if j > 0:
            rim = pltpu.roll(rim, 8 * j, 2)
        rims = jnp.where(jnp.bitwise_and(lane + (4 - 8 * j), 127) < 8, rim, rims)
    out[:, 2 * R] = rims


def turn_kernel(metric, inverses, cells, advected, ring, pair, cross):
    even = is_even()
    rim = cells[:, 2 * R].reshape(L, 128).T
    sub = lax.broadcasted_iota(jnp.int32, (8, L), 0)
    for j in range(R):
        for h in range(2):
            tile = cells[:, h * R + j].reshape(L, 128).T
            ring[j, h * 128 : (h + 1) * 128, :] = tile
            advected[pl.ds(h * 128 * R + j, 128, stride=R), :] = tile
        before = (8 * j - 8) % 128
        tail = jnp.where(sub < 4, rim[8 * j : 8 * j + 8], rim[before : before + 8])
        ring[j, W:E, :] = jnp.where(sub == 3, metric[j], tail)
    for i in range(H):
        for base, size, high, low in (
            (i * E, E, ring[R - H + i], ring[i]),
            (T + i * L, L, inverses[R - H + i], inverses[i]),
        ):
            pair[base : base + size] = jnp.where(even, high, low)
            cross[base : base + size] = jnp.where(even, low, high)


def vertical_rows(vertical):
    lane = lax.broadcasted_iota(jnp.int32, (1, L), 1)
    coef = vertical[...]
    return coef, jnp.where(lane == L - 1, 0.0, coef), jnp.where(lane == 0, 0.0, coef)


def precondition(inverse, value):
    m_high, m_low = halves(inverse)
    v_high, v_low = halves(value)
    right = jnp.concatenate(
        [
            jnp.concatenate([m_high, m_high], 1),
            jnp.concatenate([m_low, m_low], 1),
        ],
        0,
    )
    both = dot_nt(jnp.concatenate([v_high, v_low], 1), right)
    return both[:, :L] + both[:, L:]


def operate(q, south, north, m, rows):
    coef, upper, lower = rows
    result = q * (2.0 * m + 2.0 * coef + 2.1)
    result = result - m * (pltpu.roll(q, 1, 0) + pltpu.roll(q, E - 1, 0))
    result = result - (south + north)
    result = result - upper * pltpu.roll(q, L - 1, 1)
    return result - lower * pltpu.roll(q, 1, 1)


def partial(a, b):
    return jnp.sum((a[:W] * b[:W]).reshape(W // 8, 8, L), 0)


def gram(depth, other):
    return 3 + depth * (depth + 1) // 2 + other


def inside(depth, j):
    return depth < j < R - 1 - depth


def inner_kernel(metric, vertical, inverses, ring, search, field, totals):
    rows = vertical_rows(vertical)
    sums = [jnp.zeros((8, L), jnp.float32) for _ in range(9)]
    for depth in range(3):
        for j in range(depth, R - depth):
            search[depth, j] = precondition(
                inverses[j], ring[j] if depth == 0 else field[depth - 1, j]
            )
        for j in range(depth + 1, R - 1 - depth):
            result = operate(
                search[depth, j], search[depth, j - 1], search[depth, j + 1],
                jnp.full((1, L), metric[j], jnp.float32), rows,
            )
            field[depth, j] = result
            sums[depth] = sums[depth] + partial(ring[j], result)
            for other in range(depth):
                k = gram(depth, other)
                sums[k] = sums[k] + partial(field[other, j], result)
            k = gram(depth, depth)
            sums[k] = sums[k] + partial(result, result)
    for k in range(9):
        totals[k] = sums[k]


def outer_kernel(
    metric, vertical, inverses, ring, pair, cross, search, field, totals,
    new_search, new_field, sums_out, wide,
):
    even = is_even()
    lane = lax.broadcasted_iota(jnp.int32, (1, L), 1)
    rows = vertical_rows(vertical)
    sums = [totals[k] for k in range(9)]

    def beyond(j, base, size):
        part = slice(base, base + size)
        first, second = (cross, pair) if j < 0 else (pair, cross)
        return jnp.where(even, first[part], second[part])

    def inverse(j):
        if 0 <= j < R:
            return inverses[j]
        return beyond(j, T + (j + H if j < 0 else j - R) * L, L)

    def metric_of(j):
        if 0 <= j < R:
            return jnp.full((1, L), metric[j], jnp.float32)
        return beyond(j, (j + H if j < 0 else j - R) * E + W + 3, 1)

    def start(j):
        if 0 <= j < R:
            return ring[j]
        return beyond(j, (j + H if j < 0 else j - R) * E, E)

    def image(depth, j):
        if inside(depth, j):
            return field[depth, j]
        if 0 <= j < R:
            return new_field[depth, j]
        return wide[1, depth, j + H if j < 0 else j - R + H]

    def direction(depth, j):
        if depth <= j < R - depth:
            return search[depth, j]
        if 0 <= j < R:
            return new_search[depth, j]
        return wide[0, depth, j + H if j < 0 else j - R + H]

    for depth in range(3):
        reach = H - depth
        for j in range(-reach, R + reach):
            if depth <= j < R - depth:
                continue
            value = precondition(
                inverse(j), start(j) if depth == 0 else image(depth - 1, j)
            )
            if 0 <= j < R:
                new_search[depth, j] = value
            else:
                wide[0, depth, j + H if j < 0 else j - R + H] = value
        for j in range(-reach + 1, R + reach - 1):
            if inside(depth, j):
                continue
            result = operate(
                direction(depth, j), direction(depth, j - 1), direction(depth, j + 1),
                metric_of(j), rows,
            )
            if not 0 <= j < R:
                wide[1, depth, j + H if j < 0 else j - R + H] = result
                continue
            new_field[depth, j] = result
            sums[depth] = sums[depth] + partial(start(j), result)
            for other in range(depth):
                k = gram(depth, other)
                sums[k] = sums[k] + partial(image(other, j), result)
            k = gram(depth, depth)
            sums[k] = sums[k] + partial(result, result)
    row = jnp.zeros((1, L), jnp.float32)
    for k in range(9):
        total = jnp.sum(jnp.sum(sums[k], 0, keepdims=True), 1, keepdims=True)
        row = jnp.where(lane == k, total, row)
    sums_out[...] = jnp.broadcast_to(row, sums_out.shape)


def finish_kernel(
    sums, ring, search, field, new_search, new_field, pressure, residual, held, left, sems
):
    lane = lax.broadcasted_iota(jnp.int32, (1, L), 1)
    row = jnp.sum(sums[...], 0, keepdims=True)

    def entry(index):
        value = jnp.sum(jnp.where(lane == index, row, 0.0), 1, keepdims=True)
        return jnp.broadcast_to(value, (1, L))

    b1, b2, b3, g11, g12, g22, g13, g23, g33 = (entry(i) for i in range(9))
    l21 = g12 / g11
    l31 = g13 / g11
    d2 = g22 - l21 * g12
    cross = g23 - l21 * g13
    l32 = cross / d2
    d3 = g33 - l31 * g13 - l32 * cross
    c2 = b2 - l21 * b1
    y1 = b1 / g11
    y2 = c2 / d2
    y3 = (b3 - l31 * b1 - l32 * c2) / d3
    k3 = y3
    k2 = y2 - l32 * k3
    k1 = y1 - l21 * k2 - l31 * k3
    parts = 4
    size = W // parts
    copies = []
    for part in range(parts):
        span = slice(part * size, (part + 1) * size)
        for j in range(R):
            q = [
                (search if depth <= j < R - depth else new_search)[depth, j, span]
                for depth in range(3)
            ]
            v = [
                (field if inside(depth, j) else new_field)[depth, j, span]
                for depth in range(3)
            ]
            to = pl.ds(part * size * R + j, size, stride=R)
            held[to, :] = k1 * q[0] + k2 * q[1] + k3 * q[2]
            left[to, :] = ring[j, span] - k1 * v[0] - k2 * v[1] - k3 * v[2]
        block = pl.ds(part * size * R, size * R)
        for i, (source, target) in enumerate(((held, pressure), (left, residual))):
            copy = pltpu.make_async_copy(
                source.at[block, :], target.at[block, :], sems.at[part, i]
            )
            copy.start()
            copies.append(copy)
    for copy in copies:
        copy.wait()


VMEM = pl.BlockSpec(memory_space=pltpu.VMEM)
SMEM = pl.BlockSpec(memory_space=pltpu.SMEM)
HBM = pl.BlockSpec(memory_space=pltpu.HBM)


def call(kernel, ins, outs, scratch=(), limit=32, flops=0, where=VMEM):
    return pl.pallas_call(
        kernel,
        out_shape=tuple(jax.ShapeDtypeStruct(s, jnp.float32) for s in outs),
        in_specs=list(ins),
        out_specs=tuple(where for _ in outs),
        scratch_shapes=[
            pltpu.VMEM(s, jnp.float32) if isinstance(s, tuple) else s for s in scratch
        ],
        compiler_params=pltpu.CompilerParams(vmem_limit_bytes=limit * MIB),
        cost_estimate=pl.CostEstimate(
            flops=flops, bytes_accessed=8 * MIB, transcendentals=0
        ),
    )


def body(count, tracer, offsets, frac_lon, frac_lat, frac_lev, metric, vertical_coef, inverses):
    in_chip = [(i, i ^ 1) for i in range(count)]
    across = [(i, i - 1 + 2 * (i % 2)) for i in range(1, count - 1)]
    flat = tracer.reshape(W * R, L)
    pair_out, cross_out = call(edges_kernel, (VMEM,), ((2 * W, L), (2 * W, L)))(flat)
    cross_in = lax.ppermute(cross_out, LAT, across)
    pair_in = lax.ppermute(pair_out, LAT, in_chip)
    fractions = jnp.broadcast_to(
        jnp.concatenate([frac_lat, frac_lev])[:, None], (2 * R, L)
    )
    (turned,) = call(mix_kernel, (VMEM,) * 4, ((NL, 2, R, 8, 128),))(
        fractions, flat, pair_in, cross_in
    )
    lines = lax.all_to_all(turned, LON, 0, 0, tiled=True)
    (moved,) = call(
        shift_kernel,
        (SMEM, SMEM, VMEM),
        ((NL, 2 * R + 1, 8, 128),),
        scratch=((R, 2 * B, 8, 128),),
    )(offsets, frac_lon, lines.reshape(B, R, 8, 128))
    back = lax.all_to_all(moved, LON, 0, 0, tiled=True)
    advected, ring, pair_out, cross_out = call(
        turn_kernel,
        (SMEM, VMEM, VMEM),
        ((W * R, L), (R, E, L), (T + H * L, L), (T + H * L, L)),
    )(metric, inverses, back)
    cross = lax.ppermute(cross_out, LAT, across)
    pair = lax.ppermute(pair_out, LAT, in_chip)
    vertical = vertical_coef.reshape(1, L)
    search, images, totals = call(
        inner_kernel,
        (SMEM, VMEM, VMEM, VMEM),
        ((3, R, E, L), (3, R, E, L), (9, 8, L)),
        flops=2 * 10**9,
    )(metric, vertical, inverses, ring)
    new_search, new_images, sums = call(
        outer_kernel,
        (SMEM,) + (VMEM,) * 8,
        ((3, R, E, L), (3, R, E, L), (count * NL, L)),
        scratch=((2, 3, 2 * H, E, L),),
    )(metric, vertical, inverses, ring, pair, cross, search, images, totals)
    gathered = lax.all_to_all(sums, LON_LAT, 0, 0, tiled=True)
    pressure, residual = call(
        finish_kernel,
        (VMEM,) * 6,
        ((W * R, L), (W * R, L)),
        scratch=((W * R, L), (W * R, L), pltpu.SemaphoreType.DMA((4, 2))),
        where=HBM,
    )(gathered, ring, search, images, new_search, new_images)
    return tuple(x.reshape(W, R, L) for x in (advected, pressure, residual))


def solution(mesh):
    count = mesh.shape["lat"]
    split = Mesh(mesh.devices.reshape(4, 4, count // 2, 2), LON_LAT)
    placed = (P(LON, LAT, None), P(LAT), P(LAT), P(LAT), P(LAT), P(LAT), P(), P(LAT, None, None))
    return jax.shard_map(
        functools.partial(body, count),
        mesh=split,
        in_specs=placed,
        out_specs=(P(LON, LAT, None),) * 3,
        check_vma=False,
    )
```

time: 126 us -> 102 us (0.81)
  Pallas kernels: 28.4 us -> 12.3 us
  blocking collectives: 65.2 us -> 58.3 us
  waiting for transfers between devices: 7.04 us -> 10.2 us
  local copies, waits for them, and re-layouts: 4.26 us -> 1.32 us
  starting transfers between devices: 19.6 us -> 18.1 us
    pallas_call x1, Pallas kernels: 17.5 us -> 1.96 us  [body(): call(shift_kernel, (SMEM, SMEM, VMEM), ((NL, 2 * R + 1, 8, 128),), scratc...]
    all_to_all x1, blocking collectives: 22.2 us -> 16.9 us  [body(): lines = lax.all_to_all(turned, LON, 0, 0, tiled=True)]
    all_to_all x1, blocking collectives: 21.3 us -> 17.2 us  [body(): back = lax.all_to_all(moved, LON, 0, 0, tiled=True)]
    ppermute x6 -> x4, waiting for transfers between devices: 7.04 us -> 10.2 us  [the longest x1 5.16 us: body(): cross = lax.ppermute(cross_out, LAT, across)]
    unnamed x20 -> x12, local copies, waits for them, and re-layouts: 4.26 us -> 1.25 us
    all_to_all x1, blocking collectives: 21.8 us -> 24.1 us  [body(): gathered = lax.all_to_all(sums, LON_LAT, 0, 0, tiled=True)]
    ppermute x6 -> x4, starting transfers between devices: 19.6 us -> 18.1 us  [the longest x1 12.9 us: body(): cross = lax.ppermute(cross_out, LAT, across)]
    pallas_call x5 -> x6, Pallas kernels: 10.9 us -> 10.3 us  [the longest x1 3.31 us: body(): call(outer_kernel, (SMEM,) + (VMEM,) * 8, ((3, R, E, L), (3, R, E, L), (c...]
  transfers between devices with their start and end apart: 6 -> 4, of which waited for: 3 -> 2; matrix products, arithmetic and copies ran while one was open for 0% -> 1% of each run, Pallas kernels for 0% -> 2%
where the time goes in v2:
time: 102 us
  blocking collectives  58.3 us (57%)
  starting transfers between devices  18.1 us (18%)
  Pallas kernels  12.3 us (12%)
  waiting for transfers between devices  10.2 us (10%)
  local copies, waits for them, and re-layouts  1.32 us (1%)
    all_to_all x1, blocking collectives, body(): gathered = lax.all_to_all(sums, LON_LAT, 0, 0, tiled=True)  24.1 us
    all_to_all x1, blocking collectives, body(): back = lax.all_to_all(moved, LON, 0, 0, tiled=True)  17.2 us
    all_to_all x1, blocking collectives, body(): lines = lax.all_to_all(turned, LON, 0, 0, tiled=True)  16.9 us
    ppermute x1, starting transfers between devices, body(): cross = lax.ppermute(cross_out, LAT, across)  12.9 us
    ppermute x1, waiting for transfers between devices, body(): cross = lax.ppermute(cross_out, LAT, across)  5.16 us
    ppermute x1, waiting for transfers between devices, body(): cross_in = lax.ppermute(cross_out, LAT, across)  5.01 us
    ppermute x1, starting transfers between devices, body(): pair_in = lax.ppermute(pair_out, LAT, in_chip)  3.33 us
    pallas_call x1, Pallas kernels, body(): call(outer_kernel, (SMEM,) + (VMEM,) * 8, ((3, R, E, L), (3, R, E, L), (c...  3.31 us
  transfers between devices with their start and end apart: 4, of which 2 were waited for; matrix products, arithmetic and copies ran while one was open for 1% of the time, Pallas kernels for 2%

profile of v2, /device:TPU:1, one launch (start us, length us, event | category | flops | bytes accessed | tf_op | source)
XLA Modules:
  0.0 101.7 jit_solution(5650007242435294074)
XLA Ops:
  0.7 1.2 %copy-done = f32[256,8,128]{2,1,0:T(8,128)S(1)} copy-done((f32[256,8,128]{2,1,0:T(8,128)S(1)}, f32[256,8,128]{2,1,0:T(8,128)}, u32[]{:S(2)}) %copy-start) | copy-done | bytes 1048600
  1.9 0.1 shard_map.103
  2.0 3.3 %collective-permute-start = (f32[512,128]{1,0:T(8,128)S(1)}, f32[512,128]{1,0:T(8,128)S(1)}, u32[]{:S(2)}, u32[]{:S(2)}) collective-permute-start(f32[512,128]{1,0:T(8,128)S(1)} %get-tuple-element.17), channel_id=1, source_target_pairs={{0,1},{1,0},{2,3},{3,2},{4,5},{5,4},{6,7},{7,6},{8,9},{9,8},{10,11... | collective-permute-start | bytes 786440 | tf_op jit(solution)/shard_map/ppermute | solution.py:395
  5.3 1.9 %collective-permute-start.1 = (f32[512,128]{1,0:T(8,128)S(1)}, f32[512,128]{1,0:T(8,128)S(1)}, u32[]{:S(2)}, u32[]{:S(2)}) collective-permute-start(f32[512,128]{1,0:T(8,128)S(1)} %get-tuple-element.18), channel_id=1, source_target_pairs={{1,2},{2,1},{3,4},{4,3},{5,6},{6,5},{7,8},{8,7},{9,10},{10,9},{11,... | collective-permute-start | bytes 786440 | tf_op jit(solution)/shard_map/ppermute | solution.py:394
  7.2 0.7 pad_maximum_fusion
  8.0 0.0 collective-permute-done.pair
  8.0 5.0 %collective-permute-done.1.cross = f32[512,128]{1,0:T(8,128)S(1)} collective-permute-done((f32[512,128]{1,0:T(8,128)S(1)}, f32[512,128]{1,0:T(8,128)S(1)}, u32[]{:S(2)}, u32[]{:S(2)}) %collective-permute-start.1) | collective-permute-done | bytes 262176 | tf_op jit(solution)/shard_map/ppermute | solution.py:394
  13.0 0.1 broadcast_in_dim.2.fractions
  13.0 0.8 shard_map.104
  13.9 0.0 copy-start.1
  13.9 0.0 copy-start.2
  13.9 16.9 %all_to_all.21 = f32[16,2,8,8,128]{4,3,2,1,0:T(8,128)S(1)} all-to-all(f32[16,2,8,8,128]{4,3,2,1,0:T(8,128)S(1)} %shard_map.104), channel_id=1, replica_groups=mesh['lon_0'=4,'lon_1'=4,'lat_0'=8,'lat_1'=2] {'lon_0','lon_1'}, dimensions={0} | all-to-all | bytes 2097152 | tf_op jit(solution)/shard_map/all_to_all | solution.py:402
  30.8 0.0 copy-done.4
  30.8 2.0 %shard_map.105 = f32[16,17,8,128]{3,2,1,0:T(8,128)S(1)} custom-call(s32[8]{0:T(128)S(1)} %copy-done.3, f32[8]{0:T(128)S(1)} %copy-done.4, f32[32,8,8,128]{3,2,1,0:T(8,128)S(1)} %bitcast.12), custom_call_target="tpu_custom_call" | custom-call | bytes 8388608 | tf_op jit(solution)/shard_map/pallas_call | solution.py:403
  32.8 17.2 %all_to_all.22.cells = f32[16,17,8,128]{3,2,1,0:T(8,128)S(1)} all-to-all(f32[16,17,8,128]{3,2,1,0:T(8,128)S(1)} %shard_map.105), channel_id=1, replica_groups=mesh['lon_0'=4,'lon_1'=4,'lat_0'=8,'lat_1'=2] {'lon_0','lon_1'}, dimensions={0} | all-to-all | bytes 2228224 | tf_op jit(solution)/shard_map/all_to_all | solution.py:409
  50.0 1.9 %shard_map.106 = (f32[2048,128]{1,0:T(8,128)}, f32[8,264,128]{2,1,0:T(8,128)S(1)}, f32[1176,128]{1,0:T(8,128)S(1)}, f32[1176,128]{1,0:T(8,128)S(1)}) custom-call(f32[8]{0:T(128)S(1)} %copy-done.2, f32[8,128,128]{2,1,0:T(8,128)S(1)} %copy-done.1, f32[16,17,8,128]{3,2,1,0:T(8,128)S(1)} %all_to_all.22.cells), custom_call_target="tpu_custom_call" | custom-call | bytes 8388608 | tf_op jit(solution)/shard_map/pallas_call | solution.py:410
  52.0 0.0 collective-permute-start.2
  52.0 12.9 %collective-permute-start.3 = (f32[1176,128]{1,0:T(8,128)S(1)}, f32[1176,128]{1,0:T(8,128)S(1)}, u32[]{:S(2)}, u32[]{:S(2)}) collective-permute-start(f32[1176,128]{1,0:T(8,128)S(1)} %get-tuple-element.22), channel_id=1, source_target_pairs={{1,2},{2,1},{3,4},{4,3},{5,6},{6,5},{7,8},{8,7},{9,10},{10,9},{11,... | collective-permute-start | bytes 1806344 | tf_op jit(solution)/shard_map/ppermute | solution.py:415
  64.9 2.5 %shard_map.107 = (f32[3,8,264,128]{3,2,1,0:T(8,128)S(1)}, f32[3,8,264,128]{3,2,1,0:T(8,128)S(1)}, f32[9,8,128]{2,1,0:T(8,128)S(1)}) custom-call(f32[8]{0:T(128)S(1)} %copy-done.2, f32[1,128]{1,0:T(1,128)S(1)} %bitcast.15, f32[8,128,128]{2,1,0:T(8,128)S(1)} %copy-done.1, f32[8,264,128]{2,1,0:T(8,128)S(1)} %get-tuple-element.20.ring), custom_call_target="tpu_custom_call" | custom-call | flops 2000000000 | bytes 8388608 | tf_op jit(solution)/shard_map/pallas_call | solution.py:418
  67.4 0.0 collective-permute-done.2.pair
  67.4 5.2 %collective-permute-done.3.cross = f32[1176,128]{1,0:T(8,128)S(1)} collective-permute-done((f32[1176,128]{1,0:T(8,128)S(1)}, f32[1176,128]{1,0:T(8,128)S(1)}, u32[]{:S(2)}, u32[]{:S(2)}) %collective-permute-start.3) | collective-permute-done | bytes 602144 | tf_op jit(solution)/shard_map/ppermute | solution.py:415
  72.6 3.3 %shard_map.108 = (f32[3,8,264,128]{3,2,1,0:T(8,128)S(1)}, f32[3,8,264,128]{3,2,1,0:T(8,128)S(1)}, f32[256,128]{1,0:T(8,128)S(1)}) custom-call(f32[8]{0:T(128)S(1)} %copy-done.2, f32[1,128]{1,0:T(1,128)S(1)} %bitcast.16, f32[8,128,128]{2,1,0:T(8,128)S(1)} %copy-done.1, f32[8,264,128]{2,1,0:T(8,128)S(1)} %get-tuple-element.20.ring, ...), custom_call_target="tpu_custom_call" | custom-call | bytes 8388608 | tf_op jit(solution)/shard_map/pallas_call | solution.py:424
  75.9 24.1 %all_to_all.23 = f32[256,1,128]{2,1,0:T(1,128)S(1)} all-to-all(f32[256,1,128]{2,1,0:T(1,128)S(1)} %bitcast.14), channel_id=1, replica_groups=mesh['lon_0'=4,'lon_1'=4,'lat_0'=8,'lat_1'=2] {'lon_0','lon_1','lat_0','..., dimensions={0} | all-to-all | bytes 262144 | tf_op jit(solution)/shard_map/all_to_all | solution.py:430
  100.0 1.7 %shard_map.109 = (f32[2048,128]{1,0:T(8,128)}, f32[2048,128]{1,0:T(8,128)}) custom-call(f32[256,128]{1,0:T(8,128)S(1)} %bitcast.13, f32[8,264,128]{2,1,0:T(8,128)S(1)} %get-tuple-element.20.ring, f32[3,8,264,128]{3,2,1,0:T(8,128)S(1)} %get-tuple-element.23.search, f32[3,8,264,128]{3,2,1,0:T(8,128)S(1)} %get-tuple-element.24.field, ...), custom_call_target="tpu_custom_call" | custom-call | bytes 8388608 | tf_op jit(solution)/shard_map/pallas_call | solution.py:431
  (8 shorter events, 0.0 us)
Async XLA Ops:
  0.6 30.2 %copy-start.4 = (f32[8]{0:T(128)S(1)}, f32[8]{0:T(128)}, u32[]{:S(2)}) copy-start(f32[8]{0:T(128)} %frac_lon.1) | copy-start | bytes 100
  0.6 30.2 %copy-start.3 = (s32[8]{0:T(128)S(1)}, s32[8]{0:T(128)}, u32[]{:S(2)}) copy-start(s32[8]{0:T(128)} %offsets.1) | copy-start | bytes 100
  0.7 1.2 %copy-start = (f32[256,8,128]{2,1,0:T(8,128)S(1)}, f32[256,8,128]{2,1,0:T(8,128)}, u32[]{:S(2)}) copy-start(f32[256,8,128]{2,1,0:T(8,128)} %param.8) | copy-start | bytes 3145732
  2.0 6.0 %collective-permute-start = (f32[512,128]{1,0:T(8,128)S(1)}, f32[512,128]{1,0:T(8,128)S(1)}, u32[]{:S(2)}, u32[]{:S(2)}) collective-permute-start(f32[512,128]{1,0:T(8,128)S(1)} %get-tuple-element.17), channel_id=1, source_target_pairs={{0,1},{1,0},{2,3},{3,2},{4,5},{5,4},{6,7},{7,6},{8,9},{9,8},{10,11... | collective-permute-start | bytes 786440 | tf_op jit(solution)/shard_map/ppermute | solution.py:395
  5.3 7.7 %collective-permute-start.1 = (f32[512,128]{1,0:T(8,128)S(1)}, f32[512,128]{1,0:T(8,128)S(1)}, u32[]{:S(2)}, u32[]{:S(2)}) collective-permute-start(f32[512,128]{1,0:T(8,128)S(1)} %get-tuple-element.18), channel_id=1, source_target_pairs={{1,2},{2,1},{3,4},{4,3},{5,6},{6,5},{7,8},{8,7},{9,10},{10,9},{11,... | collective-permute-start | bytes 786440 | tf_op jit(solution)/shard_map/ppermute | solution.py:394
  13.9 36.2 %copy-start.1 = (f32[8,128,128]{2,1,0:T(8,128)S(1)}, f32[8,128,128]{2,1,0:T(8,128)}, u32[]{:S(2)}) copy-start(f32[8,128,128]{2,1,0:T(8,128)} %inverses.5) | copy-start | bytes 1572868
  13.9 36.2 %copy-start.2 = (f32[8]{0:T(128)S(1)}, f32[8]{0:T(128)}, u32[]{:S(2)}) copy-start(f32[8]{0:T(128)} %metric.5) | copy-start | bytes 100
  30.8 34.1 %copy-start.5 = (f32[128]{0:T(128)S(1)}, f32[128]{0:T(128)}, u32[]{:S(2)}) copy-start(f32[128]{0:T(128)} %param.14) | copy-start | bytes 1540
  52.0 15.4 %collective-permute-start.2 = (f32[1176,128]{1,0:T(8,128)S(1)}, f32[1176,128]{1,0:T(8,128)S(1)}, u32[]{:S(2)}, u32[]{:S(2)}) collective-permute-start(f32[1176,128]{1,0:T(8,128)S(1)} %get-tuple-element.21), channel_id=1, source_target_pairs={{0,1},{1,0},{2,3},{3,2},{4,5},{5,4},{6,7},{7,6},{8,9},{9,8},{10,11... | collective-permute-start | bytes 1806344 | tf_op jit(solution)/shard_map/ppermute | solution.py:416
  52.0 20.6 %collective-permute-start.3 = (f32[1176,128]{1,0:T(8,128)S(1)}, f32[1176,128]{1,0:T(8,128)S(1)}, u32[]{:S(2)}, u32[]{:S(2)}) collective-permute-start(f32[1176,128]{1,0:T(8,128)S(1)} %get-tuple-element.22), channel_id=1, source_target_pairs={{1,2},{2,1},{3,4},{4,3},{5,6},{6,5},{7,8},{8,7},{9,10},{10,9},{11,... | collective-permute-start | bytes 1806344 | tf_op jit(solution)/shard_map/ppermute | solution.py:415

commit v3 on v2

--- a/solution.py
+++ b/solution.py
@@ -51,15 +51,20 @@
     return lax.axis_index("lat_1") == 0
 
 
+def at_end():
+    place = 2 * lax.axis_index("lat_0") + lax.axis_index("lat_1")
+    return (place == 0) | (place == 2 * lax.axis_size("lat_0") - 1)
+
+
 def edges_kernel(tracer, pair, cross):
-    even = is_even()
+    even, end = is_even(), at_end()
     last = tracer[row_of(R - 1), :]
     first = tracer[row_of(0), :]
     second = tracer[row_of(1), :]
     pair[0:W] = jnp.where(even, last, first)
     pair[W : 2 * W] = second
-    cross[0:W] = jnp.where(even, first, last)
-    cross[W : 2 * W] = second
+    cross[0:W] = jnp.where(end, 0.0, jnp.where(even, first, last))
+    cross[W : 2 * W] = jnp.where(end, 0.0, second)
 
 
 def mix_kernel(fractions, tracer, pair, cross, out):
@@ -98,7 +103,7 @@
         out[:, 1, j] = turned[:, :, 128:]
 
 
-def shift_kernel(offsets, frac_lon, cells, out, twice):
+def shift_kernel(offsets, frac_lon, cells, arrived, out, twice):
     delta = lax.broadcasted_iota(jnp.int32, (128, 128), 0) - lax.broadcasted_iota(
         jnp.int32, (128, 128), 1
     )
@@ -148,25 +153,30 @@
     out[:, 2 * R] = rims
 
 
-def turn_kernel(metric, inverses, cells, advected, ring, pair, cross):
-    even = is_even()
+def edge(j):
+    return j < H or j >= R - H
+
+
+def turned_row(cells, rim, metric, j, ref, at):
+    sub = lax.broadcasted_iota(jnp.int32, (8, L), 0)
+    for h in range(2):
+        ref[at, h * 128 : (h + 1) * 128, :] = cells[:, h * R + j].reshape(L, 128).T
+    before = (8 * j - 8) % 128
+    tail = jnp.where(sub < 4, rim[8 * j : 8 * j + 8], rim[before : before + 8])
+    ref[at, W:E, :] = jnp.where(sub == 3, metric[j], tail)
+
+
+def turn_kernel(metric, inverses, cells, ring, pair, cross):
+    even, end = is_even(), at_end()
     rim = cells[:, 2 * R].reshape(L, 128).T
-    sub = lax.broadcasted_iota(jnp.int32, (8, L), 0)
     for j in range(R):
-        for h in range(2):
-            tile = cells[:, h * R + j].reshape(L, 128).T
-            ring[j, h * 128 : (h + 1) * 128, :] = tile
-            advected[pl.ds(h * 128 * R + j, 128, stride=R), :] = tile
-        before = (8 * j - 8) % 128
-        tail = jnp.where(sub < 4, rim[8 * j : 8 * j + 8], rim[before : before + 8])
-        ring[j, W:E, :] = jnp.where(sub == 3, metric[j], tail)
+        if edge(j):
+            turned_row(cells, rim, metric, j, ring, j)
     for i in range(H):
-        for base, size, high, low in (
-            (i * E, E, ring[R - H + i], ring[i]),
-            (T + i * L, L, inverses[R - H + i], inverses[i]),
-        ):
-            pair[base : base + size] = jnp.where(even, high, low)
-            cross[base : base + size] = jnp.where(even, low, high)
+        high, low = ring[R - H + i], ring[i]
+        pair[i * E : (i + 1) * E] = jnp.where(even, high, low)
+        cross[i * E : (i + 1) * E] = jnp.where(end, 0.0, jnp.where(even, low, high))
+        pair[T + i * L : T + (i + 1) * L] = jnp.where(even, inverses[R - H + i], inverses[i])
 
 
 def vertical_rows(vertical):
@@ -210,7 +220,17 @@
     return depth < j < R - 1 - depth
 
 
-def inner_kernel(metric, vertical, inverses, ring, search, field, totals):
+def inner_kernel(
+    metric, vertical, inverses, cells, edges, search, field, totals, middle, advected, ring
+):
+    rim = cells[:, 2 * R].reshape(L, 128).T
+    for j in range(R):
+        if edge(j):
+            ring[j] = edges[j]
+        else:
+            turned_row(cells, rim, metric, j, ring, j)
+            middle[j - H] = ring[j]
+        advected[row_of(j), :] = ring[j, :W]
     rows = vertical_rows(vertical)
     sums = [jnp.zeros((8, L), jnp.float32) for _ in range(9)]
     for depth in range(3):
@@ -235,7 +255,7 @@
 
 
 def outer_kernel(
-    metric, vertical, inverses, ring, pair, cross, search, field, totals,
+    metric, vertical, inverses, cross_inv, edges, middle, pair, cross, search, field, totals,
     new_search, new_field, sums_out, wide,
 ):
     even = is_even()
@@ -251,7 +271,10 @@
     def inverse(j):
         if 0 <= j < R:
             return inverses[j]
-        return beyond(j, T + (j + H if j < 0 else j - R) * L, L)
+        i = j + H if j < 0 else j - R
+        near = pair[T + i * L : T + (i + 1) * L]
+        far = cross_inv[i * L : (i + 1) * L]
+        return jnp.where(even, far, near) if j < 0 else jnp.where(even, near, far)
 
     def metric_of(j):
         if 0 <= j < R:
@@ -260,7 +283,7 @@
 
     def start(j):
         if 0 <= j < R:
-            return ring[j]
+            return edges[j] if edge(j) else middle[j - H]
         return beyond(j, (j + H if j < 0 else j - R) * E, E)
 
     def image(depth, j):
@@ -314,7 +337,7 @@
 
 
 def finish_kernel(
-    sums, ring, search, field, new_search, new_field, pressure, residual, held, left, sems
+    sums, edges, middle, search, field, new_search, new_field, pressure, residual, held, left, sems
 ):
     lane = lax.broadcasted_iota(jnp.int32, (1, L), 1)
     row = jnp.sum(sums[...], 0, keepdims=True)
@@ -353,7 +376,8 @@
             ]
             to = pl.ds(part * size * R + j, size, stride=R)
             held[to, :] = k1 * q[0] + k2 * q[1] + k3 * q[2]
-            left[to, :] = ring[j, span] - k1 * v[0] - k2 * v[1] - k3 * v[2]
+            first = edges[j, span] if edge(j) else middle[j - H, span]
+            left[to, :] = first - k1 * v[0] - k2 * v[1] - k3 * v[2]
         block = pl.ds(part * size * R, size * R)
         for i, (source, target) in enumerate(((held, pressure), (left, residual))):
             copy = pltpu.make_async_copy(
@@ -368,6 +392,7 @@
 VMEM = pl.BlockSpec(memory_space=pltpu.VMEM)
 SMEM = pl.BlockSpec(memory_space=pltpu.SMEM)
 HBM = pl.BlockSpec(memory_space=pltpu.HBM)
+ANY = pl.BlockSpec(memory_space=pl.ANY)
 
 
 def call(kernel, ins, outs, scratch=(), limit=32, flops=0, where=VMEM):
@@ -388,7 +413,7 @@
 
 def body(count, tracer, offsets, frac_lon, frac_lat, frac_lev, metric, vertical_coef, inverses):
     in_chip = [(i, i ^ 1) for i in range(count)]
-    across = [(i, i - 1 + 2 * (i % 2)) for i in range(1, count - 1)]
+    across = [(i, (i - 1 + 2 * (i % 2)) % count) for i in range(count)]
     flat = tracer.reshape(W * R, L)
     pair_out, cross_out = call(edges_kernel, (VMEM,), ((2 * W, L), (2 * W, L)))(flat)
     cross_in = lax.ppermute(cross_out, LAT, across)
@@ -399,42 +424,45 @@
     (turned,) = call(mix_kernel, (VMEM,) * 4, ((NL, 2, R, 8, 128),))(
         fractions, flat, pair_in, cross_in
     )
+    first = jnp.where(is_even(), 0, R - H)
+    inv_out = lax.dynamic_slice_in_dim(inverses, first, H, 0).reshape(H * L, L)
+    inv_out = jnp.where(at_end(), 0.0, inv_out)
+    inv_in = lax.ppermute(inv_out, LAT, across)
     lines = lax.all_to_all(turned, LON, 0, 0, tiled=True)
     (moved,) = call(
         shift_kernel,
-        (SMEM, SMEM, VMEM),
+        (SMEM, SMEM, VMEM, ANY),
         ((NL, 2 * R + 1, 8, 128),),
         scratch=((R, 2 * B, 8, 128),),
-    )(offsets, frac_lon, lines.reshape(B, R, 8, 128))
+    )(offsets, frac_lon, lines.reshape(B, R, 8, 128), inv_in)
     back = lax.all_to_all(moved, LON, 0, 0, tiled=True)
-    advected, ring, pair_out, cross_out = call(
-        turn_kernel,
-        (SMEM, VMEM, VMEM),
-        ((W * R, L), (R, E, L), (T + H * L, L), (T + H * L, L)),
+    edges, pair_out, cross_out = call(
+        turn_kernel, (SMEM, VMEM, VMEM), ((R, E, L), (T + H * L, L), (T, L))
     )(metric, inverses, back)
     cross = lax.ppermute(cross_out, LAT, across)
     pair = lax.ppermute(pair_out, LAT, in_chip)
     vertical = vertical_coef.reshape(1, L)
-    search, images, totals = call(
+    search, images, totals, middle, advected = call(
         inner_kernel,
-        (SMEM, VMEM, VMEM, VMEM),
-        ((3, R, E, L), (3, R, E, L), (9, 8, L)),
+        (SMEM, VMEM, VMEM, VMEM, VMEM),
+        ((3, R, E, L), (3, R, E, L), (9, 8, L), (R - 2 * H, E, L), (W * R, L)),
+        scratch=((R, E, L),),
         flops=2 * 10**9,
-    )(metric, vertical, inverses, ring)
+    )(metric, vertical, inverses, back, edges)
     new_search, new_images, sums = call(
         outer_kernel,
-        (SMEM,) + (VMEM,) * 8,
+        (SMEM,) + (VMEM,) * 10,
         ((3, R, E, L), (3, R, E, L), (count * NL, L)),
         scratch=((2, 3, 2 * H, E, L),),
-    )(metric, vertical, inverses, ring, pair, cross, search, images, totals)
+    )(metric, vertical, inverses, inv_in, edges, middle, pair, cross, search, images, totals)
     gathered = lax.all_to_all(sums, LON_LAT, 0, 0, tiled=True)
     pressure, residual = call(
         finish_kernel,
-        (VMEM,) * 6,
+        (VMEM,) * 7,
         ((W * R, L), (W * R, L)),
         scratch=((W * R, L), (W * R, L), pltpu.SemaphoreType.DMA((4, 2))),
         where=HBM,
-    )(gathered, ring, search, images, new_search, new_images)
+    )(gathered, edges, middle, search, images, new_search, new_images)
     return tuple(x.reshape(W, R, L) for x in (advected, pressure, residual))
 
 

time: 102 us -> 98 us (0.961)
  blocking collectives: 58.3 us -> 41.6 us
  waiting for transfers between devices: 10.2 us -> 18 us
  starting transfers between devices: 18.1 us -> 22.7 us
    all_to_all x1 -> x0, blocking collectives: 16.9 us -> none  [body(): lines = lax.all_to_all(turned, LON, 0, 0, tiled=True)]
    ppermute x1, starting transfers between devices: 12.9 us -> 5.97 us  [body(): cross = lax.ppermute(cross_out, LAT, across)]
    all_to_all x0 -> x1, waiting for transfers between devices: none -> 6.61 us  [body(): lines = lax.all_to_all(turned, LON, 0, 0, tiled=True)]
    ppermute x1, starting transfers between devices: 0.01 us -> 6.6 us  [body(): pair = lax.ppermute(pair_out, LAT, in_chip)]
    all_to_all x0 -> x1, starting transfers between devices: none -> 4.86 us  [body(): lines = lax.all_to_all(turned, LON, 0, 0, tiled=True)]
    ppermute x0 -> x1, waiting for transfers between devices: none -> 3.35 us  [body(): inv_in = lax.ppermute(inv_out, LAT, across)]
    ppermute x1, waiting for transfers between devices: 5.16 us -> 2.68 us  [body(): cross = lax.ppermute(cross_out, LAT, across)]
    ppermute x0 -> x1, starting transfers between devices: none -> 1.99 us  [body(): inv_in = lax.ppermute(inv_out, LAT, across)]
  transfers between devices with their start and end apart: 4 -> 6, of which waited for: 2 -> 5; matrix products, arithmetic and copies ran while one was open for 1% -> 1% of each run, Pallas kernels for 2% -> 3%
where the time goes in v3:
time: 98 us; the launch traced here: 97.7 us
  blocking collectives  41.6 us (42%)
  starting transfers between devices  22.7 us (23%)
  waiting for transfers between devices  18 us (18%)
  Pallas kernels  12.6 us (13%)
  local copies, waits for them, and re-layouts  1.32 us (1%)
    all_to_all x1, blocking collectives, body(): gathered = lax.all_to_all(sums, LON_LAT, 0, 0, tiled=True)  25.3 us
    all_to_all x1, blocking collectives, body(): back = lax.all_to_all(moved, LON, 0, 0, tiled=True)  16.3 us
    all_to_all x1, waiting for transfers between devices, body(): lines = lax.all_to_all(turned, LON, 0, 0, tiled=True)  6.61 us
    ppermute x1, starting transfers between devices, body(): pair = lax.ppermute(pair_out, LAT, in_chip)  6.6 us
    ppermute x1, starting transfers between devices, body(): cross = lax.ppermute(cross_out, LAT, across)  5.97 us
    ppermute x1, waiting for transfers between devices, body(): cross_in = lax.ppermute(cross_out, LAT, across)  4.93 us
    all_to_all x1, starting transfers between devices, body(): lines = lax.all_to_all(turned, LON, 0, 0, tiled=True)  4.86 us
    ppermute x1, waiting for transfers between devices, body(): inv_in = lax.ppermute(inv_out, LAT, across)  3.35 us
  transfers between devices with their start and end apart: 6, of which 5 were waited for; matrix products, arithmetic and copies ran while one was open for 1% of the time, Pallas kernels for 3%

profile of v3, /device:TPU:1, one launch (start us, length us, event | category | flops | bytes accessed | tf_op | source)
XLA Modules:
  0.0 97.7 jit_solution(15096686407076410109)
XLA Ops:
  0.7 1.2 %copy-done = f32[256,8,128]{2,1,0:T(8,128)S(1)} copy-done((f32[256,8,128]{2,1,0:T(8,128)S(1)}, f32[256,8,128]{2,1,0:T(8,128)}, u32[]{:S(2)}) %copy-start) | copy-done | bytes 1048600
  1.9 0.1 shard_map.103
  2.0 3.3 %collective-permute-start = (f32[512,128]{1,0:T(8,128)S(1)}, f32[512,128]{1,0:T(8,128)S(1)}, u32[]{:S(2)}, u32[]{:S(2)}) collective-permute-start(f32[512,128]{1,0:T(8,128)S(1)} %get-tuple-element.18), channel_id=1, source_target_pairs={{0,1},{1,0},{2,3},{3,2},{4,5},{5,4},{6,7},{7,6},{8,9},{9,8},{10,11... | collective-permute-start | bytes 786440 | tf_op jit(solution)/shard_map/ppermute | solution.py:420
  5.3 0.0 collective-permute-start.1
  5.3 0.7 pad_maximum_fusion
  6.1 0.4 collective-permute-done.pair
  6.5 4.9 %collective-permute-done.1.cross = f32[512,128]{1,0:T(8,128)S(1)} collective-permute-done((f32[512,128]{1,0:T(8,128)S(1)}, f32[512,128]{1,0:T(8,128)S(1)}, u32[]{:S(2)}, u32[]{:S(2)}) %collective-permute-start.1) | collective-permute-done | bytes 262176 | tf_op jit(solution)/shard_map/ppermute | solution.py:419
  11.4 0.1 broadcast_in_dim.10.fractions
  11.5 1.8 %shard_map.104 = f32[16,2,8,8,128]{4,3,2,1,0:T(8,128)} custom-call(f32[16,128]{1,0:T(8,128)S(1)} %broadcast_in_dim.10.fractions, f32[2048,128]{1,0:T(8,128)S(1)} %bitcast.12, f32[512,128]{1,0:T(8,128)S(1)} %collective-permute-done.pair, f32[512,128]{1,0:T(8,128)S(1)} %collective-permute-done.1.cross), custom_call_target="tpu_custom_call" | custom-call | bytes 8388608 | tf_op jit(solution)/shard_map/pallas_call | solution.py:424
  13.3 4.9 %all-to-all-start = ((f32[16,2,8,8,128]{4,3,2,1,0:T(8,128)}), f32[16,2,8,8,128]{4,3,2,1,0:T(8,128)S(1)}, u32[]{:S(2)}, u32[]{:S(2)}) async-start(f32[16,2,8,8,128]{4,3,2,1,0:T(8,128)} %shard_map.104), calls=%async_computation | async-start | bytes 2097152 | tf_op jit(solution)/shard_map/all_to_all | solution.py:431
  18.2 0.0 copy-start.3
  18.2 2.0 %collective-permute-start.2 = (f32[384,128]{1,0:T(8,128)S(1)}, f32[384,128]{1,0:T(8,128)S(1)}, u32[]{:S(2)}, u32[]{:S(2)}) collective-permute-start(f32[384,128]{1,0:T(8,128)S(1)} %bitcast.18), channel_id=1, source_target_pairs={{0,15},{1,2},{2,1},{3,4},{4,3},{5,6},{6,5},{7,8},{8,7},{9,10},{10,... | collective-permute-start | bytes 589832 | tf_op jit(solution)/shard_map/ppermute | solution.py:430
  20.2 3.4 %collective-permute-done.2.arrived.cross_inv = f32[384,128]{1,0:T(8,128)S(1)} collective-permute-done((f32[384,128]{1,0:T(8,128)S(1)}, f32[384,128]{1,0:T(8,128)S(1)}, u32[]{:S(2)}, u32[]{:S(2)}) %collective-permute-start.2) | collective-permute-done | bytes 196640 | tf_op jit(solution)/shard_map/ppermute | solution.py:430
  23.5 6.6 %all-to-all-done = f32[16,2,8,8,128]{4,3,2,1,0:T(8,128)S(1)} async-done(((f32[16,2,8,8,128]{4,3,2,1,0:T(8,128)}), f32[16,2,8,8,128]{4,3,2,1,0:T(8,128)S(1)}, u32[]{:S(2)}, u32[]{:S(2)}) %all-to-all-start) | async-done | bytes 1048608 | tf_op jit(solution)/shard_map/all_to_all | solution.py:431
  30.2 1.9 %shard_map.105 = f32[16,17,8,128]{3,2,1,0:T(8,128)S(1)} custom-call(s32[8]{0:T(128)S(1)} %copy-done.4, f32[8]{0:T(128)S(1)} %copy-done.5, f32[32,8,8,128]{3,2,1,0:T(8,128)S(1)} %bitcast.13, f32[384,128]{1,0:T(8,128)S(1)} %collective-permute-done.2.arrived.cross_inv), custom_call_target="tpu_custom_call" | custom-call | bytes 8388608 | tf_op jit(solution)/shard_map/pallas_call | solution.py:432
  32.1 16.3 %all_to_all.21.cells = f32[16,17,8,128]{3,2,1,0:T(8,128)S(1)} all-to-all(f32[16,17,8,128]{3,2,1,0:T(8,128)S(1)} %shard_map.105), channel_id=1, replica_groups=mesh['lon_0'=4,'lon_1'=4,'lat_0'=8,'lat_1'=2] {'lon_0','lon_1'}, dimensions={0} | all-to-all | bytes 2228224 | tf_op jit(solution)/shard_map/all_to_all | solution.py:438
  48.4 0.8 shard_map.106
  49.2 6.6 %collective-permute-start.3 = (f32[1176,128]{1,0:T(8,128)S(1)}, f32[1176,128]{1,0:T(8,128)S(1)}, u32[]{:S(2)}, u32[]{:S(2)}) collective-permute-start(f32[1176,128]{1,0:T(8,128)S(1)} %get-tuple-element.23), channel_id=1, source_target_pairs={{0,1},{1,0},{2,3},{3,2},{4,5},{5,4},{6,7},{7,6},{8,9},{9,8},{10,11... | collective-permute-start | bytes 1806344 | tf_op jit(solution)/shard_map/ppermute | solution.py:443
  55.8 6.0 %collective-permute-start.4 = (f32[792,128]{1,0:T(8,128)S(1)}, f32[792,128]{1,0:T(8,128)S(1)}, u32[]{:S(2)}, u32[]{:S(2)}) collective-permute-start(f32[792,128]{1,0:T(8,128)S(1)} %get-tuple-element.24), channel_id=1, source_target_pairs={{0,15},{1,2},{2,1},{3,4},{4,3},{5,6},{6,5},{7,8},{8,7},{9,10},{10,... | collective-permute-start | bytes 1216520 | tf_op jit(solution)/shard_map/ppermute | solution.py:442
  61.8 2.9 %shard_map.107 = (f32[3,8,264,128]{3,2,1,0:T(8,128)S(1)}, f32[3,8,264,128]{3,2,1,0:T(8,128)S(1)}, f32[9,8,128]{2,1,0:T(8,128)S(1)}, f32[2,264,128]{2,1,0:T(8,128)S(1)}, f32[2048,128]{1,0:T(8,128)}) custom-call(f32[8]{0:T(128)S(1)} %copy-done.2, f32[1,128]{1,0:T(1,128)S(1)} %bitcast.16, f32[8,128,128]{2,1,0:T(8,128)S(1)} %copy-done.1, ...), custom_call_target="tpu_custom_call" | custom-call | flops 2000000000 | bytes 8388608 | tf_op jit(solution)/shard_map/pallas_call | solution.py:445
  64.7 2.7 %collective-permute-done.4.cross = f32[792,128]{1,0:T(8,128)S(1)} collective-permute-done((f32[792,128]{1,0:T(8,128)S(1)}, f32[792,128]{1,0:T(8,128)S(1)}, u32[]{:S(2)}, u32[]{:S(2)}) %collective-permute-start.4) | collective-permute-done | bytes 405536 | tf_op jit(solution)/shard_map/ppermute | solution.py:442
  67.4 3.3 %shard_map.108 = (f32[3,8,264,128]{3,2,1,0:T(8,128)S(1)}, f32[3,8,264,128]{3,2,1,0:T(8,128)S(1)}, f32[256,128]{1,0:T(8,128)S(1)}) custom-call(f32[8]{0:T(128)S(1)} %copy-done.2, f32[1,128]{1,0:T(1,128)S(1)} %bitcast.17, f32[8,128,128]{2,1,0:T(8,128)S(1)} %copy-done.1, f32[384,128]{1,0:T(8,128)S(1)} %collective-permute-done.2.arrived.cross_inv, ...), custom_call_target="tpu_custom_call" | custom-call | bytes 8388608 | tf_op jit(solution)/shard_map/pallas_call | solution.py:452
  70.7 25.3 %all_to_all.22 = f32[256,1,128]{2,1,0:T(1,128)S(1)} all-to-all(f32[256,1,128]{2,1,0:T(1,128)S(1)} %bitcast.15), channel_id=1, replica_groups=mesh['lon_0'=4,'lon_1'=4,'lat_0'=8,'lat_1'=2] {'lon_0','lon_1','lat_0','..., dimensions={0} | all-to-all | bytes 262144 | tf_op jit(solution)/shard_map/all_to_all | solution.py:458
  96.0 1.7 %shard_map.109 = (f32[2048,128]{1,0:T(8,128)}, f32[2048,128]{1,0:T(8,128)}) custom-call(f32[256,128]{1,0:T(8,128)S(1)} %bitcast.14, f32[8,264,128]{2,1,0:T(8,128)S(1)} %get-tuple-element.20.edges, f32[2,264,128]{2,1,0:T(8,128)S(1)} %get-tuple-element.22.middle, f32[3,8,264,128]{3,2,1,0:T(8,128)S(1)} %get-tuple-element.25.search, ...), custom_call_target="tpu_custom_call" | custom-call | bytes 8388608 | tf_op jit(solution)/shard_map/pallas_call | solution.py:459
  (12 shorter events, 0.0 us)
Async XLA Ops:
  0.6 29.5 %copy-start.5 = (f32[8]{0:T(128)S(1)}, f32[8]{0:T(128)}, u32[]{:S(2)}) copy-start(f32[8]{0:T(128)} %frac_lon.1) | copy-start | bytes 100
  0.6 29.5 %copy-start.4 = (s32[8]{0:T(128)S(1)}, s32[8]{0:T(128)}, u32[]{:S(2)}) copy-start(s32[8]{0:T(128)} %offsets.1) | copy-start | bytes 100
  0.7 1.2 %copy-start = (f32[256,8,128]{2,1,0:T(8,128)S(1)}, f32[256,8,128]{2,1,0:T(8,128)}, u32[]{:S(2)}) copy-start(f32[256,8,128]{2,1,0:T(8,128)} %param.8) | copy-start | bytes 3145732
  1.9 16.3 %copy-start.1 = (f32[8,128,128]{2,1,0:T(8,128)S(1)}, f32[8,128,128]{2,1,0:T(8,128)}, u32[]{:S(2)}) copy-start(f32[8,128,128]{2,1,0:T(8,128)} %inverses.5) | copy-start | bytes 1572868
  2.0 4.5 %collective-permute-start = (f32[512,128]{1,0:T(8,128)S(1)}, f32[512,128]{1,0:T(8,128)S(1)}, u32[]{:S(2)}, u32[]{:S(2)}) collective-permute-start(f32[512,128]{1,0:T(8,128)S(1)} %get-tuple-element.18), channel_id=1, source_target_pairs={{0,1},{1,0},{2,3},{3,2},{4,5},{5,4},{6,7},{7,6},{8,9},{9,8},{10,11... | collective-permute-start | bytes 786440 | tf_op jit(solution)/shard_map/ppermute | solution.py:420
  5.3 6.1 %collective-permute-start.1 = (f32[512,128]{1,0:T(8,128)S(1)}, f32[512,128]{1,0:T(8,128)S(1)}, u32[]{:S(2)}, u32[]{:S(2)}) collective-permute-start(f32[512,128]{1,0:T(8,128)S(1)} %get-tuple-element.19), channel_id=1, source_target_pairs={{0,15},{1,2},{2,1},{3,4},{4,3},{5,6},{6,5},{7,8},{8,7},{9,10},{10,... | collective-permute-start | bytes 786440 | tf_op jit(solution)/shard_map/ppermute | solution.py:419
  13.3 35.1 %copy-start.2 = (f32[8]{0:T(128)S(1)}, f32[8]{0:T(128)}, u32[]{:S(2)}) copy-start(f32[8]{0:T(128)} %metric.5) | copy-start | bytes 100
  13.3 16.9 %all-to-all-start = ((f32[16,2,8,8,128]{4,3,2,1,0:T(8,128)}), f32[16,2,8,8,128]{4,3,2,1,0:T(8,128)S(1)}, u32[]{:S(2)}, u32[]{:S(2)}) async-start(f32[16,2,8,8,128]{4,3,2,1,0:T(8,128)} %shard_map.104), calls=%async_computation | async-start | bytes 2097152 | tf_op jit(solution)/shard_map/all_to_all | solution.py:431
  18.2 43.7 %copy-start.3 = (f32[128]{0:T(128)S(1)}, f32[128]{0:T(128)}, u32[]{:S(2)}) copy-start(f32[128]{0:T(128)} %param.14) | copy-start | bytes 1540
  18.2 5.3 %collective-permute-start.2 = (f32[384,128]{1,0:T(8,128)S(1)}, f32[384,128]{1,0:T(8,128)S(1)}, u32[]{:S(2)}, u32[]{:S(2)}) collective-permute-start(f32[384,128]{1,0:T(8,128)S(1)} %bitcast.18), channel_id=1, source_target_pairs={{0,15},{1,2},{2,1},{3,4},{4,3},{5,6},{6,5},{7,8},{8,7},{9,10},{10,... | collective-permute-start | bytes 589832 | tf_op jit(solution)/shard_map/ppermute | solution.py:430
  49.2 18.2 %collective-permute-start.3 = (f32[1176,128]{1,0:T(8,128)S(1)}, f32[1176,128]{1,0:T(8,128)S(1)}, u32[]{:S(2)}, u32[]{:S(2)}) collective-permute-start(f32[1176,128]{1,0:T(8,128)S(1)} %get-tuple-element.23), channel_id=1, source_target_pairs={{0,1},{1,0},{2,3},{3,2},{4,5},{5,4},{6,7},{7,6},{8,9},{9,8},{10,11... | collective-permute-start | bytes 1806344 | tf_op jit(solution)/shard_map/ppermute | solution.py:443
  55.8 11.6 %collective-permute-start.4 = (f32[792,128]{1,0:T(8,128)S(1)}, f32[792,128]{1,0:T(8,128)S(1)}, u32[]{:S(2)}, u32[]{:S(2)}) collective-permute-start(f32[792,128]{1,0:T(8,128)S(1)} %get-tuple-element.24), channel_id=1, source_target_pairs={{0,15},{1,2},{2,1},{3,4},{4,3},{5,6},{6,5},{7,8},{8,7},{9,10},{10,... | collective-permute-start | bytes 1216520 | tf_op jit(solution)/shard_map/ppermute | solution.py:442

commit v4 on v3

v4 whole, which is shorter than its diff:
```python
import functools

import jax
import jax.numpy as jnp
from jax import lax
from jax.experimental import pallas as pl
from jax.experimental.pallas import tpu as pltpu
from jax.sharding import Mesh
from jax.sharding import PartitionSpec as P

LON = ("lon_0", "lon_1")
LAT = ("lat_0", "lat_1")
LON_LAT = ("lon_0", "lon_1", "lat_0", "lat_1")
W = 256
R = 8
L = 128
H = 3
E = W + 8
NL = 16
B = 2 * NL
T = H * E
MIB = 1 << 20
CORE = (1, 2, 3, 4, 5)
SIDE = (0, 6, 7)


def weights(f):
    sixth = 1.0 / 6.0
    return (
        -f * (f - 1.0) * (f - 2.0) * sixth,
        (f + 1.0) * (f - 1.0) * (f - 2.0) * 0.5,
        -(f + 1.0) * f * (f - 2.0) * 0.5,
        (f + 1.0) * f * (f - 1.0) * sixth,
    )


def halves(x):
    high = x.astype(jnp.bfloat16)
    return high, (x - high.astype(jnp.float32)).astype(jnp.bfloat16)


def dot_nt(a, b):
    return lax.dot_general(
        a, b, (((1,), (1,)), ((), ())), preferred_element_type=jnp.float32
    )


def row_of(j):
    return pl.ds(j, W, stride=R)


def is_even():
    return lax.axis_index("lat_1") == 0


def at_end():
    place = 2 * lax.axis_index("lat_0") + lax.axis_index("lat_1")
    return (place == 0) | (place == 2 * lax.axis_size("lat_0") - 1)


def edges_kernel(tracer, pair, cross):
    even, end = is_even(), at_end()
    last = tracer[row_of(R - 1), :]
    first = tracer[row_of(0), :]
    second = tracer[row_of(1), :]
    pair[0:W] = jnp.where(even, last, first)
    pair[W : 2 * W] = second
    cross[0:W] = jnp.where(end, 0.0, jnp.where(even, first, last))
    cross[W : 2 * W] = jnp.where(end, 0.0, second)


def mix_rows(rows, row, fractions, held, out, sems):
    delta = lax.broadcasted_iota(jnp.int32, (L, L), 1) - lax.broadcasted_iota(
        jnp.int32, (L, L), 0
    )
    copies = []
    for at, j in enumerate(rows):
        w = weights(fractions[j : j + 1, :])
        mixed = w[0] * row(j - 1) + w[1] * row(j) + w[2] * row(j + 1) + w[3] * row(j + 2)
        v = weights(fractions[R + j : R + j + 1, :])
        table = jnp.zeros((L, L), jnp.float32)
        for m in range(4):
            table = jnp.where(delta == m - 1, v[m], table)
        t_high, t_low = halves(table)
        m_high, m_low = halves(mixed)
        left = jnp.concatenate(
            [
                jnp.concatenate([t_high, t_high], 1),
                jnp.concatenate([t_low, t_low], 1),
            ],
            0,
        )
        both = dot_nt(left, jnp.concatenate([m_high, m_low], 1))
        turned = (both[:L] + both[L:]).reshape(NL, 8, W)
        held[at, :, 0] = turned[:, :, :128]
        held[at, :, 1] = turned[:, :, 128:]
        copies.append(
            pltpu.make_async_copy(held.at[at], out.at[:, :, j], sems.at[at])
        )
        copies[-1].start()
    for copy in copies:
        copy.wait()


def mix_core_kernel(fractions, tracer, out, held, sems):
    mix_rows(CORE, lambda k: tracer[row_of(k), :], fractions, held, out, sems)


def mix_side_kernel(fractions, tracer, pair, cross, begun, out, held, sems):
    even = is_even()

    def row(k):
        if k < 0:
            return jnp.where(even, cross[0:W], pair[0:W])
        if k >= R:
            part = slice((k - R) * W, (k - R + 1) * W)
            return jnp.where(even, pair[part], cross[part])
        return tracer[row_of(k), :]

    mix_rows(SIDE, row, fractions, held, out, sems)


def shift_kernel(offsets, frac_lon, cells, out, twice):
    delta = lax.broadcasted_iota(jnp.int32, (128, 128), 0) - lax.broadcasted_iota(
        jnp.int32, (128, 128), 1
    )
    lane = lax.broadcasted_iota(jnp.int32, (1, 1, 128), 2)
    rims = jnp.zeros((NL, 8, 128), jnp.float32)
    for j in range(R):
        w = weights(frac_lon[j])
        off = offsets[j]
        turns = lax.shift_right_logical(off, 7)
        rest = jnp.bitwise_and(off, 127)
        placed = delta + rest
        left, right_high, right_low = [], [], []
        for k in range(3):
            table = jnp.zeros((128, 128), jnp.float32)
            for m in range(4):
                table = jnp.where(placed == m - 1 - 128 * (k - 1), w[m], table)
            t_high, t_low = halves(table)
            right_high += [t_high, t_high]
            right_low += [t_low, t_low]
            if k == 0:
                part = jnp.concatenate([cells[B - 1 :, j], cells[: B - 1, j]], 0)
            elif k == 1:
                part = cells[:, j]
            else:
                part = jnp.concatenate([cells[1:, j], cells[:1, j]], 0)
            left += list(halves(part.reshape(B * 8, 128)))
        right = jnp.concatenate(
            [jnp.concatenate(right_high, 0), jnp.concatenate(right_low, 0)], 1
        )
        both = jnp.dot(
            jnp.concatenate(left, 1), right, preferred_element_type=jnp.float32
        )
        value = (both[:, :128] + both[:, 128:]).reshape(B, 8, 128)
        twice[j, :B] = value
        twice[j, B:] = value
        start = jnp.bitwise_and(B - turns, B - 1)
        moved = twice[j, pl.ds(start, B)].reshape(NL, 2, 8, 128)
        near, far = moved[:, 0], moved[:, 1]
        out[:, j] = near
        out[:, R + j] = far
        east = jnp.concatenate([near[1:], near[:1]], 0)
        west = jnp.concatenate([far[NL - 1 :], far[: NL - 1]], 0)
        rim = jnp.where(lane < 64, east, west)
        if j > 0:
            rim = pltpu.roll(rim, 8 * j, 2)
        rims = jnp.where(jnp.bitwise_and(lane + (4 - 8 * j), 127) < 8, rim, rims)
    out[:, 2 * R] = rims


def edge(j):
    return j < H or j >= R - H


def turned_row(cells, rim, j, ref, at):
    sub = lax.broadcasted_iota(jnp.int32, (8, L), 0)
    for h in range(2):
        ref[at, h * 128 : (h + 1) * 128, :] = cells[:, h * R + j].reshape(L, 128).T
    before = (8 * j - 8) % 128
    tail = jnp.where(sub < 4, rim[8 * j : 8 * j + 8], rim[before : before + 8])
    ref[at, W:E, :] = tail


def vertical_rows(vertical):
    lane = lax.broadcasted_iota(jnp.int32, (1, L), 1)
    coef = vertical[...]
    return coef, jnp.where(lane == L - 1, 0.0, coef), jnp.where(lane == 0, 0.0, coef)


def precondition(inverse, value):
    m_high, m_low = halves(inverse)
    v_high, v_low = halves(value)
    right = jnp.concatenate(
        [
            jnp.concatenate([m_high, m_high], 1),
            jnp.concatenate([m_low, m_low], 1),
        ],
        0,
    )
    both = dot_nt(jnp.concatenate([v_high, v_low], 1), right)
    return both[:, :L] + both[:, L:]


def alone(q, m, rows):
    coef, upper, lower = rows
    result = q * (2.0 * m + 2.0 * coef + 2.1)
    result = result - m * (pltpu.roll(q, 1, 0) + pltpu.roll(q, E - 1, 0))
    result = result - upper * pltpu.roll(q, L - 1, 1)
    return result - lower * pltpu.roll(q, 1, 1)


def operate(q, south, north, m, rows):
    return alone(q, m, rows) - (south + north)


def metric_row(metric, j):
    return jnp.full((1, L), metric[j], jnp.float32)


Q1 = {0: 0, 1: 1, 2: 2, 5: 3, 6: 4, 7: 5}
V1_PART = {0: 6, 7: 7}
V1 = {1: 8, 6: 9}
Q2_PART = {0: 10, 7: 11}
Q2 = {1: 12, 6: 13}
V2_PART = {0: 14, 7: 15}
EARLY = 16
ENDS = ((0, 1, 2, 3), (7, 6, 5, 4))


def turn_kernel(metric, vertical, inverses, cells, ring, pair, cross, early):
    even, end = is_even(), at_end()
    rows = vertical_rows(vertical)
    rim = cells[:, 2 * R].reshape(L, 128).T
    for j in range(R):
        if edge(j):
            turned_row(cells, rim, j, ring, j)
            early[Q1[j]] = precondition(inverses[j], ring[j])
    for e, i, i2, _ in ENDS:
        early[V1_PART[e]] = alone(early[Q1[e]], metric_row(metric, e), rows) - early[Q1[i]]
        early[V1[i]] = operate(
            early[Q1[i]], early[Q1[e]], early[Q1[i2]], metric_row(metric, i), rows
        )
    for e, i, _, _ in ENDS:
        early[Q2_PART[e]] = precondition(inverses[e], early[V1_PART[e]])
        early[Q2[i]] = precondition(inverses[i], early[V1[i]])
    for e, i, _, _ in ENDS:
        early[V2_PART[e]] = (
            alone(early[Q2_PART[e]], metric_row(metric, e), rows) - early[Q2[i]]
        )
    sent = [
        (k * E, E, early[place[7]], early[place[0]])
        for k, place in enumerate((Q1, Q2_PART, V2_PART))
    ]
    sent.append((T, L, inverses[7], inverses[0]))
    sent.append((W + 3, 1, metric_row(metric, 7), metric_row(metric, 0)))
    for base, size, high, low in sent:
        pair[base : base + size] = jnp.where(even, high, low)
        cross[base : base + size] = jnp.where(end, 0.0, jnp.where(even, low, high))


def partial(a, b):
    return jnp.sum((a[:W] * b[:W]).reshape(W // 8, 8, L), 0)


def gram(depth, other):
    return 3 + depth * (depth + 1) // 2 + other


def tally(sums, depth, first, images, result):
    sums[depth] = sums[depth] + partial(first, result)
    for other in range(depth):
        k = gram(depth, other)
        sums[k] = sums[k] + partial(images[other], result)
    k = gram(depth, depth)
    sums[k] = sums[k] + partial(result, result)


def direction_of(search, new_search, early, depth, j):
    if depth == 0:
        return (early, Q1[j]) if j in Q1 else (search, 0, j)
    if 2 <= j <= 5:
        return (search, depth, j)
    return (early, Q2[j]) if depth == 1 and j in Q2 else (new_search, depth, j)


def image_of(field, new_field, early, depth, j):
    if depth == 0 and j in V1:
        return (early, V1[j])
    inner = 3 <= j <= 4 if depth == 2 else 2 <= j <= 5
    return (field if inner else new_field, depth, j)


def read(place, *more):
    return place[0][(*place[1:], *more)]


def inner_kernel(
    metric, vertical, inverses, cells, edges, early, search, field, totals, middle, advected, ring
):
    rows = vertical_rows(vertical)
    rim = cells[:, 2 * R].reshape(L, 128).T
    for j in range(R):
        if edge(j):
            ring[j] = edges[j]
        else:
            turned_row(cells, rim, j, ring, j)
            middle[j - H] = ring[j]
        advected[row_of(j), :] = ring[j, :W]
    sums = [jnp.zeros((8, L), jnp.float32) for _ in range(9)]

    def q(depth, j):
        return read(direction_of(search, None, early, depth, j))

    def v(depth, j):
        return read(image_of(field, None, early, depth, j))

    for depth, solved, applied in ((0, (3, 4), range(2, 6)), (1, range(2, 6), range(2, 6)), (2, range(2, 6), (3, 4))):
        for j in solved:
            search[depth, j] = precondition(
                inverses[j], ring[j] if depth == 0 else v(depth - 1, j)
            )
        for j in applied:
            field[depth, j] = operate(
                q(depth, j), q(depth, j - 1), q(depth, j + 1), metric_row(metric, j), rows
            )
        for j in (1, *applied, 6) if depth == 0 else applied:
            tally(sums, depth, ring[j], [v(o, j) for o in range(depth)], v(depth, j))
    for k in range(9):
        totals[k] = sums[k]


def outer_kernel(
    metric, vertical, inverses, edges, pair, cross, early, search, field, totals,
    new_search, new_field, sums_out,
):
    even = is_even()
    lane = lax.broadcasted_iota(jnp.int32, (1, L), 1)
    rows = vertical_rows(vertical)
    sums = [totals[k] for k in range(9)]

    def beyond(e, base, size):
        part = slice(base, base + size)
        first, second = (cross, pair) if e == 0 else (pair, cross)
        return jnp.where(even, first[part], second[part])

    def q(depth, j):
        return read(direction_of(search, new_search, early, depth, j))

    def v(depth, j):
        return read(image_of(field, new_field, early, depth, j))

    def add(depth, j):
        tally(sums, depth, edges[j], [v(o, j) for o in range(depth)], v(depth, j))

    def apply(depth, j, south_or_north, other):
        new_field[depth, j] = operate(
            q(depth, j), south_or_north, other, metric_row(metric, j), rows
        )
        add(depth, j)

    outside = []
    for e, _, _, _ in ENDS:
        outside.append(
            (
                beyond(e, T, L),
                beyond(e, W + 3, 1),
                precondition(beyond(e, T, L), early[Q1[e]]),
            )
        )
        new_field[0, e] = early[V1_PART[e]] - beyond(e, 0, E)
        add(0, e)
    for e, _, _, _ in ENDS:
        new_search[1, e] = precondition(inverses[e], new_field[0, e])
    last = []
    for (e, i, i2, _), (inverse, m, extra) in zip(ENDS, outside):
        apply(1, e, q(1, i), beyond(e, E, E) - extra)
        apply(1, i, q(1, e), q(1, i2))
        image = beyond(e, 2 * E, E) - alone(extra, m, rows) - q(1, e)
        last.append(precondition(inverse, image))
    for e, i, _, _ in ENDS:
        new_search[2, e] = precondition(inverses[e], new_field[1, e])
        new_search[2, i] = precondition(inverses[i], new_field[1, i])
    for (e, i, i2, i3), far in zip(ENDS, last):
        apply(2, e, q(2, i), far)
        apply(2, i, q(2, e), q(2, i2))
        apply(2, i2, q(2, i), q(2, i3))
    row = jnp.zeros((1, L), jnp.float32)
    for k in range(9):
        total = jnp.sum(jnp.sum(sums[k], 0, keepdims=True), 1, keepdims=True)
        row = jnp.where(lane == k, total, row)
    sums_out[...] = jnp.broadcast_to(row, sums_out.shape)


def finish_kernel(
    sums, edges, middle, early, search, field, new_search, new_field, pressure, residual,
    held, left, sems,
):
    lane = lax.broadcasted_iota(jnp.int32, (1, L), 1)
    row = jnp.sum(sums[...], 0, keepdims=True)

    def entry(index):
        value = jnp.sum(jnp.where(lane == index, row, 0.0), 1, keepdims=True)
        return jnp.broadcast_to(value, (1, L))

    b1, b2, b3, g11, g12, g22, g13, g23, g33 = (entry(i) for i in range(9))
    l21 = g12 / g11
    l31 = g13 / g11
    d2 = g22 - l21 * g12
    cross = g23 - l21 * g13
    l32 = cross / d2
    d3 = g33 - l31 * g13 - l32 * cross
    c2 = b2 - l21 * b1
    y1 = b1 / g11
    y2 = c2 / d2
    y3 = (b3 - l31 * b1 - l32 * c2) / d3
    k3 = y3
    k2 = y2 - l32 * k3
    k1 = y1 - l21 * k2 - l31 * k3
    parts = 4
    size = W // parts
    copies = []
    for part in range(parts):
        span = slice(part * size, (part + 1) * size)
        for j in range(R):
            q = [
                read(direction_of(search, new_search, early, depth, j), span)
                for depth in range(3)
            ]
            v = [
                read(image_of(field, new_field, early, depth, j), span)
                for depth in range(3)
            ]
            to = pl.ds(part * size * R + j, size, stride=R)
            held[to, :] = k1 * q[0] + k2 * q[1] + k3 * q[2]
            first = edges[j, span] if edge(j) else middle[j - H, span]
            left[to, :] = first - k1 * v[0] - k2 * v[1] - k3 * v[2]
        block = pl.ds(part * size * R, size * R)
        for i, (source, target) in enumerate(((held, pressure), (left, residual))):
            copy = pltpu.make_async_copy(
                source.at[block, :], target.at[block, :], sems.at[part, i]
            )
            copy.start()
            copies.append(copy)
    for copy in copies:
        copy.wait()


VMEM = pl.BlockSpec(memory_space=pltpu.VMEM)
SMEM = pl.BlockSpec(memory_space=pltpu.SMEM)
HBM = pl.BlockSpec(memory_space=pltpu.HBM)
ANY = pl.BlockSpec(memory_space=pl.ANY)


def call(
    kernel, ins, outs, scratch=(), limit=32, flops=0, where=VMEM, aliases=None, dtype=jnp.float32
):
    return pl.pallas_call(
        kernel,
        out_shape=tuple(jax.ShapeDtypeStruct(s, dtype) for s in outs),
        in_specs=list(ins),
        out_specs=tuple(where for _ in outs),
        scratch_shapes=[
            pltpu.VMEM(s, jnp.float32) if isinstance(s, tuple) else s for s in scratch
        ],
        input_output_aliases=aliases or {},
        compiler_params=pltpu.CompilerParams(vmem_limit_bytes=limit * MIB),
        cost_estimate=pl.CostEstimate(
            flops=flops, bytes_accessed=8 * MIB, transcendentals=0
        ),
    )


def body(count, tracer, offsets, frac_lon, frac_lat, frac_lev, metric, vertical_coef, inverses):
    in_chip = [(i, i ^ 1) for i in range(count)]
    across = [(i, (i - 1 + 2 * (i % 2)) % count) for i in range(count)]
    flat = tracer.reshape(W * R, L)
    pair_out, cross_out = call(edges_kernel, (VMEM,), ((2 * W, L), (2 * W, L)))(flat)
    cross_in = lax.ppermute(cross_out, LAT, across)
    pair_in = lax.ppermute(pair_out, LAT, in_chip)
    fractions = jnp.broadcast_to(
        jnp.concatenate([frac_lat, frac_lev])[:, None], (2 * R, L)
    )
    turned = None
    for kernel, n, extra in (
        (mix_core_kernel, 5, ()),
        (mix_side_kernel, 3, (pair_in, cross_in)),
    ):
        more = () if turned is None else (turned,)
        (turned,) = call(
            kernel,
            (VMEM,) * (2 + len(extra)) + (ANY,) * len(more),
            ((NL, 2, R, 8, 128),),
            scratch=((n, NL, 2, 8, 128), pltpu.SemaphoreType.DMA((n,))),
            where=ANY,
            aliases={4: 0} if more else None,
            flops=10**9,
        )(fractions, flat, *extra, *more)
    lines = lax.all_to_all(turned, LON, 0, 0, tiled=True)
    (moved,) = call(
        shift_kernel,
        (SMEM, SMEM, VMEM),
        ((NL, 2 * R + 1, 8, 128),),
        scratch=((R, 2 * B, 8, 128),),
    )(offsets, frac_lon, lines.reshape(B, R, 8, 128))
    back = lax.all_to_all(moved, LON, 0, 0, tiled=True)
    vertical = vertical_coef.reshape(1, L)
    edges, pair_out, cross_out, early = call(
        turn_kernel,
        (SMEM, VMEM, VMEM, VMEM),
        ((R, E, L), (T + L, L), (T + L, L), (EARLY, E, L)),
    )(metric, vertical, inverses, back)
    cross = lax.ppermute(cross_out, LAT, across)
    pair = lax.ppermute(pair_out, LAT, in_chip)
    search, images, totals, middle, advected = call(
        inner_kernel,
        (SMEM,) + (VMEM,) * 5,
        ((3, R, E, L), (3, R, E, L), (9, 8, L), (R - 2 * H, E, L), (W * R, L)),
        scratch=((R, E, L),),
        flops=2 * 10**9,
    )(metric, vertical, inverses, back, edges, early)
    new_search, new_images, sums = call(
        outer_kernel,
        (SMEM,) + (VMEM,) * 9,
        ((3, R, E, L), (3, R, E, L), (count * NL, L)),
    )(metric, vertical, inverses, edges, pair, cross, early, search, images, totals)
    gathered = lax.all_to_all(sums, LON_LAT, 0, 0, tiled=True)
    pressure, residual = call(
        finish_kernel,
        (VMEM,) * 8,
        ((W * R, L), (W * R, L)),
        scratch=((W * R, L), (W * R, L), pltpu.SemaphoreType.DMA((4, 2))),
        where=HBM,
    )(gathered, edges, middle, early, search, images, new_search, new_images)
    return tuple(x.reshape(W, R, L) for x in (advected, pressure, residual))


def solution(mesh):
    count = mesh.shape["lat"]
    split = Mesh(mesh.devices.reshape(4, 4, count // 2, 2), LON_LAT)
    placed = (P(LON, LAT, None), P(LAT), P(LAT), P(LAT), P(LAT), P(LAT), P(), P(LAT, None, None))
    return jax.shard_map(
        functools.partial(body, count),
        mesh=split,
        in_specs=placed,
        out_specs=(P(LON, LAT, None),) * 3,
        check_vma=False,
    )
```

time: 98 us -> 96.4 us (0.984)
  blocking collectives: 41.6 us -> 57.4 us
  waiting for transfers between devices: 18 us -> 6.9 us
  starting transfers between devices: 22.7 us -> 15.8 us
    all_to_all x0 -> x1, blocking collectives: none -> 16.6 us  [body(): lines = lax.all_to_all(turned, LON, 0, 0, tiled=True)]
    all_to_all x1 -> x0, waiting for transfers between devices: 6.61 us -> none  [body(): lines = lax.all_to_all(turned, LON, 0, 0, tiled=True)]
    all_to_all x1 -> x0, starting transfers between devices: 4.86 us -> none  [body(): lines = lax.all_to_all(turned, LON, 0, 0, tiled=True)]
    ppermute x1 -> x0, waiting for transfers between devices: 3.35 us -> none  [body(): inv_in = lax.ppermute(inv_out, LAT, across)]
    ppermute x1 -> x0, starting transfers between devices: 1.99 us -> none  [body(): inv_in = lax.ppermute(inv_out, LAT, across)]
    ppermute x1, waiting for transfers between devices: 4.93 us -> 3.79 us  [body(): cross_in = lax.ppermute(cross_out, LAT, across)]
    pallas_call x6 -> x7, Pallas kernels: 12.5 us -> 13.2 us  [the longest x1 3.19 us: body(): call(inner_kernel, (SMEM,) + (VMEM,) * 5, ((3, R, E, L), (3, R, E, L), (9...]
  transfers between devices with their start and end apart: 6 -> 4, of which waited for: 5 -> 2; matrix products, arithmetic and copies ran while one was open for 1% -> 1% of each run, Pallas kernels for 3% -> 5%
where the time goes in v4:
time: 96.4 us; the launch traced here: 96.2 us
  blocking collectives  57.4 us (60%)
  starting transfers between devices  15.8 us (16%)
  Pallas kernels  13.3 us (14%)
  waiting for transfers between devices  6.9 us (7%)
  local copies, waits for them, and re-layouts  1.32 us (1%)
    all_to_all x1, blocking collectives, body(): gathered = lax.all_to_all(sums, LON_LAT, 0, 0, tiled=True)  24.8 us
    all_to_all x1, blocking collectives, body(): lines = lax.all_to_all(turned, LON, 0, 0, tiled=True)  16.6 us
    all_to_all x1, blocking collectives, body(): back = lax.all_to_all(moved, LON, 0, 0, tiled=True)  16 us
    ppermute x1, starting transfers between devices, body(): pair = lax.ppermute(pair_out, LAT, in_chip)  6.77 us
    ppermute x1, starting transfers between devices, body(): cross = lax.ppermute(cross_out, LAT, across)  5.69 us
    ppermute x1, waiting for transfers between devices, body(): cross_in = lax.ppermute(cross_out, LAT, across)  3.79 us
    ppermute x1, starting transfers between devices, body(): pair_in = lax.ppermute(pair_out, LAT, in_chip)  3.33 us
    pallas_call x1, Pallas kernels, body(): call(inner_kernel, (SMEM,) + (VMEM,) * 5, ((3, R, E, L), (3, R, E, L), (9...  3.19 us
  transfers between devices with their start and end apart: 4, of which 2 were waited for; matrix products, arithmetic and copies ran while one was open for 1% of the time, Pallas kernels for 5%

profile of v4, /device:TPU:1, one launch (start us, length us, event | category | flops | bytes accessed | tf_op | source)
XLA Modules:
  0.0 96.2 jit_solution(9434816435602629072)
XLA Ops:
  0.6 1.2 %copy-done.1 = f32[256,8,128]{2,1,0:T(8,128)S(1)} copy-done((f32[256,8,128]{2,1,0:T(8,128)S(1)}, f32[256,8,128]{2,1,0:T(8,128)}, u32[]{:S(2)}) %copy-start.1) | copy-done | bytes 1048600
  1.9 0.1 shard_map.103
  2.0 3.3 %collective-permute-start = (f32[512,128]{1,0:T(8,128)S(1)}, f32[512,128]{1,0:T(8,128)S(1)}, u32[]{:S(2)}, u32[]{:S(2)}) collective-permute-start(f32[512,128]{1,0:T(8,128)S(1)} %get-tuple-element.19), channel_id=1, source_target_pairs={{0,1},{1,0},{2,3},{3,2},{4,5},{5,4},{6,7},{7,6},{8,9},{9,8},{10,11... | collective-permute-start | bytes 786440 | tf_op jit(solution)/shard_map/ppermute | solution.py:481
  5.3 0.7 pad_maximum_fusion
  6.0 0.1 broadcast_in_dim.2.fractions
  6.1 1.4 %shard_map.104.begun = f32[16,2,8,8,128]{4,3,2,1,0:T(8,128)S(1)} custom-call(f32[16,128]{1,0:T(8,128)S(1)} %broadcast_in_dim.2.fractions, f32[2048,128]{1,0:T(8,128)S(1)} %bitcast.12), custom_call_target="tpu_custom_call" | custom-call | flops 1000000000 | bytes 8388608 | tf_op jit(solution)/shard_map/pallas_call | solution.py:491
  7.6 0.0 copy-start.4
  7.6 0.0 copy-start.5
  7.6 3.8 %collective-permute-done.1.cross = f32[512,128]{1,0:T(8,128)S(1)} collective-permute-done((f32[512,128]{1,0:T(8,128)S(1)}, f32[512,128]{1,0:T(8,128)S(1)}, u32[]{:S(2)}, u32[]{:S(2)}) %collective-permute-start.1) | collective-permute-done | bytes 262176 | tf_op jit(solution)/shard_map/ppermute | solution.py:480
  11.4 0.9 shard_map.105
  12.2 0.0 copy-start
  12.3 0.0 copy-start.2
  12.3 0.0 copy-start.3
  12.3 16.6 %all_to_all.21 = f32[16,2,8,8,128]{4,3,2,1,0:T(8,128)S(1)} all-to-all(f32[16,2,8,8,128]{4,3,2,1,0:T(8,128)S(1)} %shard_map.105), channel_id=1, replica_groups=mesh['lon_0'=4,'lon_1'=4,'lat_0'=8,'lat_1'=2] {'lon_0','lon_1'}, dimensions={0} | all-to-all | bytes 2097152 | tf_op jit(solution)/shard_map/all_to_all | solution.py:500
  28.8 2.0 %shard_map.106 = f32[16,17,8,128]{3,2,1,0:T(8,128)S(1)} custom-call(s32[8]{0:T(128)S(1)} %copy-done.4, f32[8]{0:T(128)S(1)} %copy-done.5, f32[32,8,8,128]{3,2,1,0:T(8,128)S(1)} %bitcast.10), custom_call_target="tpu_custom_call" | custom-call | bytes 8388608 | tf_op jit(solution)/shard_map/pallas_call | solution.py:501
  30.8 16.0 %all_to_all.22.cells = f32[16,17,8,128]{3,2,1,0:T(8,128)S(1)} all-to-all(f32[16,17,8,128]{3,2,1,0:T(8,128)S(1)} %shard_map.106), channel_id=1, replica_groups=mesh['lon_0'=4,'lon_1'=4,'lat_0'=8,'lat_1'=2] {'lon_0','lon_1'}, dimensions={0} | all-to-all | bytes 2228224 | tf_op jit(solution)/shard_map/all_to_all | solution.py:507
  46.8 1.5 %shard_map.107 = (f32[8,264,128]{2,1,0:T(8,128)S(1)}, f32[920,128]{1,0:T(8,128)S(1)}, f32[920,128]{1,0:T(8,128)S(1)}, f32[16,264,128]{2,1,0:T(8,128)S(1)}) custom-call(f32[8]{0:T(128)S(1)} %copy-done.2, f32[1,128]{1,0:T(1,128)S(1)} %bitcast.16, f32[8,128,128]{2,1,0:T(8,128)S(1)} %copy-done, f32[16,17,8,128]{3,2,1,0:T(8,128)S(1)} %all_to_all.22.cells), custom_call_target="tpu_custom_call" | custom-call | bytes 8388608 | tf_op jit(solution)/shard_map/pallas_call | solution.py:509
  48.3 6.8 %collective-permute-start.2 = (f32[920,128]{1,0:T(8,128)S(1)}, f32[920,128]{1,0:T(8,128)S(1)}, u32[]{:S(2)}, u32[]{:S(2)}) collective-permute-start(f32[920,128]{1,0:T(8,128)S(1)} %get-tuple-element.24), channel_id=1, source_target_pairs={{0,1},{1,0},{2,3},{3,2},{4,5},{5,4},{6,7},{7,6},{8,9},{9,8},{10,11... | collective-permute-start | bytes 1413128 | tf_op jit(solution)/shard_map/ppermute | solution.py:515
  55.1 5.7 %collective-permute-start.3 = (f32[920,128]{1,0:T(8,128)S(1)}, f32[920,128]{1,0:T(8,128)S(1)}, u32[]{:S(2)}, u32[]{:S(2)}) collective-permute-start(f32[920,128]{1,0:T(8,128)S(1)} %get-tuple-element.25), channel_id=1, source_target_pairs={{0,15},{1,2},{2,1},{3,4},{4,3},{5,6},{6,5},{7,8},{8,7},{9,10},{10,... | collective-permute-start | bytes 1413128 | tf_op jit(solution)/shard_map/ppermute | solution.py:514
  60.8 3.2 %shard_map.108 = (f32[3,8,264,128]{3,2,1,0:T(8,128)S(1)}, f32[3,8,264,128]{3,2,1,0:T(8,128)S(1)}, f32[9,8,128]{2,1,0:T(8,128)S(1)}, f32[2,264,128]{2,1,0:T(8,128)S(1)}, f32[2048,128]{1,0:T(8,128)}) custom-call(f32[8]{0:T(128)S(1)} %copy-done.2, f32[1,128]{1,0:T(1,128)S(1)} %bitcast.17, f32[8,128,128]{2,1,0:T(8,128)S(1)} %copy-done, ...), custom_call_target="tpu_custom_call" | custom-call | flops 2000000000 | bytes 8388608 | tf_op jit(solution)/shard_map/pallas_call | solution.py:516
  64.0 3.1 %collective-permute-done.3.cross = f32[920,128]{1,0:T(8,128)S(1)} collective-permute-done((f32[920,128]{1,0:T(8,128)S(1)}, f32[920,128]{1,0:T(8,128)S(1)}, u32[]{:S(2)}, u32[]{:S(2)}) %collective-permute-start.3) | collective-permute-done | bytes 471072 | tf_op jit(solution)/shard_map/ppermute | solution.py:514
  67.1 2.6 %shard_map.109 = (f32[3,8,264,128]{3,2,1,0:T(8,128)S(1)}, f32[3,8,264,128]{3,2,1,0:T(8,128)S(1)}, f32[256,128]{1,0:T(8,128)S(1)}) custom-call(f32[8]{0:T(128)S(1)} %copy-done.2, f32[1,128]{1,0:T(1,128)S(1)} %bitcast.18, f32[8,128,128]{2,1,0:T(8,128)S(1)} %copy-done, f32[8,264,128]{2,1,0:T(8,128)S(1)} %get-tuple-element.21.edges, ...), custom_call_target="tpu_custom_call" | custom-call | bytes 8388608 | tf_op jit(solution)/shard_map/pallas_call | solution.py:523
  69.7 24.8 %all_to_all.23 = f32[256,1,128]{2,1,0:T(1,128)S(1)} all-to-all(f32[256,1,128]{2,1,0:T(1,128)S(1)} %bitcast.15), channel_id=1, replica_groups=mesh['lon_0'=4,'lon_1'=4,'lat_0'=8,'lat_1'=2] {'lon_0','lon_1','lat_0','..., dimensions={0} | all-to-all | bytes 262144 | tf_op jit(solution)/shard_map/all_to_all | solution.py:528
  94.5 1.7 %shard_map.110 = (f32[2048,128]{1,0:T(8,128)}, f32[2048,128]{1,0:T(8,128)}) custom-call(f32[256,128]{1,0:T(8,128)S(1)} %bitcast.14, f32[8,264,128]{2,1,0:T(8,128)S(1)} %get-tuple-element.21.edges, f32[2,264,128]{2,1,0:T(8,128)S(1)} %get-tuple-element.30.middle, f32[16,264,128]{2,1,0:T(8,128)S(1)} %get-tuple-element.22.early, ...), custom_call_target="tpu_custom_call" | custom-call | bytes 8388608 | tf_op jit(solution)/shard_map/pallas_call | solution.py:529
  (9 shorter events, 0.0 us)
Async XLA Ops:
  0.6 1.2 %copy-start.1 = (f32[256,8,128]{2,1,0:T(8,128)S(1)}, f32[256,8,128]{2,1,0:T(8,128)}, u32[]{:S(2)}) copy-start(f32[256,8,128]{2,1,0:T(8,128)} %param.8) | copy-start | bytes 3145732
  2.0 5.6 %collective-permute-start = (f32[512,128]{1,0:T(8,128)S(1)}, f32[512,128]{1,0:T(8,128)S(1)}, u32[]{:S(2)}, u32[]{:S(2)}) collective-permute-start(f32[512,128]{1,0:T(8,128)S(1)} %get-tuple-element.19), channel_id=1, source_target_pairs={{0,1},{1,0},{2,3},{3,2},{4,5},{5,4},{6,7},{7,6},{8,9},{9,8},{10,11... | collective-permute-start | bytes 786440 | tf_op jit(solution)/shard_map/ppermute | solution.py:481
  5.3 6.1 %collective-permute-start.1 = (f32[512,128]{1,0:T(8,128)S(1)}, f32[512,128]{1,0:T(8,128)S(1)}, u32[]{:S(2)}, u32[]{:S(2)}) collective-permute-start(f32[512,128]{1,0:T(8,128)S(1)} %get-tuple-element.20), channel_id=1, source_target_pairs={{0,15},{1,2},{2,1},{3,4},{4,3},{5,6},{6,5},{7,8},{8,7},{9,10},{10,... | collective-permute-start | bytes 786440 | tf_op jit(solution)/shard_map/ppermute | solution.py:480
  7.6 21.3 %copy-start.4 = (s32[8]{0:T(128)S(1)}, s32[8]{0:T(128)}, u32[]{:S(2)}) copy-start(s32[8]{0:T(128)} %offsets.1) | copy-start | bytes 100
  7.6 21.3 %copy-start.5 = (f32[8]{0:T(128)S(1)}, f32[8]{0:T(128)}, u32[]{:S(2)}) copy-start(f32[8]{0:T(128)} %frac_lon.1) | copy-start | bytes 100
  12.2 34.6 %copy-start = (f32[8,128,128]{2,1,0:T(8,128)S(1)}, f32[8,128,128]{2,1,0:T(8,128)}, u32[]{:S(2)}) copy-start(f32[8,128,128]{2,1,0:T(8,128)} %inverses.5) | copy-start | bytes 1572868
  12.3 34.6 %copy-start.2 = (f32[8]{0:T(128)S(1)}, f32[8]{0:T(128)}, u32[]{:S(2)}) copy-start(f32[8]{0:T(128)} %metric.5) | copy-start | bytes 100
  12.3 34.6 %copy-start.3 = (f32[128]{0:T(128)S(1)}, f32[128]{0:T(128)}, u32[]{:S(2)}) copy-start(f32[128]{0:T(128)} %param.14) | copy-start | bytes 1540
  48.3 15.6 %collective-permute-start.2 = (f32[920,128]{1,0:T(8,128)S(1)}, f32[920,128]{1,0:T(8,128)S(1)}, u32[]{:S(2)}, u32[]{:S(2)}) collective-permute-start(f32[920,128]{1,0:T(8,128)S(1)} %get-tuple-element.24), channel_id=1, source_target_pairs={{0,1},{1,0},{2,3},{3,2},{4,5},{5,4},{6,7},{7,6},{8,9},{9,8},{10,11... | collective-permute-start | bytes 1413128 | tf_op jit(solution)/shard_map/ppermute | solution.py:515
  55.1 12.0 %collective-permute-start.3 = (f32[920,128]{1,0:T(8,128)S(1)}, f32[920,128]{1,0:T(8,128)S(1)}, u32[]{:S(2)}, u32[]{:S(2)}) collective-permute-start(f32[920,128]{1,0:T(8,128)S(1)} %get-tuple-element.25), channel_id=1, source_target_pairs={{0,15},{1,2},{2,1},{3,4},{4,3},{5,6},{6,5},{7,8},{8,7},{9,10},{10,... | collective-permute-start | bytes 1413128 | tf_op jit(solution)/shard_map/ppermute | solution.py:514

commit v5 on v4

--- a/solution.py
+++ b/solution.py
@@ -106,7 +106,7 @@
     mix_rows(CORE, lambda k: tracer[row_of(k), :], fractions, held, out, sems)
 
 
-def mix_side_kernel(fractions, tracer, pair, cross, begun, out, held, sems):
+def mix_side_kernel(fractions, tracer, cross, pair, begun, out, held, sems):
     even = is_even()
 
     def row(k):
@@ -229,7 +229,7 @@
 ENDS = ((0, 1, 2, 3), (7, 6, 5, 4))
 
 
-def turn_kernel(metric, vertical, inverses, cells, ring, pair, cross, early):
+def turn_kernel(metric, vertical, inverses, cells, ring, cross, early):
     even, end = is_even(), at_end()
     rows = vertical_rows(vertical)
     rim = cells[:, 2 * R].reshape(L, 128).T
@@ -249,15 +249,18 @@
         early[V2_PART[e]] = (
             alone(early[Q2_PART[e]], metric_row(metric, e), rows) - early[Q2[i]]
         )
+    for base, size, high, low in sent_rows(metric, inverses, early):
+        cross[base : base + size] = jnp.where(end, 0.0, jnp.where(even, low, high))
+
+
+def sent_rows(metric, inverses, early):
     sent = [
         (k * E, E, early[place[7]], early[place[0]])
         for k, place in enumerate((Q1, Q2_PART, V2_PART))
     ]
     sent.append((T, L, inverses[7], inverses[0]))
     sent.append((W + 3, 1, metric_row(metric, 7), metric_row(metric, 0)))
-    for base, size, high, low in sent:
-        pair[base : base + size] = jnp.where(even, high, low)
-        cross[base : base + size] = jnp.where(end, 0.0, jnp.where(even, low, high))
+    return sent
 
 
 def partial(a, b):
@@ -297,8 +300,11 @@
 
 
 def inner_kernel(
-    metric, vertical, inverses, cells, edges, early, search, field, totals, middle, advected, ring
+    metric, vertical, inverses, cells, edges, early,
+    search, field, totals, middle, advected, pair, ring,
 ):
+    for base, size, high, low in sent_rows(metric, inverses, early):
+        pair[base : base + size] = jnp.where(is_even(), high, low)
     rows = vertical_rows(vertical)
     rim = cells[:, 2 * R].reshape(L, 128).T
     for j in range(R):
@@ -454,13 +460,13 @@
 
 
 def call(
-    kernel, ins, outs, scratch=(), limit=32, flops=0, where=VMEM, aliases=None, dtype=jnp.float32
+    kernel, ins, outs, scratch=(), limit=32, flops=0, where=(), aliases=None, dtype=jnp.float32
 ):
     return pl.pallas_call(
         kernel,
         out_shape=tuple(jax.ShapeDtypeStruct(s, dtype) for s in outs),
         in_specs=list(ins),
-        out_specs=tuple(where for _ in outs),
+        out_specs=where or (VMEM,) * len(outs),
         scratch_shapes=[
             pltpu.VMEM(s, jnp.float32) if isinstance(s, tuple) else s for s in scratch
         ],
@@ -477,26 +483,27 @@
     across = [(i, (i - 1 + 2 * (i % 2)) % count) for i in range(count)]
     flat = tracer.reshape(W * R, L)
     pair_out, cross_out = call(edges_kernel, (VMEM,), ((2 * W, L), (2 * W, L)))(flat)
+    pair_in = lax.ppermute(pair_out, LAT, in_chip)
     cross_in = lax.ppermute(cross_out, LAT, across)
-    pair_in = lax.ppermute(pair_out, LAT, in_chip)
     fractions = jnp.broadcast_to(
         jnp.concatenate([frac_lat, frac_lev])[:, None], (2 * R, L)
     )
-    turned = None
-    for kernel, n, extra in (
-        (mix_core_kernel, 5, ()),
-        (mix_side_kernel, 3, (pair_in, cross_in)),
-    ):
-        more = () if turned is None else (turned,)
-        (turned,) = call(
-            kernel,
-            (VMEM,) * (2 + len(extra)) + (ANY,) * len(more),
-            ((NL, 2, R, 8, 128),),
-            scratch=((n, NL, 2, 8, 128), pltpu.SemaphoreType.DMA((n,))),
-            where=ANY,
-            aliases={4: 0} if more else None,
-            flops=10**9,
-        )(fractions, flat, *extra, *more)
+    (begun,) = call(
+        mix_core_kernel,
+        (VMEM,) * 2,
+        ((NL, 2, R, 8, 128),),
+        scratch=((5, NL, 2, 8, 128), pltpu.SemaphoreType.DMA((5,))),
+        where=(ANY,),
+        flops=10**9,
+    )(fractions, flat)
+    (turned,) = call(
+        mix_side_kernel,
+        (VMEM,) * 4 + (ANY,),
+        ((NL, 2, R, 8, 128),),
+        scratch=((3, NL, 2, 8, 128), pltpu.SemaphoreType.DMA((3,))),
+        where=(ANY,),
+        aliases={4: 0},
+    )(fractions, flat, cross_in, pair_in, begun)
     lines = lax.all_to_all(turned, LON, 0, 0, tiled=True)
     (moved,) = call(
         shift_kernel,
@@ -506,20 +513,20 @@
     )(offsets, frac_lon, lines.reshape(B, R, 8, 128))
     back = lax.all_to_all(moved, LON, 0, 0, tiled=True)
     vertical = vertical_coef.reshape(1, L)
-    edges, pair_out, cross_out, early = call(
+    edges, cross_out, early = call(
         turn_kernel,
         (SMEM, VMEM, VMEM, VMEM),
-        ((R, E, L), (T + L, L), (T + L, L), (EARLY, E, L)),
+        ((R, E, L), (T + L, L), (EARLY, E, L)),
     )(metric, vertical, inverses, back)
     cross = lax.ppermute(cross_out, LAT, across)
-    pair = lax.ppermute(pair_out, LAT, in_chip)
-    search, images, totals, middle, advected = call(
+    search, images, totals, middle, advected, pair_out = call(
         inner_kernel,
         (SMEM,) + (VMEM,) * 5,
-        ((3, R, E, L), (3, R, E, L), (9, 8, L), (R - 2 * H, E, L), (W * R, L)),
+        ((3, R, E, L), (3, R, E, L), (9, 8, L), (R - 2 * H, E, L), (W * R, L), (T + L, L)),
         scratch=((R, E, L),),
         flops=2 * 10**9,
     )(metric, vertical, inverses, back, edges, early)
+    pair = lax.ppermute(pair_out, LAT, in_chip)
     new_search, new_images, sums = call(
         outer_kernel,
         (SMEM,) + (VMEM,) * 9,
@@ -531,7 +538,7 @@
         (VMEM,) * 8,
         ((W * R, L), (W * R, L)),
         scratch=((W * R, L), (W * R, L), pltpu.SemaphoreType.DMA((4, 2))),
-        where=HBM,
+        where=(HBM, HBM),
     )(gathered, edges, middle, early, search, images, new_search, new_images)
     return tuple(x.reshape(W, R, L) for x in (advected, pressure, residual))
 

time: 96.4 us -> 95.1 us (0.987)
  waiting for transfers between devices: 6.9 us -> 1.47 us
  blocking collectives: 57.4 us -> 60.5 us
    all_to_all x1, blocking collectives: 16.6 us -> 21.7 us  [body(): lines = lax.all_to_all(turned, LON, 0, 0, tiled=True)]
    ppermute x1, waiting for transfers between devices: 3.79 us -> 0.01 us  [body(): cross_in = lax.ppermute(cross_out, LAT, across)]
    all_to_all x1, blocking collectives: 24.8 us -> 21.4 us  [body(): gathered = lax.all_to_all(sums, LON_LAT, 0, 0, tiled=True)]
    ppermute x1, starting transfers between devices: 0.01 us -> 3.11 us  [body(): cross_in = lax.ppermute(cross_out, LAT, across)]
    ppermute x1, waiting for transfers between devices: 3.1 us -> 0.01 us  [body(): cross = lax.ppermute(cross_out, LAT, across)]
    ppermute x1, starting transfers between devices: 6.77 us -> 4.17 us  [body(): pair = lax.ppermute(pair_out, LAT, in_chip)]
    ppermute x1, waiting for transfers between devices: 0.01 us -> 1.46 us  [body(): pair = lax.ppermute(pair_out, LAT, in_chip)]
    all_to_all x1, blocking collectives: 16 us -> 17.4 us  [body(): back = lax.all_to_all(moved, LON, 0, 0, tiled=True)]
  transfers between devices with their start and end apart: 4 -> 4, of which waited for: 2 -> 1; matrix products, arithmetic and copies ran while one was open for 1% -> 1% of each run, Pallas kernels for 5% -> 5%
where the time goes in v5:
time: 95.1 us; the launch traced here: 94.8 us
  blocking collectives  60.5 us (64%)
  starting transfers between devices  16.7 us (18%)
  Pallas kernels  13.4 us (14%)
  waiting for transfers between devices  1.47 us (2%)
  local copies, waits for them, and re-layouts  1.32 us (1%)
    all_to_all x1, blocking collectives, body(): lines = lax.all_to_all(turned, LON, 0, 0, tiled=True)  21.7 us
    all_to_all x1, blocking collectives, body(): gathered = lax.all_to_all(sums, LON_LAT, 0, 0, tiled=True)  21.4 us
    all_to_all x1, blocking collectives, body(): back = lax.all_to_all(moved, LON, 0, 0, tiled=True)  17.4 us
    ppermute x1, starting transfers between devices, body(): cross = lax.ppermute(cross_out, LAT, across)  5.68 us
    ppermute x1, starting transfers between devices, body(): pair = lax.ppermute(pair_out, LAT, in_chip)  4.17 us
    ppermute x1, starting transfers between devices, body(): pair_in = lax.ppermute(pair_out, LAT, in_chip)  3.77 us
    pallas_call x1, Pallas kernels, body(): call(inner_kernel, (SMEM,) + (VMEM,) * 5, ((3, R, E, L), (3, R, E, L), (9...  3.23 us
    ppermute x1, starting transfers between devices, body(): cross_in = lax.ppermute(cross_out, LAT, across)  3.11 us
  transfers between devices with their start and end apart: 4, of which 1 were waited for; matrix products, arithmetic and copies ran while one was open for 1% of the time, Pallas kernels for 5%

profile of v5, /device:TPU:1, one launch (start us, length us, event | category | flops | bytes accessed | tf_op | source)
XLA Modules:
  0.0 94.8 jit_solution(6115264301451192485)
XLA Ops:
  0.6 1.2 %copy-done = f32[256,8,128]{2,1,0:T(8,128)S(1)} copy-done((f32[256,8,128]{2,1,0:T(8,128)S(1)}, f32[256,8,128]{2,1,0:T(8,128)}, u32[]{:S(2)}) %copy-start) | copy-done | bytes 1048600
  1.9 0.1 shard_map.103
  2.0 3.1 %collective-permute-start = (f32[512,128]{1,0:T(8,128)S(1)}, f32[512,128]{1,0:T(8,128)S(1)}, u32[]{:S(2)}, u32[]{:S(2)}) collective-permute-start(f32[512,128]{1,0:T(8,128)S(1)} %get-tuple-element.19), channel_id=1, source_target_pairs={{0,15},{1,2},{2,1},{3,4},{4,3},{5,6},{6,5},{7,8},{8,7},{9,10},{10,... | collective-permute-start | bytes 786440 | tf_op jit(solution)/shard_map/ppermute | solution.py:487
  5.1 3.8 %collective-permute-start.1 = (f32[512,128]{1,0:T(8,128)S(1)}, f32[512,128]{1,0:T(8,128)S(1)}, u32[]{:S(2)}, u32[]{:S(2)}) collective-permute-start(f32[512,128]{1,0:T(8,128)S(1)} %get-tuple-element.20), channel_id=1, source_target_pairs={{0,1},{1,0},{2,3},{3,2},{4,5},{5,4},{6,7},{7,6},{8,9},{9,8},{10,11... | collective-permute-start | bytes 786440 | tf_op jit(solution)/shard_map/ppermute | solution.py:486
  8.8 0.7 pad_maximum_fusion
  9.6 0.1 broadcast_in_dim.2.fractions
  9.7 1.4 %shard_map.104.begun = f32[16,2,8,8,128]{4,3,2,1,0:T(8,128)S(1)} custom-call(f32[16,128]{1,0:T(8,128)S(1)} %broadcast_in_dim.2.fractions, f32[2048,128]{1,0:T(8,128)S(1)} %bitcast.11), custom_call_target="tpu_custom_call" | custom-call | flops 1000000000 | bytes 8388608 | tf_op jit(solution)/shard_map/pallas_call | solution.py:491
  11.1 0.0 copy-start.4
  11.1 0.0 copy-start.5
  11.2 0.9 shard_map.105
  12.0 0.0 copy-start.1
  12.0 0.0 copy-start.2
  12.0 0.0 copy-start.3
  12.1 21.7 %all_to_all.21 = f32[16,2,8,8,128]{4,3,2,1,0:T(8,128)S(1)} all-to-all(f32[16,2,8,8,128]{4,3,2,1,0:T(8,128)S(1)} %shard_map.105), channel_id=1, replica_groups=mesh['lon_0'=4,'lon_1'=4,'lat_0'=8,'lat_1'=2] {'lon_0','lon_1'}, dimensions={0} | all-to-all | bytes 2097152 | tf_op jit(solution)/shard_map/all_to_all | solution.py:507
  33.7 2.0 %shard_map.106 = f32[16,17,8,128]{3,2,1,0:T(8,128)S(1)} custom-call(s32[8]{0:T(128)S(1)} %copy-done.4, f32[8]{0:T(128)S(1)} %copy-done.5, f32[32,8,8,128]{3,2,1,0:T(8,128)S(1)} %bitcast.13), custom_call_target="tpu_custom_call" | custom-call | bytes 8388608 | tf_op jit(solution)/shard_map/pallas_call | solution.py:508
  35.7 17.4 %all_to_all.22.cells = f32[16,17,8,128]{3,2,1,0:T(8,128)S(1)} all-to-all(f32[16,17,8,128]{3,2,1,0:T(8,128)S(1)} %shard_map.106), channel_id=1, replica_groups=mesh['lon_0'=4,'lon_1'=4,'lat_0'=8,'lat_1'=2] {'lon_0','lon_1'}, dimensions={0} | all-to-all | bytes 2228224 | tf_op jit(solution)/shard_map/all_to_all | solution.py:514
  53.1 1.5 %shard_map.107 = (f32[8,264,128]{2,1,0:T(8,128)S(1)}, f32[920,128]{1,0:T(8,128)S(1)}, f32[16,264,128]{2,1,0:T(8,128)S(1)}) custom-call(f32[8]{0:T(128)S(1)} %copy-done.2, f32[1,128]{1,0:T(1,128)S(1)} %bitcast.16, f32[8,128,128]{2,1,0:T(8,128)S(1)} %copy-done.1, f32[16,17,8,128]{3,2,1,0:T(8,128)S(1)} %all_to_all.22.cells), custom_call_target="tpu_custom_call" | custom-call | bytes 8388608 | tf_op jit(solution)/shard_map/pallas_call | solution.py:516
  54.6 5.7 %collective-permute-start.3 = (f32[920,128]{1,0:T(8,128)S(1)}, f32[920,128]{1,0:T(8,128)S(1)}, u32[]{:S(2)}, u32[]{:S(2)}) collective-permute-start(f32[920,128]{1,0:T(8,128)S(1)} %get-tuple-element.25), channel_id=1, source_target_pairs={{0,15},{1,2},{2,1},{3,4},{4,3},{5,6},{6,5},{7,8},{8,7},{9,10},{10,... | collective-permute-start | bytes 1413128 | tf_op jit(solution)/shard_map/ppermute | solution.py:521
  60.3 3.2 %shard_map.108 = (f32[3,8,264,128]{3,2,1,0:T(8,128)S(1)}, f32[3,8,264,128]{3,2,1,0:T(8,128)S(1)}, f32[9,8,128]{2,1,0:T(8,128)S(1)}, f32[2,264,128]{2,1,0:T(8,128...) custom-call(f32[8]{0:T(128)S(1)} %copy-done.2, f32[1,128]{1,0:T(1,128)S(1)} %bitcast.17, ...), custom_call_target="tpu_custom_call" | custom-call | flops 2000000000 | bytes 8388608 | tf_op jit(solution)/shard_map/pallas_call | solution.py:522
  63.5 4.2 %collective-permute-start.2 = (f32[920,128]{1,0:T(8,128)S(1)}, f32[920,128]{1,0:T(8,128)S(1)}, u32[]{:S(2)}, u32[]{:S(2)}) collective-permute-start(f32[920,128]{1,0:T(8,128)S(1)} %get-tuple-element.24), channel_id=1, source_target_pairs={{0,1},{1,0},{2,3},{3,2},{4,5},{5,4},{6,7},{7,6},{8,9},{9,8},{10,11... | collective-permute-start | bytes 1413128 | tf_op jit(solution)/shard_map/ppermute | solution.py:529
  67.7 1.5 %collective-permute-done.2.pair = f32[920,128]{1,0:T(8,128)S(1)} collective-permute-done((f32[920,128]{1,0:T(8,128)S(1)}, f32[920,128]{1,0:T(8,128)S(1)}, u32[]{:S(2)}, u32[]{:S(2)}) %collective-permute-start.2) | collective-permute-done | bytes 471072 | tf_op jit(solution)/shard_map/ppermute | solution.py:529
  69.2 2.6 %shard_map.109 = (f32[3,8,264,128]{3,2,1,0:T(8,128)S(1)}, f32[3,8,264,128]{3,2,1,0:T(8,128)S(1)}, f32[256,128]{1,0:T(8,128)S(1)}) custom-call(f32[8]{0:T(128)S(1)} %copy-done.2, f32[1,128]{1,0:T(1,128)S(1)} %bitcast.18, f32[8,128,128]{2,1,0:T(8,128)S(1)} %copy-done.1, f32[8,264,128]{2,1,0:T(8,128)S(1)} %get-tuple-element.21.edges, ...), custom_call_target="tpu_custom_call" | custom-call | bytes 8388608 | tf_op jit(solution)/shard_map/pallas_call | solution.py:530
  71.8 21.4 %all_to_all.23 = f32[256,1,128]{2,1,0:T(1,128)S(1)} all-to-all(f32[256,1,128]{2,1,0:T(1,128)S(1)} %bitcast.15), channel_id=1, replica_groups=mesh['lon_0'=4,'lon_1'=4,'lat_0'=8,'lat_1'=2] {'lon_0','lon_1','lat_0','..., dimensions={0} | all-to-all | bytes 262144 | tf_op jit(solution)/shard_map/all_to_all | solution.py:535
  93.1 1.7 %shard_map.110 = (f32[2048,128]{1,0:T(8,128)}, f32[2048,128]{1,0:T(8,128)}) custom-call(f32[256,128]{1,0:T(8,128)S(1)} %bitcast.14, f32[8,264,128]{2,1,0:T(8,128)S(1)} %get-tuple-element.21.edges, f32[2,264,128]{2,1,0:T(8,128)S(1)} %get-tuple-element.30.middle, f32[16,264,128]{2,1,0:T(8,128)S(1)} %get-tuple-element.22.early, ...), custom_call_target="tpu_custom_call" | custom-call | bytes 8388608 | tf_op jit(solution)/shard_map/pallas_call | solution.py:536
  (9 shorter events, 0.0 us)
Async XLA Ops:
  0.6 1.2 %copy-start = (f32[256,8,128]{2,1,0:T(8,128)S(1)}, f32[256,8,128]{2,1,0:T(8,128)}, u32[]{:S(2)}) copy-start(f32[256,8,128]{2,1,0:T(8,128)} %param.8) | copy-start | bytes 3145732
  2.0 9.2 %collective-permute-start = (f32[512,128]{1,0:T(8,128)S(1)}, f32[512,128]{1,0:T(8,128)S(1)}, u32[]{:S(2)}, u32[]{:S(2)}) collective-permute-start(f32[512,128]{1,0:T(8,128)S(1)} %get-tuple-element.19), channel_id=1, source_target_pairs={{0,15},{1,2},{2,1},{3,4},{4,3},{5,6},{6,5},{7,8},{8,7},{9,10},{10,... | collective-permute-start | bytes 786440 | tf_op jit(solution)/shard_map/ppermute | solution.py:487
  5.1 6.1 %collective-permute-start.1 = (f32[512,128]{1,0:T(8,128)S(1)}, f32[512,128]{1,0:T(8,128)S(1)}, u32[]{:S(2)}, u32[]{:S(2)}) collective-permute-start(f32[512,128]{1,0:T(8,128)S(1)} %get-tuple-element.20), channel_id=1, source_target_pairs={{0,1},{1,0},{2,3},{3,2},{4,5},{5,4},{6,7},{7,6},{8,9},{9,8},{10,11... | collective-permute-start | bytes 786440 | tf_op jit(solution)/shard_map/ppermute | solution.py:486
  11.1 22.6 %copy-start.4 = (s32[8]{0:T(128)S(1)}, s32[8]{0:T(128)}, u32[]{:S(2)}) copy-start(s32[8]{0:T(128)} %offsets.1) | copy-start | bytes 100
  11.1 22.6 %copy-start.5 = (f32[8]{0:T(128)S(1)}, f32[8]{0:T(128)}, u32[]{:S(2)}) copy-start(f32[8]{0:T(128)} %frac_lon.1) | copy-start | bytes 100
  12.0 41.1 %copy-start.1 = (f32[8,128,128]{2,1,0:T(8,128)S(1)}, f32[8,128,128]{2,1,0:T(8,128)}, u32[]{:S(2)}) copy-start(f32[8,128,128]{2,1,0:T(8,128)} %inverses.5) | copy-start | bytes 1572868
  12.0 41.1 %copy-start.2 = (f32[8]{0:T(128)S(1)}, f32[8]{0:T(128)}, u32[]{:S(2)}) copy-start(f32[8]{0:T(128)} %metric.5) | copy-start | bytes 100
  12.0 41.1 %copy-start.3 = (f32[128]{0:T(128)S(1)}, f32[128]{0:T(128)}, u32[]{:S(2)}) copy-start(f32[128]{0:T(128)} %param.14) | copy-start | bytes 1540
  54.6 13.1 %collective-permute-start.3 = (f32[920,128]{1,0:T(8,128)S(1)}, f32[920,128]{1,0:T(8,128)S(1)}, u32[]{:S(2)}, u32[]{:S(2)}) collective-permute-start(f32[920,128]{1,0:T(8,128)S(1)} %get-tuple-element.25), channel_id=1, source_target_pairs={{0,15},{1,2},{2,1},{3,4},{4,3},{5,6},{6,5},{7,8},{8,7},{9,10},{10,... | collective-permute-start | bytes 1413128 | tf_op jit(solution)/shard_map/ppermute | solution.py:521
  63.5 5.6 %collective-permute-start.2 = (f32[920,128]{1,0:T(8,128)S(1)}, f32[920,128]{1,0:T(8,128)S(1)}, u32[]{:S(2)}, u32[]{:S(2)}) collective-permute-start(f32[920,128]{1,0:T(8,128)S(1)} %get-tuple-element.24), channel_id=1, source_target_pairs={{0,1},{1,0},{2,3},{3,2},{4,5},{5,4},{6,7},{7,6},{8,9},{9,8},{10,11... | collective-permute-start | bytes 1413128 | tf_op jit(solution)/shard_map/ppermute | solution.py:529

commit v6 on v5

--- a/solution.py
+++ b/solution.py
@@ -170,17 +170,13 @@
     out[:, 2 * R] = rims
 
 
-def edge(j):
-    return j < H or j >= R - H
-
-
 def turned_row(cells, rim, j, ref, at):
     sub = lax.broadcasted_iota(jnp.int32, (8, L), 0)
     for h in range(2):
         ref[at, h * 128 : (h + 1) * 128, :] = cells[:, h * R + j].reshape(L, 128).T
-    before = (8 * j - 8) % 128
-    tail = jnp.where(sub < 4, rim[8 * j : 8 * j + 8], rim[before : before + 8])
-    ref[at, W:E, :] = tail
+    here = pl.multiple_of(8 * j, 8)
+    before = pl.multiple_of(jnp.bitwise_and(8 * j + 120, 127), 8)
+    ref[at, W:E, :] = jnp.where(sub < 4, rim[pl.ds(here, 8), :], rim[pl.ds(before, 8), :])
 
 
 def vertical_rows(vertical):
@@ -219,48 +215,49 @@
     return jnp.full((1, L), metric[j], jnp.float32)
 
 
-Q1 = {0: 0, 1: 1, 2: 2, 5: 3, 6: 4, 7: 5}
-V1_PART = {0: 6, 7: 7}
-V1 = {1: 8, 6: 9}
-Q2_PART = {0: 10, 7: 11}
-Q2 = {1: 12, 6: 13}
-V2_PART = {0: 14, 7: 15}
-EARLY = 16
+Q1 = {0: 0, 1: 1, 2: 2, 7: 8, 6: 9, 5: 10}
+V1_PART = {0: 3, 7: 11}
+V1 = {1: 4, 6: 12}
+Q2_PART = {0: 5, 7: 13}
+Q2 = {1: 6, 6: 14}
+V2_PART = {0: 7, 7: 15}
+EARLY = 8
 ENDS = ((0, 1, 2, 3), (7, 6, 5, 4))
 
 
-def turn_kernel(metric, vertical, inverses, cells, ring, cross, early):
-    even, end = is_even(), at_end()
-    rows = vertical_rows(vertical)
-    rim = cells[:, 2 * R].reshape(L, 128).T
-    for j in range(R):
-        if edge(j):
-            turned_row(cells, rim, j, ring, j)
-            early[Q1[j]] = precondition(inverses[j], ring[j])
-    for e, i, i2, _ in ENDS:
-        early[V1_PART[e]] = alone(early[Q1[e]], metric_row(metric, e), rows) - early[Q1[i]]
-        early[V1[i]] = operate(
-            early[Q1[i]], early[Q1[e]], early[Q1[i2]], metric_row(metric, i), rows
-        )
-    for e, i, _, _ in ENDS:
-        early[Q2_PART[e]] = precondition(inverses[e], early[V1_PART[e]])
-        early[Q2[i]] = precondition(inverses[i], early[V1[i]])
-    for e, i, _, _ in ENDS:
-        early[V2_PART[e]] = (
-            alone(early[Q2_PART[e]], metric_row(metric, e), rows) - early[Q2[i]]
-        )
-    for base, size, high, low in sent_rows(metric, inverses, early):
-        cross[base : base + size] = jnp.where(end, 0.0, jnp.where(even, low, high))
-
-
-def sent_rows(metric, inverses, early):
-    sent = [
-        (k * E, E, early[place[7]], early[place[0]])
-        for k, place in enumerate((Q1, Q2_PART, V2_PART))
-    ]
-    sent.append((T, L, inverses[7], inverses[0]))
-    sent.append((W + 3, 1, metric_row(metric, 7), metric_row(metric, 0)))
-    return sent
+def row_at(end, k):
+    return jnp.where(end == 0, k, R - 1 - k)
+
+
+def solve_end(end, metric, rows, inverses, cells, rim, ring, at, early, base):
+    j = [row_at(end, k) for k in range(H)]
+    for k in range(H):
+        turned_row(cells, rim, j[k], ring, at(k))
+        early[base + k] = precondition(inverses[j[k]], ring[at(k)])
+    m0, m1 = metric_row(metric, j[0]), metric_row(metric, j[1])
+    early[base + 3] = alone(early[base], m0, rows) - early[base + 1]
+    early[base + 4] = operate(early[base + 1], early[base], early[base + 2], m1, rows)
+    early[base + 5] = precondition(inverses[j[0]], early[base + 3])
+    early[base + 6] = precondition(inverses[j[1]], early[base + 4])
+    early[base + 7] = alone(early[base + 5], m0, rows) - early[base + 6]
+
+
+def fill(out, end, metric, inverses, early, base, blank=None):
+    j = row_at(end, 0)
+    sent = [(n * E, E, early[base + k]) for n, k in enumerate((0, 5, 7))]
+    sent += [(T, L, inverses[j]), (W + 3, 1, metric_row(metric, j))]
+    for start, size, value in sent:
+        value = value if blank is None else jnp.where(blank, 0.0, value)
+        out[start : start + size] = value
+
+
+def turn_kernel(metric, vertical, inverses, cells, ring, cross, early, rim):
+    rim[...] = cells[:, 2 * R].reshape(L, 128).T
+    end = jnp.where(is_even(), 0, 1)
+    solve_end(
+        end, metric, vertical_rows(vertical), inverses, cells, rim, ring, lambda k: k, early, 0
+    )
+    fill(cross, end, metric, inverses, early, 0, at_end())
 
 
 def partial(a, b):
@@ -300,19 +297,25 @@
 
 
 def inner_kernel(
-    metric, vertical, inverses, cells, edges, early,
-    search, field, totals, middle, advected, pair, ring,
+    metric, vertical, inverses, cells, turned, begun,
+    search, field, totals, ring, early, advected, pair, rim,
 ):
-    for base, size, high, low in sent_rows(metric, inverses, early):
-        pair[base : base + size] = jnp.where(is_even(), high, low)
     rows = vertical_rows(vertical)
-    rim = cells[:, 2 * R].reshape(L, 128).T
+    rim[...] = cells[:, 2 * R].reshape(L, 128).T
+    across = jnp.where(is_even(), 0, 1)
+    for k in range(H):
+        ring[row_at(across, k)] = turned[k]
+    for k in range(EARLY):
+        early[EARLY * across + k] = begun[k]
+    end = 1 - across
+    solve_end(
+        end, metric, rows, inverses, cells, rim, ring,
+        lambda k: row_at(end, k), early, EARLY * end,
+    )
+    fill(pair, end, metric, inverses, early, EARLY * end)
+    for j in range(H, R - H):
+        turned_row(cells, rim, j, ring, j)
     for j in range(R):
-        if edge(j):
-            ring[j] = edges[j]
-        else:
-            turned_row(cells, rim, j, ring, j)
-            middle[j - H] = ring[j]
         advected[row_of(j), :] = ring[j, :W]
     sums = [jnp.zeros((8, L), jnp.float32) for _ in range(9)]
 
@@ -400,7 +403,7 @@
 
 
 def finish_kernel(
-    sums, edges, middle, early, search, field, new_search, new_field, pressure, residual,
+    sums, edges, early, search, field, new_search, new_field, pressure, residual,
     held, left, sems,
 ):
     lane = lax.broadcasted_iota(jnp.int32, (1, L), 1)
@@ -440,7 +443,7 @@
             ]
             to = pl.ds(part * size * R + j, size, stride=R)
             held[to, :] = k1 * q[0] + k2 * q[1] + k3 * q[2]
-            first = edges[j, span] if edge(j) else middle[j - H, span]
+            first = edges[j, span]
             left[to, :] = first - k1 * v[0] - k2 * v[1] - k3 * v[2]
         block = pl.ds(part * size * R, size * R)
         for i, (source, target) in enumerate(((held, pressure), (left, residual))):
@@ -513,19 +516,20 @@
     )(offsets, frac_lon, lines.reshape(B, R, 8, 128))
     back = lax.all_to_all(moved, LON, 0, 0, tiled=True)
     vertical = vertical_coef.reshape(1, L)
-    edges, cross_out, early = call(
+    some, cross_out, begun = call(
         turn_kernel,
         (SMEM, VMEM, VMEM, VMEM),
-        ((R, E, L), (T + L, L), (EARLY, E, L)),
+        ((H, E, L), (T + L, L), (EARLY, E, L)),
+        scratch=((128, L),),
     )(metric, vertical, inverses, back)
     cross = lax.ppermute(cross_out, LAT, across)
-    search, images, totals, middle, advected, pair_out = call(
+    search, images, totals, edges, early, advected, pair_out = call(
         inner_kernel,
         (SMEM,) + (VMEM,) * 5,
-        ((3, R, E, L), (3, R, E, L), (9, 8, L), (R - 2 * H, E, L), (W * R, L), (T + L, L)),
-        scratch=((R, E, L),),
+        ((3, R, E, L), (3, R, E, L), (9, 8, L), (R, E, L), (2 * EARLY, E, L), (W * R, L), (T + L, L)),
+        scratch=((128, L),),
         flops=2 * 10**9,
-    )(metric, vertical, inverses, back, edges, early)
+    )(metric, vertical, inverses, back, some, begun)
     pair = lax.ppermute(pair_out, LAT, in_chip)
     new_search, new_images, sums = call(
         outer_kernel,
@@ -535,11 +539,11 @@
     gathered = lax.all_to_all(sums, LON_LAT, 0, 0, tiled=True)
     pressure, residual = call(
         finish_kernel,
-        (VMEM,) * 8,
+        (VMEM,) * 7,
         ((W * R, L), (W * R, L)),
         scratch=((W * R, L), (W * R, L), pltpu.SemaphoreType.DMA((4, 2))),
         where=(HBM, HBM),
-    )(gathered, edges, middle, early, search, images, new_search, new_images)
+    )(gathered, edges, early, search, images, new_search, new_images)
     return tuple(x.reshape(W, R, L) for x in (advected, pressure, residual))
 
 

time: 95.1 us -> 94.7 us (level)
  transfers between devices with their start and end apart: 4 -> 4, of which waited for: 1 -> 1; matrix products, arithmetic and copies ran while one was open for 1% -> 1% of each run, Pallas kernels for 5% -> 6%
where the time goes in v6:
time: 94.7 us; the launch traced here: 94.4 us
  blocking collectives  59.6 us (63%)
  starting transfers between devices  16.7 us (18%)
  Pallas kernels  13.9 us (15%)
  waiting for transfers between devices  1.47 us (2%)
  local copies, waits for them, and re-layouts  1.32 us (1%)
    all_to_all x1, blocking collectives, body(): lines = lax.all_to_all(turned, LON, 0, 0, tiled=True)  21.5 us
    all_to_all x1, blocking collectives, body(): gathered = lax.all_to_all(sums, LON_LAT, 0, 0, tiled=True)  20.6 us
    all_to_all x1, blocking collectives, body(): back = lax.all_to_all(moved, LON, 0, 0, tiled=True)  17.4 us
    ppermute x1, starting transfers between devices, body(): cross = lax.ppermute(cross_out, LAT, across)  5.67 us
    ppermute x1, starting transfers between devices, body(): pair = lax.ppermute(pair_out, LAT, in_chip)  4.18 us
    pallas_call x1, Pallas kernels, body(): call(inner_kernel, (SMEM,) + (VMEM,) * 5, ((3, R, E, L), (3, R, E, L), (9...  3.95 us
    ppermute x1, starting transfers between devices, body(): pair_in = lax.ppermute(pair_out, LAT, in_chip)  3.77 us
    ppermute x1, starting transfers between devices, body(): cross_in = lax.ppermute(cross_out, LAT, across)  3.11 us
  transfers between devices with their start and end apart: 4, of which 1 were waited for; matrix products, arithmetic and copies ran while one was open for 1% of the time, Pallas kernels for 6%

profile of v6, /device:TPU:1, one launch (start us, length us, event | category | flops | bytes accessed | tf_op | source)
XLA Modules:
  0.0 94.4 jit_solution(745058286332750490)
XLA Ops:
  0.6 1.2 %copy-done = f32[256,8,128]{2,1,0:T(8,128)S(1)} copy-done((f32[256,8,128]{2,1,0:T(8,128)S(1)}, f32[256,8,128]{2,1,0:T(8,128)}, u32[]{:S(2)}) %copy-start) | copy-done | bytes 1048600
  1.9 0.1 shard_map.103
  2.0 3.1 %collective-permute-start = (f32[512,128]{1,0:T(8,128)S(1)}, f32[512,128]{1,0:T(8,128)S(1)}, u32[]{:S(2)}, u32[]{:S(2)}) collective-permute-start(f32[512,128]{1,0:T(8,128)S(1)} %get-tuple-element.20), channel_id=1, source_target_pairs={{0,15},{1,2},{2,1},{3,4},{4,3},{5,6},{6,5},{7,8},{8,7},{9,10},{10,... | collective-permute-start | bytes 786440 | tf_op jit(solution)/shard_map/ppermute | solution.py:490
  5.1 3.8 %collective-permute-start.1 = (f32[512,128]{1,0:T(8,128)S(1)}, f32[512,128]{1,0:T(8,128)S(1)}, u32[]{:S(2)}, u32[]{:S(2)}) collective-permute-start(f32[512,128]{1,0:T(8,128)S(1)} %get-tuple-element.21), channel_id=1, source_target_pairs={{0,1},{1,0},{2,3},{3,2},{4,5},{5,4},{6,7},{7,6},{8,9},{9,8},{10,11... | collective-permute-start | bytes 786440 | tf_op jit(solution)/shard_map/ppermute | solution.py:489
  8.8 0.7 pad_maximum_fusion
  9.6 0.1 broadcast_in_dim.2.fractions
  9.7 1.4 %shard_map.104.begun = f32[16,2,8,8,128]{4,3,2,1,0:T(8,128)S(1)} custom-call(f32[16,128]{1,0:T(8,128)S(1)} %broadcast_in_dim.2.fractions, f32[2048,128]{1,0:T(8,128)S(1)} %bitcast.11), custom_call_target="tpu_custom_call" | custom-call | flops 1000000000 | bytes 8388608 | tf_op jit(solution)/shard_map/pallas_call | solution.py:494
  11.1 0.0 copy-start.4
  11.1 0.0 copy-start.5
  11.1 0.0 collective-permute-done.cross
  11.1 0.0 collective-permute-done.1.pair
  11.2 0.9 shard_map.105
  12.0 21.5 %all_to_all.21 = f32[16,2,8,8,128]{4,3,2,1,0:T(8,128)S(1)} all-to-all(f32[16,2,8,8,128]{4,3,2,1,0:T(8,128)S(1)} %shard_map.105), channel_id=1, replica_groups=mesh['lon_0'=4,'lon_1'=4,'lat_0'=8,'lat_1'=2] {'lon_0','lon_1'}, dimensions={0} | all-to-all | bytes 2097152 | tf_op jit(solution)/shard_map/all_to_all | solution.py:510
  33.6 0.0 copy-start.3
  33.6 2.0 %shard_map.106 = f32[16,17,8,128]{3,2,1,0:T(8,128)S(1)} custom-call(s32[8]{0:T(128)S(1)} %copy-done.4, f32[8]{0:T(128)S(1)} %copy-done.5, f32[32,8,8,128]{3,2,1,0:T(8,128)S(1)} %bitcast.13), custom_call_target="tpu_custom_call" | custom-call | bytes 8388608 | tf_op jit(solution)/shard_map/pallas_call | solution.py:511
  35.6 17.4 %all_to_all.22.cells = f32[16,17,8,128]{3,2,1,0:T(8,128)S(1)} all-to-all(f32[16,17,8,128]{3,2,1,0:T(8,128)S(1)} %shard_map.106), channel_id=1, replica_groups=mesh['lon_0'=4,'lon_1'=4,'lat_0'=8,'lat_1'=2] {'lon_0','lon_1'}, dimensions={0} | all-to-all | bytes 2228224 | tf_op jit(solution)/shard_map/all_to_all | solution.py:517
  53.0 1.2 %shard_map.107 = (f32[3,264,128]{2,1,0:T(8,128)S(1)}, f32[920,128]{1,0:T(8,128)S(1)}, f32[8,264,128]{2,1,0:T(8,128)S(1)}) custom-call(f32[8]{0:T(128)S(1)} %copy-done.2, f32[1,128]{1,0:T(1,128)S(1)} %bitcast.16, f32[8,128,128]{2,1,0:T(8,128)S(1)} %copy-done.1, f32[16,17,8,128]{3,2,1,0:T(8,128)S(1)} %all_to_all.22.cells), custom_call_target="tpu_custom_call" | custom-call | bytes 8388608 | tf_op jit(solution)/shard_map/pallas_call | solution.py:519
  54.2 5.7 %collective-permute-start.3 = (f32[920,128]{1,0:T(8,128)S(1)}, f32[920,128]{1,0:T(8,128)S(1)}, u32[]{:S(2)}, u32[]{:S(2)}) collective-permute-start(f32[920,128]{1,0:T(8,128)S(1)} %get-tuple-element.27), channel_id=1, source_target_pairs={{0,15},{1,2},{2,1},{3,4},{4,3},{5,6},{6,5},{7,8},{8,7},{9,10},{10,... | collective-permute-start | bytes 1413128 | tf_op jit(solution)/shard_map/ppermute | solution.py:525
  59.8 4.0 %shard_map.108 = (f32[3,8,264,128]{3,2,1,0:T(8,128)S(1)}, f32[3,8,264,128]{3,2,1,0:T(8,128)S(1)}, f32[9,8,128]{2,1,0:T(8,128)S(1)}, f32[8,264,128]{2,1,0:T(8,128...) custom-call(f32[8]{0:T(128)S(1)} %copy-done.2, f32[1,128]{1,0:T(1,128)S(1)} %bitcast.17, ...), custom_call_target="tpu_custom_call" | custom-call | flops 2000000000 | bytes 8388608 | tf_op jit(solution)/shard_map/pallas_call | solution.py:526
  63.8 4.2 %collective-permute-start.2 = (f32[920,128]{1,0:T(8,128)S(1)}, f32[920,128]{1,0:T(8,128)S(1)}, u32[]{:S(2)}, u32[]{:S(2)}) collective-permute-start(f32[920,128]{1,0:T(8,128)S(1)} %get-tuple-element.26), channel_id=1, source_target_pairs={{0,1},{1,0},{2,3},{3,2},{4,5},{5,4},{6,7},{7,6},{8,9},{9,8},{10,11... | collective-permute-start | bytes 1413128 | tf_op jit(solution)/shard_map/ppermute | solution.py:533
  68.0 1.5 %collective-permute-done.2.pair = f32[920,128]{1,0:T(8,128)S(1)} collective-permute-done((f32[920,128]{1,0:T(8,128)S(1)}, f32[920,128]{1,0:T(8,128)S(1)}, u32[]{:S(2)}, u32[]{:S(2)}) %collective-permute-start.2) | collective-permute-done | bytes 471072 | tf_op jit(solution)/shard_map/ppermute | solution.py:533
  69.4 2.6 %shard_map.109 = (f32[3,8,264,128]{3,2,1,0:T(8,128)S(1)}, f32[3,8,264,128]{3,2,1,0:T(8,128)S(1)}, f32[256,128]{1,0:T(8,128)S(1)}) custom-call(f32[8]{0:T(128)S(1)} %copy-done.2, f32[1,128]{1,0:T(1,128)S(1)} %bitcast.18, f32[8,128,128]{2,1,0:T(8,128)S(1)} %copy-done.1, f32[8,264,128]{2,1,0:T(8,128)S(1)} %get-tuple-element.25.edges, ...), custom_call_target="tpu_custom_call" | custom-call | bytes 8388608 | tf_op jit(solution)/shard_map/pallas_call | solution.py:534
  72.1 20.6 %all_to_all.23 = f32[256,1,128]{2,1,0:T(1,128)S(1)} all-to-all(f32[256,1,128]{2,1,0:T(1,128)S(1)} %bitcast.15), channel_id=1, replica_groups=mesh['lon_0'=4,'lon_1'=4,'lat_0'=8,'lat_1'=2] {'lon_0','lon_1','lat_0','..., dimensions={0} | all-to-all | bytes 262144 | tf_op jit(solution)/shard_map/all_to_all | solution.py:539
  92.7 1.7 %shard_map.110 = (f32[2048,128]{1,0:T(8,128)}, f32[2048,128]{1,0:T(8,128)}) custom-call(f32[256,128]{1,0:T(8,128)S(1)} %bitcast.14, f32[8,264,128]{2,1,0:T(8,128)S(1)} %get-tuple-element.25.edges, f32[16,264,128]{2,1,0:T(8,128)S(1)} %get-tuple-element.28.early, f32[3,8,264,128]{3,2,1,0:T(8,128)S(1)} %get-tuple-element.29.search, ...), custom_call_target="tpu_custom_call" | custom-call | bytes 8388608 | tf_op jit(solution)/shard_map/pallas_call | solution.py:540
  (9 shorter events, 0.0 us)
Async XLA Ops:
  0.6 1.2 %copy-start = (f32[256,8,128]{2,1,0:T(8,128)S(1)}, f32[256,8,128]{2,1,0:T(8,128)}, u32[]{:S(2)}) copy-start(f32[256,8,128]{2,1,0:T(8,128)} %param.8) | copy-start | bytes 3145732
  2.0 9.2 %collective-permute-start = (f32[512,128]{1,0:T(8,128)S(1)}, f32[512,128]{1,0:T(8,128)S(1)}, u32[]{:S(2)}, u32[]{:S(2)}) collective-permute-start(f32[512,128]{1,0:T(8,128)S(1)} %get-tuple-element.20), channel_id=1, source_target_pairs={{0,15},{1,2},{2,1},{3,4},{4,3},{5,6},{6,5},{7,8},{8,7},{9,10},{10,... | collective-permute-start | bytes 786440 | tf_op jit(solution)/shard_map/ppermute | solution.py:490
  5.1 6.1 %collective-permute-start.1 = (f32[512,128]{1,0:T(8,128)S(1)}, f32[512,128]{1,0:T(8,128)S(1)}, u32[]{:S(2)}, u32[]{:S(2)}) collective-permute-start(f32[512,128]{1,0:T(8,128)S(1)} %get-tuple-element.21), channel_id=1, source_target_pairs={{0,1},{1,0},{2,3},{3,2},{4,5},{5,4},{6,7},{7,6},{8,9},{9,8},{10,11... | collective-permute-start | bytes 786440 | tf_op jit(solution)/shard_map/ppermute | solution.py:489
  11.1 22.4 %copy-start.4 = (s32[8]{0:T(128)S(1)}, s32[8]{0:T(128)}, u32[]{:S(2)}) copy-start(s32[8]{0:T(128)} %offsets.1) | copy-start | bytes 100
  11.1 22.4 %copy-start.5 = (f32[8]{0:T(128)S(1)}, f32[8]{0:T(128)}, u32[]{:S(2)}) copy-start(f32[8]{0:T(128)} %frac_lon.1) | copy-start | bytes 100
  33.6 19.4 %copy-start.1 = (f32[8,128,128]{2,1,0:T(8,128)S(1)}, f32[8,128,128]{2,1,0:T(8,128)}, u32[]{:S(2)}) copy-start(f32[8,128,128]{2,1,0:T(8,128)} %inverses.5) | copy-start | bytes 1572868
  33.6 19.4 %copy-start.2 = (f32[8]{0:T(128)S(1)}, f32[8]{0:T(128)}, u32[]{:S(2)}) copy-start(f32[8]{0:T(128)} %metric.5) | copy-start | bytes 100
  33.6 19.4 %copy-start.3 = (f32[128]{0:T(128)S(1)}, f32[128]{0:T(128)}, u32[]{:S(2)}) copy-start(f32[128]{0:T(128)} %param.14) | copy-start | bytes 1540
  54.2 13.8 %collective-permute-start.3 = (f32[920,128]{1,0:T(8,128)S(1)}, f32[920,128]{1,0:T(8,128)S(1)}, u32[]{:S(2)}, u32[]{:S(2)}) collective-permute-start(f32[920,128]{1,0:T(8,128)S(1)} %get-tuple-element.27), channel_id=1, source_target_pairs={{0,15},{1,2},{2,1},{3,4},{4,3},{5,6},{6,5},{7,8},{8,7},{9,10},{10,... | collective-permute-start | bytes 1413128 | tf_op jit(solution)/shard_map/ppermute | solution.py:525
  63.8 5.6 %collective-permute-start.2 = (f32[920,128]{1,0:T(8,128)S(1)}, f32[920,128]{1,0:T(8,128)S(1)}, u32[]{:S(2)}, u32[]{:S(2)}) collective-permute-start(f32[920,128]{1,0:T(8,128)S(1)} %get-tuple-element.26), channel_id=1, source_target_pairs={{0,1},{1,0},{2,3},{3,2},{4,5},{5,4},{6,7},{7,6},{8,9},{9,8},{10,11... | collective-permute-start | bytes 1413128 | tf_op jit(solution)/shard_map/ppermute | solution.py:533

commit v7 on v6

--- a/solution.py
+++ b/solution.py
@@ -69,11 +69,10 @@
     cross[W : 2 * W] = jnp.where(end, 0.0, second)
 
 
-def mix_rows(rows, row, fractions, held, out, sems):
+def mix_rows(rows, row, fractions, out, place):
     delta = lax.broadcasted_iota(jnp.int32, (L, L), 1) - lax.broadcasted_iota(
         jnp.int32, (L, L), 0
     )
-    copies = []
     for at, j in enumerate(rows):
         w = weights(fractions[j : j + 1, :])
         mixed = w[0] * row(j - 1) + w[1] * row(j) + w[2] * row(j + 1) + w[3] * row(j + 2)
@@ -92,21 +91,15 @@
         )
         both = dot_nt(left, jnp.concatenate([m_high, m_low], 1))
         turned = (both[:L] + both[L:]).reshape(NL, 8, W)
-        held[at, :, 0] = turned[:, :, :128]
-        held[at, :, 1] = turned[:, :, 128:]
-        copies.append(
-            pltpu.make_async_copy(held.at[at], out.at[:, :, j], sems.at[at])
-        )
-        copies[-1].start()
-    for copy in copies:
-        copy.wait()
-
-
-def mix_core_kernel(fractions, tracer, out, held, sems):
-    mix_rows(CORE, lambda k: tracer[row_of(k), :], fractions, held, out, sems)
-
-
-def mix_side_kernel(fractions, tracer, cross, pair, begun, out, held, sems):
+        out[:, 0, place[at]] = turned[:, :, :128]
+        out[:, 1, place[at]] = turned[:, :, 128:]
+
+
+def mix_core_kernel(fractions, tracer, out):
+    mix_rows(CORE, lambda k: tracer[row_of(k), :], fractions, out, range(len(CORE)))
+
+
+def mix_side_kernel(fractions, tracer, cross, pair, begun, out):
     even = is_even()
 
     def row(k):
@@ -117,7 +110,9 @@
             return jnp.where(even, pair[part], cross[part])
         return tracer[row_of(k), :]
 
-    mix_rows(SIDE, row, fractions, held, out, sems)
+    for at, j in enumerate(CORE):
+        out[:, :, j] = begun[:, :, at]
+    mix_rows(SIDE, row, fractions, out, SIDE)
 
 
 def shift_kernel(offsets, frac_lon, cells, out, twice):
@@ -216,13 +211,9 @@
 
 
 Q1 = {0: 0, 1: 1, 2: 2, 7: 8, 6: 9, 5: 10}
-V1_PART = {0: 3, 7: 11}
 V1 = {1: 4, 6: 12}
-Q2_PART = {0: 5, 7: 13}
 Q2 = {1: 6, 6: 14}
-V2_PART = {0: 7, 7: 15}
 EARLY = 8
-ENDS = ((0, 1, 2, 3), (7, 6, 5, 4))
 
 
 def row_at(end, k):
@@ -251,13 +242,15 @@
         out[start : start + size] = value
 
 
-def turn_kernel(metric, vertical, inverses, cells, ring, cross, early, rim):
+def turn_kernel(metric, vertical, inverses, cells, ring, cross, pair, early, rim):
     rim[...] = cells[:, 2 * R].reshape(L, 128).T
-    end = jnp.where(is_even(), 0, 1)
-    solve_end(
-        end, metric, vertical_rows(vertical), inverses, cells, rim, ring, lambda k: k, early, 0
-    )
-    fill(cross, end, metric, inverses, early, 0, at_end())
+    rows = vertical_rows(vertical)
+    for end, out, blank in ((across_end(), cross, at_end()), (1 - across_end(), pair, None)):
+        solve_end(
+            end, metric, rows, inverses, cells, rim, ring,
+            lambda k, end=end: row_at(end, k), early, EARLY * end,
+        )
+        fill(out, end, metric, inverses, early, EARLY * end, blank)
 
 
 def partial(a, b):
@@ -277,19 +270,14 @@
     sums[k] = sums[k] + partial(result, result)
 
 
-def direction_of(search, new_search, early, depth, j):
-    if depth == 0:
-        return (early, Q1[j]) if j in Q1 else (search, 0, j)
-    if 2 <= j <= 5:
-        return (search, depth, j)
-    return (early, Q2[j]) if depth == 1 and j in Q2 else (new_search, depth, j)
-
-
-def image_of(field, new_field, early, depth, j):
-    if depth == 0 and j in V1:
-        return (early, V1[j])
-    inner = 3 <= j <= 4 if depth == 2 else 2 <= j <= 5
-    return (field if inner else new_field, depth, j)
+def direction_of(search, early, depth, j):
+    if depth == 0 and j in Q1:
+        return (early, Q1[j])
+    return (early, Q2[j]) if depth == 1 and j in Q2 else (search, depth, j)
+
+
+def image_of(field, early, depth, j):
+    return (early, V1[j]) if depth == 0 and j in V1 else (field, depth, j)
 
 
 def read(place, *more):
@@ -297,33 +285,23 @@
 
 
 def inner_kernel(
-    metric, vertical, inverses, cells, turned, begun,
-    search, field, totals, ring, early, advected, pair, rim,
+    metric, vertical, inverses, cells, turned, early, search, field, totals, ring, advected, rim
 ):
     rows = vertical_rows(vertical)
     rim[...] = cells[:, 2 * R].reshape(L, 128).T
-    across = jnp.where(is_even(), 0, 1)
-    for k in range(H):
-        ring[row_at(across, k)] = turned[k]
-    for k in range(EARLY):
-        early[EARLY * across + k] = begun[k]
-    end = 1 - across
-    solve_end(
-        end, metric, rows, inverses, cells, rim, ring,
-        lambda k: row_at(end, k), early, EARLY * end,
-    )
-    fill(pair, end, metric, inverses, early, EARLY * end)
-    for j in range(H, R - H):
-        turned_row(cells, rim, j, ring, j)
     for j in range(R):
+        if H <= j < R - H:
+            turned_row(cells, rim, j, ring, j)
+        else:
+            ring[j] = turned[j]
         advected[row_of(j), :] = ring[j, :W]
     sums = [jnp.zeros((8, L), jnp.float32) for _ in range(9)]
 
     def q(depth, j):
-        return read(direction_of(search, None, early, depth, j))
+        return read(direction_of(search, early, depth, j))
 
     def v(depth, j):
-        return read(image_of(field, None, early, depth, j))
+        return read(image_of(field, early, depth, j))
 
     for depth, solved, applied in ((0, (3, 4), range(2, 6)), (1, range(2, 6), range(2, 6)), (2, range(2, 6), (3, 4))):
         for j in solved:
@@ -340,61 +318,57 @@
         totals[k] = sums[k]
 
 
-def outer_kernel(
-    metric, vertical, inverses, edges, pair, cross, early, search, field, totals,
-    new_search, new_field, sums_out,
+def across_end():
+    return jnp.where(is_even(), 0, 1)
+
+
+def end_sums(end, metric, vertical, inverses, halo, edges, early, search, field, totals, new_q, new_v):
+    rows = vertical_rows(vertical)
+    base = EARLY * end
+    e, i, i2, i3 = (row_at(end, k) for k in range(4))
+    m0, m1, m2 = (metric_row(metric, j) for j in (e, i, i2))
+    sums = [totals[k] for k in range(9)]
+    inverse = halo[T : T + L]
+    extra = precondition(inverse, early[base])
+    new_v[0] = early[base + 3] - halo[0:E]
+    tally(sums, 0, edges[e], (), new_v[0])
+    new_q[0] = precondition(inverses[e], new_v[0])
+    new_v[1] = operate(new_q[0], early[base + 6], halo[E : 2 * E] - extra, m0, rows)
+    tally(sums, 1, edges[e], (new_v[0],), new_v[1])
+    new_v[2] = operate(early[base + 6], new_q[0], search[1, i2], m1, rows)
+    tally(sums, 1, edges[i], (early[base + 4],), new_v[2])
+    outside = halo[2 * E : 3 * E] - alone(extra, halo[W + 3 : W + 4], rows) - new_q[0]
+    outside = precondition(inverse, outside)
+    new_q[1] = precondition(inverses[e], new_v[1])
+    new_q[2] = precondition(inverses[i], new_v[2])
+    new_v[3] = operate(new_q[1], new_q[2], outside, m0, rows)
+    tally(sums, 2, edges[e], (new_v[0], new_v[1]), new_v[3])
+    new_v[4] = operate(new_q[2], new_q[1], search[2, i2], m1, rows)
+    tally(sums, 2, edges[i], (early[base + 4], new_v[2]), new_v[4])
+    new_v[5] = operate(search[2, i2], new_q[2], search[2, i3], m2, rows)
+    tally(sums, 2, edges[i2], (field[0, i2], field[1, i2]), new_v[5])
+    return sums
+
+
+def chip_end_kernel(
+    metric, vertical, inverses, halo, edges, early, search, field, totals, new_q, new_v, more
 ):
-    even = is_even()
+    sums = end_sums(
+        1 - across_end(), metric, vertical, inverses, halo, edges, early, search, field,
+        totals, new_q, new_v,
+    )
+    for k in range(9):
+        more[k] = sums[k]
+
+
+def far_end_kernel(
+    metric, vertical, inverses, halo, edges, early, search, field, totals, new_q, new_v, sums_out
+):
     lane = lax.broadcasted_iota(jnp.int32, (1, L), 1)
-    rows = vertical_rows(vertical)
-    sums = [totals[k] for k in range(9)]
-
-    def beyond(e, base, size):
-        part = slice(base, base + size)
-        first, second = (cross, pair) if e == 0 else (pair, cross)
-        return jnp.where(even, first[part], second[part])
-
-    def q(depth, j):
-        return read(direction_of(search, new_search, early, depth, j))
-
-    def v(depth, j):
-        return read(image_of(field, new_field, early, depth, j))
-
-    def add(depth, j):
-        tally(sums, depth, edges[j], [v(o, j) for o in range(depth)], v(depth, j))
-
-    def apply(depth, j, south_or_north, other):
-        new_field[depth, j] = operate(
-            q(depth, j), south_or_north, other, metric_row(metric, j), rows
-        )
-        add(depth, j)
-
-    outside = []
-    for e, _, _, _ in ENDS:
-        outside.append(
-            (
-                beyond(e, T, L),
-                beyond(e, W + 3, 1),
-                precondition(beyond(e, T, L), early[Q1[e]]),
-            )
-        )
-        new_field[0, e] = early[V1_PART[e]] - beyond(e, 0, E)
-        add(0, e)
-    for e, _, _, _ in ENDS:
-        new_search[1, e] = precondition(inverses[e], new_field[0, e])
-    last = []
-    for (e, i, i2, _), (inverse, m, extra) in zip(ENDS, outside):
-        apply(1, e, q(1, i), beyond(e, E, E) - extra)
-        apply(1, i, q(1, e), q(1, i2))
-        image = beyond(e, 2 * E, E) - alone(extra, m, rows) - q(1, e)
-        last.append(precondition(inverse, image))
-    for e, i, _, _ in ENDS:
-        new_search[2, e] = precondition(inverses[e], new_field[1, e])
-        new_search[2, i] = precondition(inverses[i], new_field[1, i])
-    for (e, i, i2, i3), far in zip(ENDS, last):
-        apply(2, e, q(2, i), far)
-        apply(2, i, q(2, e), q(2, i2))
-        apply(2, i2, q(2, i), q(2, i3))
+    sums = end_sums(
+        across_end(), metric, vertical, inverses, halo, edges, early, search, field,
+        totals, new_q, new_v,
+    )
     row = jnp.zeros((1, L), jnp.float32)
     for k in range(9):
         total = jnp.sum(jnp.sum(sums[k], 0, keepdims=True), 1, keepdims=True)
@@ -403,7 +377,7 @@
 
 
 def finish_kernel(
-    sums, edges, early, search, field, new_search, new_field, pressure, residual,
+    sums, edges, early, search, field, chip_q, chip_v, far_q, far_v, pressure, residual,
     held, left, sems,
 ):
     lane = lax.broadcasted_iota(jnp.int32, (1, L), 1)
@@ -427,24 +401,43 @@
     k3 = y3
     k2 = y2 - l32 * k3
     k1 = y1 - l21 * k2 - l31 * k3
-    parts = 4
+    parts = 8
     size = W // parts
     copies = []
     for part in range(parts):
         span = slice(part * size, (part + 1) * size)
-        for j in range(R):
-            q = [
-                read(direction_of(search, new_search, early, depth, j), span)
-                for depth in range(3)
-            ]
-            v = [
-                read(image_of(field, new_field, early, depth, j), span)
-                for depth in range(3)
-            ]
+        work = [
+            (
+                j,
+                ((search, 0, j), (search, 1, j), (search, 2, j)),
+                ((field, 0, j), (field, 1, j), (field, 2, j)),
+            )
+            for j in range(H, R - H)
+        ]
+        for end, new_q, new_v in (
+            (across_end(), far_q, far_v),
+            (1 - across_end(), chip_q, chip_v),
+        ):
+            base = EARLY * end
+            for n in range(H):
+                j = row_at(end, n)
+                q = (
+                    (early, base + n),
+                    ((new_q, 0), (early, base + 6), (search, 1, j))[n],
+                    ((new_q, 1), (new_q, 2), (search, 2, j))[n],
+                )
+                v = (
+                    ((new_v, 0), (early, base + 4), (field, 0, j))[n],
+                    ((new_v, 1), (new_v, 2), (field, 1, j))[n],
+                    (new_v, 3 + n),
+                )
+                work.append((j, q, v))
+        for j, places_q, places_v in work:
+            q = [read(place, span) for place in places_q]
+            v = [read(place, span) for place in places_v]
             to = pl.ds(part * size * R + j, size, stride=R)
             held[to, :] = k1 * q[0] + k2 * q[1] + k3 * q[2]
-            first = edges[j, span]
-            left[to, :] = first - k1 * v[0] - k2 * v[1] - k3 * v[2]
+            left[to, :] = edges[j, span] - k1 * v[0] - k2 * v[1] - k3 * v[2]
         block = pl.ds(part * size * R, size * R)
         for i, (source, target) in enumerate(((held, pressure), (left, residual))):
             copy = pltpu.make_async_copy(
@@ -463,7 +456,7 @@
 
 
 def call(
-    kernel, ins, outs, scratch=(), limit=32, flops=0, where=(), aliases=None, dtype=jnp.float32
+    kernel, ins, outs, scratch=(), limit=32, flops=0, size=8 * MIB, where=(), aliases=None, dtype=jnp.float32
 ):
     return pl.pallas_call(
         kernel,
@@ -476,7 +469,7 @@
         input_output_aliases=aliases or {},
         compiler_params=pltpu.CompilerParams(vmem_limit_bytes=limit * MIB),
         cost_estimate=pl.CostEstimate(
-            flops=flops, bytes_accessed=8 * MIB, transcendentals=0
+            flops=flops, bytes_accessed=size, transcendentals=0
         ),
     )
 
@@ -492,21 +485,11 @@
         jnp.concatenate([frac_lat, frac_lev])[:, None], (2 * R, L)
     )
     (begun,) = call(
-        mix_core_kernel,
-        (VMEM,) * 2,
-        ((NL, 2, R, 8, 128),),
-        scratch=((5, NL, 2, 8, 128), pltpu.SemaphoreType.DMA((5,))),
-        where=(ANY,),
-        flops=10**9,
+        mix_core_kernel, (VMEM,) * 2, ((NL, 2, len(CORE), 8, 128),), flops=10**9
     )(fractions, flat)
-    (turned,) = call(
-        mix_side_kernel,
-        (VMEM,) * 4 + (ANY,),
-        ((NL, 2, R, 8, 128),),
-        scratch=((3, NL, 2, 8, 128), pltpu.SemaphoreType.DMA((3,))),
-        where=(ANY,),
-        aliases={4: 0},
-    )(fractions, flat, cross_in, pair_in, begun)
+    (turned,) = call(mix_side_kernel, (VMEM,) * 5, ((NL, 2, R, 8, 128),))(
+        fractions, flat, cross_in, pair_in, begun
+    )
     lines = lax.all_to_all(turned, LON, 0, 0, tiled=True)
     (moved,) = call(
         shift_kernel,
@@ -516,34 +499,38 @@
     )(offsets, frac_lon, lines.reshape(B, R, 8, 128))
     back = lax.all_to_all(moved, LON, 0, 0, tiled=True)
     vertical = vertical_coef.reshape(1, L)
-    some, cross_out, begun = call(
+    some, cross_out, pair_out, early = call(
         turn_kernel,
         (SMEM, VMEM, VMEM, VMEM),
-        ((H, E, L), (T + L, L), (EARLY, E, L)),
+        ((R, E, L), (T + L, L), (T + L, L), (2 * EARLY, E, L)),
         scratch=((128, L),),
     )(metric, vertical, inverses, back)
     cross = lax.ppermute(cross_out, LAT, across)
-    search, images, totals, edges, early, advected, pair_out = call(
+    pair = lax.ppermute(pair_out, LAT, in_chip)
+    search, images, totals, edges, advected = call(
         inner_kernel,
         (SMEM,) + (VMEM,) * 5,
-        ((3, R, E, L), (3, R, E, L), (9, 8, L), (R, E, L), (2 * EARLY, E, L), (W * R, L), (T + L, L)),
+        ((3, R, E, L), (3, R, E, L), (9, 8, L), (R, E, L), (W * R, L)),
         scratch=((128, L),),
-        flops=2 * 10**9,
-    )(metric, vertical, inverses, back, some, begun)
-    pair = lax.ppermute(pair_out, LAT, in_chip)
-    new_search, new_images, sums = call(
-        outer_kernel,
-        (SMEM,) + (VMEM,) * 9,
-        ((3, R, E, L), (3, R, E, L), (count * NL, L)),
-    )(metric, vertical, inverses, edges, pair, cross, early, search, images, totals)
+        flops=10**10,
+    )(metric, vertical, inverses, back, some, early)
+    shared = (metric, vertical, inverses)
+    known = (edges, early, search, images)
+    specs = (SMEM,) + (VMEM,) * 8
+    chip_q, chip_v, totals = call(
+        chip_end_kernel, specs, ((3, E, L), (6, E, L), (9, 8, L)), size=4096
+    )(*shared, pair, *known, totals)
+    far_q, far_v, sums = call(
+        far_end_kernel, specs, ((3, E, L), (6, E, L), (count * NL, L))
+    )(*shared, cross, *known, totals)
     gathered = lax.all_to_all(sums, LON_LAT, 0, 0, tiled=True)
     pressure, residual = call(
         finish_kernel,
-        (VMEM,) * 7,
+        (VMEM,) * 9,
         ((W * R, L), (W * R, L)),
-        scratch=((W * R, L), (W * R, L), pltpu.SemaphoreType.DMA((4, 2))),
+        scratch=((W * R, L), (W * R, L), pltpu.SemaphoreType.DMA((8, 2))),
         where=(HBM, HBM),
-    )(gathered, edges, early, search, images, new_search, new_images)
+    )(gathered, *known, chip_q, chip_v, far_q, far_v)
     return tuple(x.reshape(W, R, L) for x in (advected, pressure, residual))
 
 

time: 94.7 us -> 94 us (level)
  starting transfers between devices: 16.7 us -> 19.2 us
  waiting for transfers between devices: 1.47 us -> 0.01 us
  Pallas kernels: 13.9 us -> 12.8 us
    ppermute x1, starting transfers between devices: 5.67 us -> 8.15 us  [body(): cross = lax.ppermute(cross_out, LAT, across)]
    all_to_all x1, blocking collectives: 21.5 us -> 19.7 us  [body(): lines = lax.all_to_all(turned, LON, 0, 0, tiled=True)]
    ppermute x1, waiting for transfers between devices: 1.46 us -> 0.01 us  [body(): pair = lax.ppermute(pair_out, LAT, in_chip)]
    pallas_call x5 -> x6, Pallas kernels: 7.83 us -> 7.55 us  [the longest x1 1.78 us: body(): call(turn_kernel, (SMEM, VMEM, VMEM, VMEM), ((R, E, L), (T + L, L), (T +...]
  transfers between devices with their start and end apart: 4 -> 4, of which waited for: 1 -> 0; matrix products, arithmetic and copies ran while one was open for 1% -> 1% of each run, Pallas kernels for 6% -> 6%
where the time goes in v7:
time: 94 us; the launch traced here: 93.8 us
  blocking collectives  58.9 us (63%)
  starting transfers between devices  19.2 us (20%)
  Pallas kernels  12.8 us (14%)
  local copies, waits for them, and re-layouts  1.32 us (1%)
    all_to_all x1, blocking collectives, body(): gathered = lax.all_to_all(sums, LON_LAT, 0, 0, tiled=True)  21.4 us
    all_to_all x1, blocking collectives, body(): lines = lax.all_to_all(turned, LON, 0, 0, tiled=True)  19.7 us
    all_to_all x1, blocking collectives, body(): back = lax.all_to_all(moved, LON, 0, 0, tiled=True)  17.8 us
    ppermute x1, starting transfers between devices, body(): cross = lax.ppermute(cross_out, LAT, across)  8.15 us
    ppermute x1, starting transfers between devices, body(): pair = lax.ppermute(pair_out, LAT, in_chip)  4.19 us
    ppermute x1, starting transfers between devices, body(): pair_in = lax.ppermute(pair_out, LAT, in_chip)  3.77 us
    pallas_call x1, Pallas kernels, body(): call(inner_kernel, (SMEM,) + (VMEM,) * 5, ((3, R, E, L), (3, R, E, L), (9...  3.17 us
    ppermute x1, starting transfers between devices, body(): cross_in = lax.ppermute(cross_out, LAT, across)  3.11 us
  transfers between devices with their start and end apart: 4, of which 0 were waited for; matrix products, arithmetic and copies ran while one was open for 1% of the time, Pallas kernels for 6%

profile of v7, /device:TPU:1, one launch (start us, length us, event | category | flops | bytes accessed | tf_op | source)
XLA Modules:
  0.0 93.8 jit_solution(15152838850988081061)
XLA Ops:
  0.6 1.2 %copy-done.1 = f32[256,8,128]{2,1,0:T(8,128)S(1)} copy-done((f32[256,8,128]{2,1,0:T(8,128)S(1)}, f32[256,8,128]{2,1,0:T(8,128)}, u32[]{:S(2)}) %copy-start.1) | copy-done | bytes 1048600
  1.9 0.1 shard_map.103
  2.0 3.1 %collective-permute-start = (f32[512,128]{1,0:T(8,128)S(1)}, f32[512,128]{1,0:T(8,128)S(1)}, u32[]{:S(2)}, u32[]{:S(2)}) collective-permute-start(f32[512,128]{1,0:T(8,128)S(1)} %get-tuple-element.22), channel_id=1, source_target_pairs={{0,15},{1,2},{2,1},{3,4},{4,3},{5,6},{6,5},{7,8},{8,7},{9,10},{10,... | collective-permute-start | bytes 786440 | tf_op jit(solution)/shard_map/ppermute | solution.py:483
  5.1 3.8 %collective-permute-start.1 = (f32[512,128]{1,0:T(8,128)S(1)}, f32[512,128]{1,0:T(8,128)S(1)}, u32[]{:S(2)}, u32[]{:S(2)}) collective-permute-start(f32[512,128]{1,0:T(8,128)S(1)} %get-tuple-element.23), channel_id=1, source_target_pairs={{0,1},{1,0},{2,3},{3,2},{4,5},{5,4},{6,7},{7,6},{8,9},{9,8},{10,11... | collective-permute-start | bytes 786440 | tf_op jit(solution)/shard_map/ppermute | solution.py:482
  8.8 0.7 pad_maximum_fusion
  9.6 0.1 broadcast_in_dim.2.fractions
  9.7 0.6 shard_map.104.begun
  10.2 0.5 shard_map.105
  10.8 0.0 copy-start.4
  10.8 0.0 copy-start.5
  10.8 19.7 %all_to_all.21 = f32[16,2,8,8,128]{4,3,2,1,0:T(8,128)S(1)} all-to-all(f32[16,2,8,8,128]{4,3,2,1,0:T(8,128)S(1)} %shard_map.105), channel_id=1, replica_groups=mesh['lon_0'=4,'lon_1'=4,'lat_0'=8,'lat_1'=2] {'lon_0','lon_1'}, dimensions={0} | all-to-all | bytes 2097152 | tf_op jit(solution)/shard_map/all_to_all | solution.py:493
  30.5 2.0 %shard_map.106 = f32[16,17,8,128]{3,2,1,0:T(8,128)S(1)} custom-call(s32[8]{0:T(128)S(1)} %copy-done.4, f32[8]{0:T(128)S(1)} %copy-done.5, f32[32,8,8,128]{3,2,1,0:T(8,128)S(1)} %bitcast.13), custom_call_target="tpu_custom_call" | custom-call | bytes 8388608 | tf_op jit(solution)/shard_map/pallas_call | solution.py:494
  32.5 0.0 copy-start
  32.5 0.0 copy-start.2
  32.5 0.0 copy-start.3
  32.5 17.8 %all_to_all.22.cells = f32[16,17,8,128]{3,2,1,0:T(8,128)S(1)} all-to-all(f32[16,17,8,128]{3,2,1,0:T(8,128)S(1)} %shard_map.106), channel_id=1, replica_groups=mesh['lon_0'=4,'lon_1'=4,'lat_0'=8,'lat_1'=2] {'lon_0','lon_1'}, dimensions={0} | all-to-all | bytes 2228224 | tf_op jit(solution)/shard_map/all_to_all | solution.py:500
  50.3 1.8 %shard_map.107 = (f32[8,264,128]{2,1,0:T(8,128)S(1)}, f32[920,128]{1,0:T(8,128)S(1)}, f32[920,128]{1,0:T(8,128)S(1)}, f32[16,264,128]{2,1,0:T(8,128)S(1)}) custom-call(f32[8]{0:T(128)S(1)} %copy-done.2, f32[1,128]{1,0:T(1,128)S(1)} %bitcast.16, f32[8,128,128]{2,1,0:T(8,128)S(1)} %copy-done, f32[16,17,8,128]{3,2,1,0:T(8,128)S(1)} %all_to_all.22.cells), custom_call_target="tpu_custom_call" | custom-call | bytes 8388608 | tf_op jit(solution)/shard_map/pallas_call | solution.py:502
  52.1 8.2 %collective-permute-start.2 = (f32[920,128]{1,0:T(8,128)S(1)}, f32[920,128]{1,0:T(8,128)S(1)}, u32[]{:S(2)}, u32[]{:S(2)}) collective-permute-start(f32[920,128]{1,0:T(8,128)S(1)} %get-tuple-element.27), channel_id=1, source_target_pairs={{0,15},{1,2},{2,1},{3,4},{4,3},{5,6},{6,5},{7,8},{8,7},{9,10},{10,... | collective-permute-start | bytes 1413128 | tf_op jit(solution)/shard_map/ppermute | solution.py:508
  60.3 4.2 %collective-permute-start.3 = (f32[920,128]{1,0:T(8,128)S(1)}, f32[920,128]{1,0:T(8,128)S(1)}, u32[]{:S(2)}, u32[]{:S(2)}) collective-permute-start(f32[920,128]{1,0:T(8,128)S(1)} %get-tuple-element.31), channel_id=1, source_target_pairs={{0,1},{1,0},{2,3},{3,2},{4,5},{5,4},{6,7},{7,6},{8,9},{9,8},{10,11... | collective-permute-start | bytes 1413128 | tf_op jit(solution)/shard_map/ppermute | solution.py:509
  64.5 3.2 %shard_map.108 = (f32[3,8,264,128]{3,2,1,0:T(8,128)S(1)}, f32[3,8,264,128]{3,2,1,0:T(8,128)S(1)}, f32[9,8,128]{2,1,0:T(8,128)S(1)}, f32[8,264,128]{2,1,0:T(8,128)S(1)}, f32[2048,128]{1,0:T(8,128)}) custom-call(f32[8]{0:T(128)S(1)} %copy-done.2, f32[1,128]{1,0:T(1,128)S(1)} %bitcast.17, f32[8,128,128]{2,1,0:T(8,128)S(1)} %copy-done, ...), custom_call_target="tpu_custom_call" | custom-call | flops 10000000000 | bytes 8388608 | tf_op jit(solution)/shard_map/pallas_call | solution.py:510
  67.6 1.5 %shard_map.109 = (f32[3,264,128]{2,1,0:T(8,128)S(1)}, f32[6,264,128]{2,1,0:T(8,128)S(1)}, f32[9,8,128]{2,1,0:T(8,128)S(1)}) custom-call(f32[8]{0:T(128)S(1)} %copy-done.2, f32[1,128]{1,0:T(1,128)S(1)} %bitcast.18, f32[8,128,128]{2,1,0:T(8,128)S(1)} %copy-done, f32[920,128]{1,0:T(8,128)S(1)} %collective-permute-done.3.halo, ...), custom_call_target="tpu_custom_call" | custom-call | bytes 4096 | tf_op jit(solution)/shard_map/pallas_call | solution.py:520
  69.1 1.6 %shard_map.110 = (f32[3,264,128]{2,1,0:T(8,128)S(1)}, f32[6,264,128]{2,1,0:T(8,128)S(1)}, f32[256,128]{1,0:T(8,128)S(1)}) custom-call(f32[8]{0:T(128)S(1)} %copy-done.2, f32[1,128]{1,0:T(1,128)S(1)} %bitcast.19, f32[8,128,128]{2,1,0:T(8,128)S(1)} %copy-done, f32[920,128]{1,0:T(8,128)S(1)} %collective-permute-done.2.halo, ...), custom_call_target="tpu_custom_call" | custom-call | bytes 8388608 | tf_op jit(solution)/shard_map/pallas_call | solution.py:523
  70.7 21.4 %all_to_all.23 = f32[256,1,128]{2,1,0:T(1,128)S(1)} all-to-all(f32[256,1,128]{2,1,0:T(1,128)S(1)} %bitcast.15), channel_id=1, replica_groups=mesh['lon_0'=4,'lon_1'=4,'lat_0'=8,'lat_1'=2] {'lon_0','lon_1','lat_0','..., dimensions={0} | all-to-all | bytes 262144 | tf_op jit(solution)/shard_map/all_to_all | solution.py:526
  92.1 1.7 %shard_map.111 = (f32[2048,128]{1,0:T(8,128)}, f32[2048,128]{1,0:T(8,128)}) custom-call(f32[256,128]{1,0:T(8,128)S(1)} %bitcast.14, f32[8,264,128]{2,1,0:T(8,128)S(1)} %get-tuple-element.28.edges, f32[16,264,128]{2,1,0:T(8,128)S(1)} %get-tuple-element.25.early, f32[3,8,264,128]{3,2,1,0:T(8,128)S(1)} %get-tuple-element.29.search, ...), custom_call_target="tpu_custom_call" | custom-call | bytes 8388608 | tf_op jit(solution)/shard_map/pallas_call | solution.py:527
  (10 shorter events, 0.0 us)
Async XLA Ops:
  0.6 1.2 %copy-start.1 = (f32[256,8,128]{2,1,0:T(8,128)S(1)}, f32[256,8,128]{2,1,0:T(8,128)}, u32[]{:S(2)}) copy-start(f32[256,8,128]{2,1,0:T(8,128)} %param.8) | copy-start | bytes 3145732
  2.0 8.3 %collective-permute-start = (f32[512,128]{1,0:T(8,128)S(1)}, f32[512,128]{1,0:T(8,128)S(1)}, u32[]{:S(2)}, u32[]{:S(2)}) collective-permute-start(f32[512,128]{1,0:T(8,128)S(1)} %get-tuple-element.22), channel_id=1, source_target_pairs={{0,15},{1,2},{2,1},{3,4},{4,3},{5,6},{6,5},{7,8},{8,7},{9,10},{10,... | collective-permute-start | bytes 786440 | tf_op jit(solution)/shard_map/ppermute | solution.py:483
  5.1 5.2 %collective-permute-start.1 = (f32[512,128]{1,0:T(8,128)S(1)}, f32[512,128]{1,0:T(8,128)S(1)}, u32[]{:S(2)}, u32[]{:S(2)}) collective-permute-start(f32[512,128]{1,0:T(8,128)S(1)} %get-tuple-element.23), channel_id=1, source_target_pairs={{0,1},{1,0},{2,3},{3,2},{4,5},{5,4},{6,7},{7,6},{8,9},{9,8},{10,11... | collective-permute-start | bytes 786440 | tf_op jit(solution)/shard_map/ppermute | solution.py:482
  10.8 19.7 %copy-start.4 = (s32[8]{0:T(128)S(1)}, s32[8]{0:T(128)}, u32[]{:S(2)}) copy-start(s32[8]{0:T(128)} %offsets.1) | copy-start | bytes 100
  10.8 19.7 %copy-start.5 = (f32[8]{0:T(128)S(1)}, f32[8]{0:T(128)}, u32[]{:S(2)}) copy-start(f32[8]{0:T(128)} %frac_lon.1) | copy-start | bytes 100
  32.5 17.8 %copy-start = (f32[8,128,128]{2,1,0:T(8,128)S(1)}, f32[8,128,128]{2,1,0:T(8,128)}, u32[]{:S(2)}) copy-start(f32[8,128,128]{2,1,0:T(8,128)} %inverses.7) | copy-start | bytes 1572868
  32.5 17.8 %copy-start.2 = (f32[8]{0:T(128)S(1)}, f32[8]{0:T(128)}, u32[]{:S(2)}) copy-start(f32[8]{0:T(128)} %metric.7) | copy-start | bytes 100
  32.5 17.8 %copy-start.3 = (f32[128]{0:T(128)S(1)}, f32[128]{0:T(128)}, u32[]{:S(2)}) copy-start(f32[128]{0:T(128)} %param.14) | copy-start | bytes 1540
  52.1 17.0 %collective-permute-start.2 = (f32[920,128]{1,0:T(8,128)S(1)}, f32[920,128]{1,0:T(8,128)S(1)}, u32[]{:S(2)}, u32[]{:S(2)}) collective-permute-start(f32[920,128]{1,0:T(8,128)S(1)} %get-tuple-element.27), channel_id=1, source_target_pairs={{0,15},{1,2},{2,1},{3,4},{4,3},{5,6},{6,5},{7,8},{8,7},{9,10},{10,... | collective-permute-start | bytes 1413128 | tf_op jit(solution)/shard_map/ppermute | solution.py:508
  60.3 7.4 %collective-permute-start.3 = (f32[920,128]{1,0:T(8,128)S(1)}, f32[920,128]{1,0:T(8,128)S(1)}, u32[]{:S(2)}, u32[]{:S(2)}) collective-permute-start(f32[920,128]{1,0:T(8,128)S(1)} %get-tuple-element.31), channel_id=1, source_target_pairs={{0,1},{1,0},{2,3},{3,2},{4,5},{5,4},{6,7},{7,6},{8,9},{9,8},{10,11... | collective-permute-start | bytes 1413128 | tf_op jit(solution)/shard_map/ppermute | solution.py:509

commit v8 on v7

--- a/solution.py
+++ b/solution.py
@@ -128,19 +128,24 @@
         rest = jnp.bitwise_and(off, 127)
         placed = delta + rest
         left, right_high, right_low = [], [], []
-        for k in range(3):
+        shared = jnp.where(rest < 2, 64, 0)
+        for k in range(2):
             table = jnp.zeros((128, 128), jnp.float32)
             for m in range(4):
-                table = jnp.where(placed == m - 1 - 128 * (k - 1), w[m], table)
+                if k == 0:
+                    table = jnp.where(placed == m - 1 + 128, w[m], table)
+                    table = jnp.where(placed == m - 1 - 128, w[m], table)
+                else:
+                    table = jnp.where(placed == m - 1, w[m], table)
             t_high, t_low = halves(table)
             right_high += [t_high, t_high]
             right_low += [t_low, t_low]
             if k == 0:
-                part = jnp.concatenate([cells[B - 1 :, j], cells[: B - 1, j]], 0)
-            elif k == 1:
+                before = jnp.concatenate([cells[B - 1 :, j], cells[: B - 1, j]], 0)
+                after = jnp.concatenate([cells[1:, j], cells[:1, j]], 0)
+                part = jnp.where(lane < shared, after, before)
+            else:
                 part = cells[:, j]
-            else:
-                part = jnp.concatenate([cells[1:, j], cells[:1, j]], 0)
             left += list(halves(part.reshape(B * 8, 128)))
         right = jnp.concatenate(
             [jnp.concatenate(right_high, 0), jnp.concatenate(right_low, 0)], 1

time: 94 us -> 93.8 us (level)
  no operation moved by 1% of the time
where the time goes in v8:
time: 93.8 us; the launch traced here: 93.6 us
  blocking collectives  58.9 us (63%)
  starting transfers between devices  19.2 us (20%)
  Pallas kernels  12.6 us (13%)
  local copies, waits for them, and re-layouts  1.32 us (1%)
    all_to_all x1, blocking collectives, body(): gathered = lax.all_to_all(sums, LON_LAT, 0, 0, tiled=True)  21.4 us
    all_to_all x1, blocking collectives, body(): lines = lax.all_to_all(turned, LON, 0, 0, tiled=True)  19.7 us
    all_to_all x1, blocking collectives, body(): back = lax.all_to_all(moved, LON, 0, 0, tiled=True)  17.8 us
    ppermute x1, starting transfers between devices, body(): cross = lax.ppermute(cross_out, LAT, across)  8.15 us
    ppermute x1, starting transfers between devices, body(): pair = lax.ppermute(pair_out, LAT, in_chip)  4.16 us
    ppermute x1, starting transfers between devices, body(): pair_in = lax.ppermute(pair_out, LAT, in_chip)  3.77 us
    pallas_call x1, Pallas kernels, body(): call(inner_kernel, (SMEM,) + (VMEM,) * 5, ((3, R, E, L), (3, R, E, L), (9...  3.17 us
    ppermute x1, starting transfers between devices, body(): cross_in = lax.ppermute(cross_out, LAT, across)  3.11 us
  transfers between devices with their start and end apart: 4, of which 0 were waited for; matrix products, arithmetic and copies ran while one was open for 1% of the time, Pallas kernels for 6%

profile of v8, /device:TPU:1, one launch (start us, length us, event | category | flops | bytes accessed | tf_op | source)
XLA Modules:
  0.0 93.6 jit_solution(10547216305899092394)
XLA Ops:
  0.6 1.2 %copy-done.1 = f32[256,8,128]{2,1,0:T(8,128)S(1)} copy-done((f32[256,8,128]{2,1,0:T(8,128)S(1)}, f32[256,8,128]{2,1,0:T(8,128)}, u32[]{:S(2)}) %copy-start.1) | copy-done | bytes 1048600
  1.9 0.1 shard_map.103
  2.0 3.1 %collective-permute-start = (f32[512,128]{1,0:T(8,128)S(1)}, f32[512,128]{1,0:T(8,128)S(1)}, u32[]{:S(2)}, u32[]{:S(2)}) collective-permute-start(f32[512,128]{1,0:T(8,128)S(1)} %get-tuple-element.22), channel_id=1, source_target_pairs={{0,15},{1,2},{2,1},{3,4},{4,3},{5,6},{6,5},{7,8},{8,7},{9,10},{10,... | collective-permute-start | bytes 786440 | tf_op jit(solution)/shard_map/ppermute | solution.py:488
  5.1 3.8 %collective-permute-start.1 = (f32[512,128]{1,0:T(8,128)S(1)}, f32[512,128]{1,0:T(8,128)S(1)}, u32[]{:S(2)}, u32[]{:S(2)}) collective-permute-start(f32[512,128]{1,0:T(8,128)S(1)} %get-tuple-element.23), channel_id=1, source_target_pairs={{0,1},{1,0},{2,3},{3,2},{4,5},{5,4},{6,7},{7,6},{8,9},{9,8},{10,11... | collective-permute-start | bytes 786440 | tf_op jit(solution)/shard_map/ppermute | solution.py:487
  8.8 0.7 pad_maximum_fusion
  9.6 0.1 broadcast_in_dim.2.fractions
  9.7 0.6 shard_map.104.begun
  10.2 0.5 shard_map.105
  10.8 0.0 copy-start.4
  10.8 0.0 copy-start.5
  10.8 19.7 %all_to_all.21 = f32[16,2,8,8,128]{4,3,2,1,0:T(8,128)S(1)} all-to-all(f32[16,2,8,8,128]{4,3,2,1,0:T(8,128)S(1)} %shard_map.105), channel_id=1, replica_groups=mesh['lon_0'=4,'lon_1'=4,'lat_0'=8,'lat_1'=2] {'lon_0','lon_1'}, dimensions={0} | all-to-all | bytes 2097152 | tf_op jit(solution)/shard_map/all_to_all | solution.py:498
  30.5 1.8 %shard_map.106 = f32[16,17,8,128]{3,2,1,0:T(8,128)S(1)} custom-call(s32[8]{0:T(128)S(1)} %copy-done.4, f32[8]{0:T(128)S(1)} %copy-done.5, f32[32,8,8,128]{3,2,1,0:T(8,128)S(1)} %bitcast.13), custom_call_target="tpu_custom_call" | custom-call | bytes 8388608 | tf_op jit(solution)/shard_map/pallas_call | solution.py:499
  32.3 0.0 copy-start
  32.3 0.0 copy-start.2
  32.4 0.0 copy-start.3
  32.4 17.8 %all_to_all.22.cells = f32[16,17,8,128]{3,2,1,0:T(8,128)S(1)} all-to-all(f32[16,17,8,128]{3,2,1,0:T(8,128)S(1)} %shard_map.106), channel_id=1, replica_groups=mesh['lon_0'=4,'lon_1'=4,'lat_0'=8,'lat_1'=2] {'lon_0','lon_1'}, dimensions={0} | all-to-all | bytes 2228224 | tf_op jit(solution)/shard_map/all_to_all | solution.py:505
  50.2 1.8 %shard_map.107 = (f32[8,264,128]{2,1,0:T(8,128)S(1)}, f32[920,128]{1,0:T(8,128)S(1)}, f32[920,128]{1,0:T(8,128)S(1)}, f32[16,264,128]{2,1,0:T(8,128)S(1)}) custom-call(f32[8]{0:T(128)S(1)} %copy-done.2, f32[1,128]{1,0:T(1,128)S(1)} %bitcast.16, f32[8,128,128]{2,1,0:T(8,128)S(1)} %copy-done, f32[16,17,8,128]{3,2,1,0:T(8,128)S(1)} %all_to_all.22.cells), custom_call_target="tpu_custom_call" | custom-call | bytes 8388608 | tf_op jit(solution)/shard_map/pallas_call | solution.py:507
  52.0 8.2 %collective-permute-start.2 = (f32[920,128]{1,0:T(8,128)S(1)}, f32[920,128]{1,0:T(8,128)S(1)}, u32[]{:S(2)}, u32[]{:S(2)}) collective-permute-start(f32[920,128]{1,0:T(8,128)S(1)} %get-tuple-element.27), channel_id=1, source_target_pairs={{0,15},{1,2},{2,1},{3,4},{4,3},{5,6},{6,5},{7,8},{8,7},{9,10},{10,... | collective-permute-start | bytes 1413128 | tf_op jit(solution)/shard_map/ppermute | solution.py:513
  60.1 4.2 %collective-permute-start.3 = (f32[920,128]{1,0:T(8,128)S(1)}, f32[920,128]{1,0:T(8,128)S(1)}, u32[]{:S(2)}, u32[]{:S(2)}) collective-permute-start(f32[920,128]{1,0:T(8,128)S(1)} %get-tuple-element.31), channel_id=1, source_target_pairs={{0,1},{1,0},{2,3},{3,2},{4,5},{5,4},{6,7},{7,6},{8,9},{9,8},{10,11... | collective-permute-start | bytes 1413128 | tf_op jit(solution)/shard_map/ppermute | solution.py:514
  64.3 3.2 %shard_map.108 = (f32[3,8,264,128]{3,2,1,0:T(8,128)S(1)}, f32[3,8,264,128]{3,2,1,0:T(8,128)S(1)}, f32[9,8,128]{2,1,0:T(8,128)S(1)}, f32[8,264,128]{2,1,0:T(8,128)S(1)}, f32[2048,128]{1,0:T(8,128)}) custom-call(f32[8]{0:T(128)S(1)} %copy-done.2, f32[1,128]{1,0:T(1,128)S(1)} %bitcast.17, f32[8,128,128]{2,1,0:T(8,128)S(1)} %copy-done, ...), custom_call_target="tpu_custom_call" | custom-call | flops 10000000000 | bytes 8388608 | tf_op jit(solution)/shard_map/pallas_call | solution.py:515
  67.4 1.5 %shard_map.109 = (f32[3,264,128]{2,1,0:T(8,128)S(1)}, f32[6,264,128]{2,1,0:T(8,128)S(1)}, f32[9,8,128]{2,1,0:T(8,128)S(1)}) custom-call(f32[8]{0:T(128)S(1)} %copy-done.2, f32[1,128]{1,0:T(1,128)S(1)} %bitcast.18, f32[8,128,128]{2,1,0:T(8,128)S(1)} %copy-done, f32[920,128]{1,0:T(8,128)S(1)} %collective-permute-done.3.halo, ...), custom_call_target="tpu_custom_call" | custom-call | bytes 4096 | tf_op jit(solution)/shard_map/pallas_call | solution.py:525
  68.9 1.6 %shard_map.110 = (f32[3,264,128]{2,1,0:T(8,128)S(1)}, f32[6,264,128]{2,1,0:T(8,128)S(1)}, f32[256,128]{1,0:T(8,128)S(1)}) custom-call(f32[8]{0:T(128)S(1)} %copy-done.2, f32[1,128]{1,0:T(1,128)S(1)} %bitcast.19, f32[8,128,128]{2,1,0:T(8,128)S(1)} %copy-done, f32[920,128]{1,0:T(8,128)S(1)} %collective-permute-done.2.halo, ...), custom_call_target="tpu_custom_call" | custom-call | bytes 8388608 | tf_op jit(solution)/shard_map/pallas_call | solution.py:528
  70.5 21.4 %all_to_all.23 = f32[256,1,128]{2,1,0:T(1,128)S(1)} all-to-all(f32[256,1,128]{2,1,0:T(1,128)S(1)} %bitcast.15), channel_id=1, replica_groups=mesh['lon_0'=4,'lon_1'=4,'lat_0'=8,'lat_1'=2] {'lon_0','lon_1','lat_0','..., dimensions={0} | all-to-all | bytes 262144 | tf_op jit(solution)/shard_map/all_to_all | solution.py:531
  92.0 1.7 %shard_map.111 = (f32[2048,128]{1,0:T(8,128)}, f32[2048,128]{1,0:T(8,128)}) custom-call(f32[256,128]{1,0:T(8,128)S(1)} %bitcast.14, f32[8,264,128]{2,1,0:T(8,128)S(1)} %get-tuple-element.28.edges, f32[16,264,128]{2,1,0:T(8,128)S(1)} %get-tuple-element.25.early, f32[3,8,264,128]{3,2,1,0:T(8,128)S(1)} %get-tuple-element.29.search, ...), custom_call_target="tpu_custom_call" | custom-call | bytes 8388608 | tf_op jit(solution)/shard_map/pallas_call | solution.py:532
  (10 shorter events, 0.0 us)
Async XLA Ops:
  0.6 1.2 %copy-start.1 = (f32[256,8,128]{2,1,0:T(8,128)S(1)}, f32[256,8,128]{2,1,0:T(8,128)}, u32[]{:S(2)}) copy-start(f32[256,8,128]{2,1,0:T(8,128)} %param.8) | copy-start | bytes 3145732
  2.0 8.3 %collective-permute-start = (f32[512,128]{1,0:T(8,128)S(1)}, f32[512,128]{1,0:T(8,128)S(1)}, u32[]{:S(2)}, u32[]{:S(2)}) collective-permute-start(f32[512,128]{1,0:T(8,128)S(1)} %get-tuple-element.22), channel_id=1, source_target_pairs={{0,15},{1,2},{2,1},{3,4},{4,3},{5,6},{6,5},{7,8},{8,7},{9,10},{10,... | collective-permute-start | bytes 786440 | tf_op jit(solution)/shard_map/ppermute | solution.py:488
  5.1 5.2 %collective-permute-start.1 = (f32[512,128]{1,0:T(8,128)S(1)}, f32[512,128]{1,0:T(8,128)S(1)}, u32[]{:S(2)}, u32[]{:S(2)}) collective-permute-start(f32[512,128]{1,0:T(8,128)S(1)} %get-tuple-element.23), channel_id=1, source_target_pairs={{0,1},{1,0},{2,3},{3,2},{4,5},{5,4},{6,7},{7,6},{8,9},{9,8},{10,11... | collective-permute-start | bytes 786440 | tf_op jit(solution)/shard_map/ppermute | solution.py:487
  10.8 19.7 %copy-start.4 = (s32[8]{0:T(128)S(1)}, s32[8]{0:T(128)}, u32[]{:S(2)}) copy-start(s32[8]{0:T(128)} %offsets.1) | copy-start | bytes 100
  10.8 19.7 %copy-start.5 = (f32[8]{0:T(128)S(1)}, f32[8]{0:T(128)}, u32[]{:S(2)}) copy-start(f32[8]{0:T(128)} %frac_lon.1) | copy-start | bytes 100
  32.3 17.8 %copy-start = (f32[8,128,128]{2,1,0:T(8,128)S(1)}, f32[8,128,128]{2,1,0:T(8,128)}, u32[]{:S(2)}) copy-start(f32[8,128,128]{2,1,0:T(8,128)} %inverses.7) | copy-start | bytes 1572868
  32.3 17.8 %copy-start.2 = (f32[8]{0:T(128)S(1)}, f32[8]{0:T(128)}, u32[]{:S(2)}) copy-start(f32[8]{0:T(128)} %metric.7) | copy-start | bytes 100
  32.4 17.8 %copy-start.3 = (f32[128]{0:T(128)S(1)}, f32[128]{0:T(128)}, u32[]{:S(2)}) copy-start(f32[128]{0:T(128)} %param.14) | copy-start | bytes 1540
  52.0 17.0 %collective-permute-start.2 = (f32[920,128]{1,0:T(8,128)S(1)}, f32[920,128]{1,0:T(8,128)S(1)}, u32[]{:S(2)}, u32[]{:S(2)}) collective-permute-start(f32[920,128]{1,0:T(8,128)S(1)} %get-tuple-element.27), channel_id=1, source_target_pairs={{0,15},{1,2},{2,1},{3,4},{4,3},{5,6},{6,5},{7,8},{8,7},{9,10},{10,... | collective-permute-start | bytes 1413128 | tf_op jit(solution)/shard_map/ppermute | solution.py:513
  60.1 7.3 %collective-permute-start.3 = (f32[920,128]{1,0:T(8,128)S(1)}, f32[920,128]{1,0:T(8,128)S(1)}, u32[]{:S(2)}, u32[]{:S(2)}) collective-permute-start(f32[920,128]{1,0:T(8,128)S(1)} %get-tuple-element.31), channel_id=1, source_target_pairs={{0,1},{1,0},{2,3},{3,2},{4,5},{5,4},{6,7},{7,6},{8,9},{9,8},{10,11... | collective-permute-start | bytes 1413128 | tf_op jit(solution)/shard_map/ppermute | solution.py:514

commit v9 on v8

--- a/solution.py
+++ b/solution.py
@@ -227,15 +227,18 @@
 
 def solve_end(end, metric, rows, inverses, cells, rim, ring, at, early, base):
     j = [row_at(end, k) for k in range(H)]
+    q = []
     for k in range(H):
         turned_row(cells, rim, j[k], ring, at(k))
-        early[base + k] = precondition(inverses[j[k]], ring[at(k)])
+        q.append(precondition(inverses[j[k]], ring[at(k)]))
     m0, m1 = metric_row(metric, j[0]), metric_row(metric, j[1])
-    early[base + 3] = alone(early[base], m0, rows) - early[base + 1]
-    early[base + 4] = operate(early[base + 1], early[base], early[base + 2], m1, rows)
-    early[base + 5] = precondition(inverses[j[0]], early[base + 3])
-    early[base + 6] = precondition(inverses[j[1]], early[base + 4])
-    early[base + 7] = alone(early[base + 5], m0, rows) - early[base + 6]
+    part = alone(q[0], m0, rows) - q[1]
+    whole = operate(q[1], q[0], q[2], m1, rows)
+    next_part = precondition(inverses[j[0]], part)
+    next_whole = precondition(inverses[j[1]], whole)
+    last = alone(next_part, m0, rows) - next_whole
+    for k, value in enumerate((*q, part, whole, next_part, next_whole, last)):
+        early[base + k] = value
 
 
 def fill(out, end, metric, inverses, early, base, blank=None):

time: 93.8 us -> 93.8 us (level)
  no operation moved by 1% of the time
where the time goes in v9:
time: 93.8 us; the launch traced here: 93.6 us
  blocking collectives  59 us (63%)
  starting transfers between devices  19.2 us (20%)
  Pallas kernels  12.6 us (13%)
  local copies, waits for them, and re-layouts  1.32 us (1%)
    all_to_all x1, blocking collectives, body(): gathered = lax.all_to_all(sums, LON_LAT, 0, 0, tiled=True)  21.5 us
    all_to_all x1, blocking collectives, body(): lines = lax.all_to_all(turned, LON, 0, 0, tiled=True)  19.7 us
    all_to_all x1, blocking collectives, body(): back = lax.all_to_all(moved, LON, 0, 0, tiled=True)  17.8 us
    ppermute x1, starting transfers between devices, body(): cross = lax.ppermute(cross_out, LAT, across)  8.16 us
    ppermute x1, starting transfers between devices, body(): pair = lax.ppermute(pair_out, LAT, in_chip)  4.15 us
    ppermute x1, starting transfers between devices, body(): pair_in = lax.ppermute(pair_out, LAT, in_chip)  3.77 us
    pallas_call x1, Pallas kernels, body(): call(inner_kernel, (SMEM,) + (VMEM,) * 5, ((3, R, E, L), (3, R, E, L), (9...  3.17 us
    ppermute x1, starting transfers between devices, body(): cross_in = lax.ppermute(cross_out, LAT, across)  3.11 us
  transfers between devices with their start and end apart: 4, of which 0 were waited for; matrix products, arithmetic and copies ran while one was open for 1% of the time, Pallas kernels for 6%

profile of v9, /device:TPU:1, one launch (start us, length us, event | category | flops | bytes accessed | tf_op | source)
XLA Modules:
  0.0 93.6 jit_solution(17316759151874319568)
XLA Ops:
  0.6 1.2 %copy-done.1 = f32[256,8,128]{2,1,0:T(8,128)S(1)} copy-done((f32[256,8,128]{2,1,0:T(8,128)S(1)}, f32[256,8,128]{2,1,0:T(8,128)}, u32[]{:S(2)}) %copy-start.1) | copy-done | bytes 1048600
  1.9 0.1 shard_map.103
  2.0 3.1 %collective-permute-start = (f32[512,128]{1,0:T(8,128)S(1)}, f32[512,128]{1,0:T(8,128)S(1)}, u32[]{:S(2)}, u32[]{:S(2)}) collective-permute-start(f32[512,128]{1,0:T(8,128)S(1)} %get-tuple-element.22), channel_id=1, source_target_pairs={{0,15},{1,2},{2,1},{3,4},{4,3},{5,6},{6,5},{7,8},{8,7},{9,10},{10,... | collective-permute-start | bytes 786440 | tf_op jit(solution)/shard_map/ppermute | solution.py:491
  5.1 3.8 %collective-permute-start.1 = (f32[512,128]{1,0:T(8,128)S(1)}, f32[512,128]{1,0:T(8,128)S(1)}, u32[]{:S(2)}, u32[]{:S(2)}) collective-permute-start(f32[512,128]{1,0:T(8,128)S(1)} %get-tuple-element.23), channel_id=1, source_target_pairs={{0,1},{1,0},{2,3},{3,2},{4,5},{5,4},{6,7},{7,6},{8,9},{9,8},{10,11... | collective-permute-start | bytes 786440 | tf_op jit(solution)/shard_map/ppermute | solution.py:490
  8.8 0.7 pad_maximum_fusion
  9.6 0.1 broadcast_in_dim.2.fractions
  9.7 0.6 shard_map.104.begun
  10.2 0.5 shard_map.105
  10.8 0.0 copy-start.4
  10.8 0.0 copy-start.5
  10.8 19.7 %all_to_all.21 = f32[16,2,8,8,128]{4,3,2,1,0:T(8,128)S(1)} all-to-all(f32[16,2,8,8,128]{4,3,2,1,0:T(8,128)S(1)} %shard_map.105), channel_id=1, replica_groups=mesh['lon_0'=4,'lon_1'=4,'lat_0'=8,'lat_1'=2] {'lon_0','lon_1'}, dimensions={0} | all-to-all | bytes 2097152 | tf_op jit(solution)/shard_map/all_to_all | solution.py:501
  30.5 1.8 %shard_map.106 = f32[16,17,8,128]{3,2,1,0:T(8,128)S(1)} custom-call(s32[8]{0:T(128)S(1)} %copy-done.4, f32[8]{0:T(128)S(1)} %copy-done.5, f32[32,8,8,128]{3,2,1,0:T(8,128)S(1)} %bitcast.13), custom_call_target="tpu_custom_call" | custom-call | bytes 8388608 | tf_op jit(solution)/shard_map/pallas_call | solution.py:502
  32.3 0.0 copy-start
  32.3 0.0 copy-start.2
  32.4 0.0 copy-start.3
  32.4 17.8 %all_to_all.22.cells = f32[16,17,8,128]{3,2,1,0:T(8,128)S(1)} all-to-all(f32[16,17,8,128]{3,2,1,0:T(8,128)S(1)} %shard_map.106), channel_id=1, replica_groups=mesh['lon_0'=4,'lon_1'=4,'lat_0'=8,'lat_1'=2] {'lon_0','lon_1'}, dimensions={0} | all-to-all | bytes 2228224 | tf_op jit(solution)/shard_map/all_to_all | solution.py:508
  50.2 1.8 %shard_map.107 = (f32[8,264,128]{2,1,0:T(8,128)S(1)}, f32[920,128]{1,0:T(8,128)S(1)}, f32[920,128]{1,0:T(8,128)S(1)}, f32[16,264,128]{2,1,0:T(8,128)S(1)}) custom-call(f32[8]{0:T(128)S(1)} %copy-done.2, f32[1,128]{1,0:T(1,128)S(1)} %bitcast.16, f32[8,128,128]{2,1,0:T(8,128)S(1)} %copy-done, f32[16,17,8,128]{3,2,1,0:T(8,128)S(1)} %all_to_all.22.cells), custom_call_target="tpu_custom_call" | custom-call | bytes 8388608 | tf_op jit(solution)/shard_map/pallas_call | solution.py:510
  51.9 8.2 %collective-permute-start.2 = (f32[920,128]{1,0:T(8,128)S(1)}, f32[920,128]{1,0:T(8,128)S(1)}, u32[]{:S(2)}, u32[]{:S(2)}) collective-permute-start(f32[920,128]{1,0:T(8,128)S(1)} %get-tuple-element.27), channel_id=1, source_target_pairs={{0,15},{1,2},{2,1},{3,4},{4,3},{5,6},{6,5},{7,8},{8,7},{9,10},{10,... | collective-permute-start | bytes 1413128 | tf_op jit(solution)/shard_map/ppermute | solution.py:516
  60.1 4.2 %collective-permute-start.3 = (f32[920,128]{1,0:T(8,128)S(1)}, f32[920,128]{1,0:T(8,128)S(1)}, u32[]{:S(2)}, u32[]{:S(2)}) collective-permute-start(f32[920,128]{1,0:T(8,128)S(1)} %get-tuple-element.31), channel_id=1, source_target_pairs={{0,1},{1,0},{2,3},{3,2},{4,5},{5,4},{6,7},{7,6},{8,9},{9,8},{10,11... | collective-permute-start | bytes 1413128 | tf_op jit(solution)/shard_map/ppermute | solution.py:517
  64.2 3.2 %shard_map.108 = (f32[3,8,264,128]{3,2,1,0:T(8,128)S(1)}, f32[3,8,264,128]{3,2,1,0:T(8,128)S(1)}, f32[9,8,128]{2,1,0:T(8,128)S(1)}, f32[8,264,128]{2,1,0:T(8,128)S(1)}, f32[2048,128]{1,0:T(8,128)}) custom-call(f32[8]{0:T(128)S(1)} %copy-done.2, f32[1,128]{1,0:T(1,128)S(1)} %bitcast.17, f32[8,128,128]{2,1,0:T(8,128)S(1)} %copy-done, ...), custom_call_target="tpu_custom_call" | custom-call | flops 10000000000 | bytes 8388608 | tf_op jit(solution)/shard_map/pallas_call | solution.py:518
  67.4 1.5 %shard_map.109 = (f32[3,264,128]{2,1,0:T(8,128)S(1)}, f32[6,264,128]{2,1,0:T(8,128)S(1)}, f32[9,8,128]{2,1,0:T(8,128)S(1)}) custom-call(f32[8]{0:T(128)S(1)} %copy-done.2, f32[1,128]{1,0:T(1,128)S(1)} %bitcast.18, f32[8,128,128]{2,1,0:T(8,128)S(1)} %copy-done, f32[920,128]{1,0:T(8,128)S(1)} %collective-permute-done.3.halo, ...), custom_call_target="tpu_custom_call" | custom-call | bytes 4096 | tf_op jit(solution)/shard_map/pallas_call | solution.py:528
  68.9 1.6 %shard_map.110 = (f32[3,264,128]{2,1,0:T(8,128)S(1)}, f32[6,264,128]{2,1,0:T(8,128)S(1)}, f32[256,128]{1,0:T(8,128)S(1)}) custom-call(f32[8]{0:T(128)S(1)} %copy-done.2, f32[1,128]{1,0:T(1,128)S(1)} %bitcast.19, f32[8,128,128]{2,1,0:T(8,128)S(1)} %copy-done, f32[920,128]{1,0:T(8,128)S(1)} %collective-permute-done.2.halo, ...), custom_call_target="tpu_custom_call" | custom-call | bytes 8388608 | tf_op jit(solution)/shard_map/pallas_call | solution.py:531
  70.5 21.5 %all_to_all.23 = f32[256,1,128]{2,1,0:T(1,128)S(1)} all-to-all(f32[256,1,128]{2,1,0:T(1,128)S(1)} %bitcast.15), channel_id=1, replica_groups=mesh['lon_0'=4,'lon_1'=4,'lat_0'=8,'lat_1'=2] {'lon_0','lon_1','lat_0','..., dimensions={0} | all-to-all | bytes 262144 | tf_op jit(solution)/shard_map/all_to_all | solution.py:534
  91.9 1.7 %shard_map.111 = (f32[2048,128]{1,0:T(8,128)}, f32[2048,128]{1,0:T(8,128)}) custom-call(f32[256,128]{1,0:T(8,128)S(1)} %bitcast.14, f32[8,264,128]{2,1,0:T(8,128)S(1)} %get-tuple-element.28.edges, f32[16,264,128]{2,1,0:T(8,128)S(1)} %get-tuple-element.25.early, f32[3,8,264,128]{3,2,1,0:T(8,128)S(1)} %get-tuple-element.29.search, ...), custom_call_target="tpu_custom_call" | custom-call | bytes 8388608 | tf_op jit(solution)/shard_map/pallas_call | solution.py:535
  (10 shorter events, 0.0 us)
Async XLA Ops:
  0.6 1.2 %copy-start.1 = (f32[256,8,128]{2,1,0:T(8,128)S(1)}, f32[256,8,128]{2,1,0:T(8,128)}, u32[]{:S(2)}) copy-start(f32[256,8,128]{2,1,0:T(8,128)} %param.8) | copy-start | bytes 3145732
  2.0 8.3 %collective-permute-start = (f32[512,128]{1,0:T(8,128)S(1)}, f32[512,128]{1,0:T(8,128)S(1)}, u32[]{:S(2)}, u32[]{:S(2)}) collective-permute-start(f32[512,128]{1,0:T(8,128)S(1)} %get-tuple-element.22), channel_id=1, source_target_pairs={{0,15},{1,2},{2,1},{3,4},{4,3},{5,6},{6,5},{7,8},{8,7},{9,10},{10,... | collective-permute-start | bytes 786440 | tf_op jit(solution)/shard_map/ppermute | solution.py:491
  5.1 5.2 %collective-permute-start.1 = (f32[512,128]{1,0:T(8,128)S(1)}, f32[512,128]{1,0:T(8,128)S(1)}, u32[]{:S(2)}, u32[]{:S(2)}) collective-permute-start(f32[512,128]{1,0:T(8,128)S(1)} %get-tuple-element.23), channel_id=1, source_target_pairs={{0,1},{1,0},{2,3},{3,2},{4,5},{5,4},{6,7},{7,6},{8,9},{9,8},{10,11... | collective-permute-start | bytes 786440 | tf_op jit(solution)/shard_map/ppermute | solution.py:490
  10.8 19.7 %copy-start.4 = (s32[8]{0:T(128)S(1)}, s32[8]{0:T(128)}, u32[]{:S(2)}) copy-start(s32[8]{0:T(128)} %offsets.1) | copy-start | bytes 100
  10.8 19.7 %copy-start.5 = (f32[8]{0:T(128)S(1)}, f32[8]{0:T(128)}, u32[]{:S(2)}) copy-start(f32[8]{0:T(128)} %frac_lon.1) | copy-start | bytes 100
  32.3 17.8 %copy-start = (f32[8,128,128]{2,1,0:T(8,128)S(1)}, f32[8,128,128]{2,1,0:T(8,128)}, u32[]{:S(2)}) copy-start(f32[8,128,128]{2,1,0:T(8,128)} %inverses.7) | copy-start | bytes 1572868
  32.3 17.8 %copy-start.2 = (f32[8]{0:T(128)S(1)}, f32[8]{0:T(128)}, u32[]{:S(2)}) copy-start(f32[8]{0:T(128)} %metric.7) | copy-start | bytes 100
  32.4 17.8 %copy-start.3 = (f32[128]{0:T(128)S(1)}, f32[128]{0:T(128)}, u32[]{:S(2)}) copy-start(f32[128]{0:T(128)} %param.14) | copy-start | bytes 1540
  51.9 16.9 %collective-permute-start.2 = (f32[920,128]{1,0:T(8,128)S(1)}, f32[920,128]{1,0:T(8,128)S(1)}, u32[]{:S(2)}, u32[]{:S(2)}) collective-permute-start(f32[920,128]{1,0:T(8,128)S(1)} %get-tuple-element.27), channel_id=1, source_target_pairs={{0,15},{1,2},{2,1},{3,4},{4,3},{5,6},{6,5},{7,8},{8,7},{9,10},{10,... | collective-permute-start | bytes 1413128 | tf_op jit(solution)/shard_map/ppermute | solution.py:516
  60.1 7.3 %collective-permute-start.3 = (f32[920,128]{1,0:T(8,128)S(1)}, f32[920,128]{1,0:T(8,128)S(1)}, u32[]{:S(2)}, u32[]{:S(2)}) collective-permute-start(f32[920,128]{1,0:T(8,128)S(1)} %get-tuple-element.31), channel_id=1, source_target_pairs={{0,1},{1,0},{2,3},{3,2},{4,5},{5,4},{6,7},{7,6},{8,9},{9,8},{10,11... | collective-permute-start | bytes 1413128 | tf_op jit(solution)/shard_map/ppermute | solution.py:517
